TPU v7x, 32 devices: a whole 2x2x4 slice. The times are simulated.
32 devices in a mesh: head: 2 (over y), seq: 16 (over z, x, core).
Axes of the slice: x: 2, y: 2, z: 4, core: 2. Of those that a mesh axis runs over, the one named last changes fastest.
Arguments:
- inputs: bfloat16 [2, 16, 512, 1024], P(None, 'seq'), may hold values from -6 to 6
- lengths: int32 [2, 16], replicated, may hold values from 128 to 512
- query_weight: bfloat16 [1024, 1024], P('seq', 'head'), may hold values from -0.1875 to 0.1875
- key_weight: bfloat16 [1024, 1024], P('seq', 'head'), may hold values from -0.1875 to 0.1875
- value_weight: bfloat16 [1024, 1024], P('seq', 'head'), may hold values from -0.1875 to 0.1875
- position_weight: bfloat16 [1024, 1024], P('seq', 'head'), may hold values from -0.1875 to 0.1875
- content_bias: bfloat16 [1024], P(('head', 'seq')), may hold values from -3 to 3
- position_bias: bfloat16 [1024], P(('head', 'seq')), may hold values from -3 to 3
- output_weight: bfloat16 [1024, 1024], P(('head', 'seq')), may hold values from -0.5 to 0.5
- output_bias: bfloat16 [1024], P('seq'), may hold values from -2 to 2
- first_gain: bfloat16 [1024], P('seq'), may hold values from 0.5 to 1.5
- first_shift: bfloat16 [1024], P('seq'), may hold values from -2 to 2
- up_weight: bfloat16 [1024, 4096], P(None, ('head', 'seq')), may hold values from -0.1875 to 0.1875
- up_bias: bfloat16 [4096], P(('head', 'seq')), may hold values from -2 to 2
- down_weight: bfloat16 [4096, 1024], P(('head', 'seq')), may hold values from -0.09375 to 0.09375
- down_bias: bfloat16 [1024], P('seq'), may hold values from -2 to 2
- second_gain: bfloat16 [1024], P('seq'), may hold values from 0.5 to 1.5
- second_shift: bfloat16 [1024], P('seq'), may hold values from -2 to 2
- squeeze_weight: bfloat16 [3072, 1024], P(None, ('head', 'seq')), may hold values from -0.109375 to 0.109375
- squeeze_bias: bfloat16 [1024], P(('head', 'seq')), may hold values from -2 to 2
- cotangent: bfloat16 [2, 16, 512, 1024], P(None, 'seq'), may hold values from -6 to 6
Outputs:
- outputs: bfloat16 [2, 16, 512, 1024], P(None, 'seq', 'head')
- input_grad: bfloat16 [2, 16, 512, 1024], P(None, 'seq', 'head')
- query_grad: float32 [1024, 1024], P('seq', 'head')
- key_grad: float32 [1024, 1024], P('seq', 'head')
- value_grad: float32 [1024, 1024], P('seq', 'head')
- position_grad: float32 [1024, 1024], P('seq', 'head')
- content_bias_grad: float32 [1024], P(('head', 'seq'))
- position_bias_grad: float32 [1024], P(('head', 'seq'))
- output_weight_grad: float32 [1024, 1024], P(('head', 'seq'))
- output_bias_grad: float32 [1024], P(('head', 'seq'))
- first_gain_grad: float32 [1024], P(('head', 'seq'))
- first_shift_grad: float32 [1024], P(('head', 'seq'))
- up_weight_grad: float32 [1024, 4096], P(None, ('head', 'seq'))
- up_bias_grad: float32 [4096], P(('head', 'seq'))
- down_weight_grad: float32 [4096, 1024], P(('head', 'seq'))
- down_bias_grad: float32 [1024], P(('head', 'seq'))
- second_gain_grad: float32 [1024], P(('head', 'seq'))
- second_shift_grad: float32 [1024], P(('head', 'seq'))
- squeeze_weight_grad: float32 [3072, 1024], P(None, ('head', 'seq'))
- squeeze_bias_grad: float32 [1024], P(('head', 'seq'))
All inputs are finite; a program needn't handle non-finite values.
Results may differ from a plain program's by a relative error of at most 0.017.
Values may be sent and summed in bfloat16 or wider, within the bound.
A program may use at most 320 MiB of HBM per device.

v0:
```python
import jax
import jax.numpy as jnp
from jax import lax
from jax.sharding import PartitionSpec as P

HD = 128


epsilon = 1e-05


def shifted(array, axis, by):
    count = lax.axis_size(axis)
    pairs = [(i, i + by) for i in range(count) if 0 <= i + by < count]
    return lax.ppermute(array, axis, pairs)


def for_sending(array):
    return jax.tree.map(lambda a: a.astype(jnp.bfloat16) if a.dtype == jnp.float32 else a, array)


def make_rounders():

    def round_value(v):
        return lax.optimization_barrier(v.astype(jnp.bfloat16)).astype(jnp.float32)

    def plain_value(v):
        return v

    rounded = jax.custom_vjp(round_value)
    passing = jax.custom_vjp(plain_value)

    def keep_round(v):
        return (round_value(v), None)

    def pass_grad(kept, grad):
        return (grad,)

    def keep_plain(v):
        return (v, None)

    def round_grad(kept, grad):
        return (round_value(grad),)

    rounded.defvjp(keep_round, pass_grad)
    passing.defvjp(keep_plain, round_grad)
    return (rounded, passing)


def low(value):
    return make_rounders()[0](value)


def low_back(value):
    return make_rounders()[1](value)


def matmul(left, right):
    return jnp.dot(left, right)


def table_rows(width, count):
    distance = jnp.arange(count - 1, -1, -1).astype(jnp.float32)[:, None]
    frequency = 10000.0 ** (-jnp.arange(0, width, 2).astype(jnp.float32) / width)
    angles = distance * frequency[None, :]
    return jnp.concatenate([jnp.sin(angles), jnp.cos(angles)], axis=1)


def normalize(values, norm_gain, norm_bias):
    centre = values - jnp.mean(values, axis=-1, keepdims=True)
    spread = jnp.mean(centre * centre, axis=-1, keepdims=True)
    return centre * lax.rsqrt(spread + epsilon) * norm_gain + norm_bias


def realign(scores):
    head_count, row_count, col_count = scores.shape
    padded = jnp.pad(scores, ((0, 0), (0, 0), (0, row_count)))
    flattened = padded.reshape(head_count, row_count * (col_count + row_count))
    flattened = lax.slice_in_dim(
        flattened, row_count - 1, row_count - 1 + row_count * (col_count + row_count - 1), axis=1
    )
    return flattened.reshape(head_count, row_count, col_count + row_count - 1)[:, :, :col_count]


def rows_valid(window_lengths, row_count):
    positions = jnp.arange(3 * row_count)
    blocks = positions // row_count
    chosen = jnp.arange(3)
    row_limit = jnp.sum(
        jnp.where(blocks[:, None] == chosen[None, :], window_lengths[None, :3], 0), axis=1
    )
    return positions % row_count < row_limit


def keys_valid(window_lengths, row_count):
    history_ok = rows_valid(window_lengths, row_count)
    places = jnp.arange(row_count)
    return jnp.concatenate(
        [history_ok[::3], places < window_lengths[3], places < window_lengths[4]]
    )


def squeeze(grouped, squeeze_weight, squeeze_bias):
    return low(low_back(matmul(grouped, squeeze_weight) + squeeze_bias))


def attend(
    squeezed,
    memory,
    current,
    allowed_keys,
    query_weight,
    key_weight,
    value_weight,
    position_weight,
    content_bias,
    position_bias,
):
    row_count, width = current.shape
    head_count = query_weight.shape[1] // HD
    scaling = HD ** (-0.5)
    keys_in = jnp.concatenate([squeezed, memory, current], axis=0)
    query = low_back(matmul(current, query_weight))
    content_query = low((query + content_bias) * scaling).reshape(row_count, head_count, HD)
    place_query = low((query + position_bias) * scaling).reshape(row_count, head_count, HD)
    key_rows = low(low_back(matmul(keys_in, key_weight))).reshape(3 * row_count, head_count, HD)
    value_rows = low(low_back(matmul(keys_in, value_weight))).reshape(3 * row_count, head_count, HD)
    places = low(low_back(matmul(low(table_rows(width, 3 * row_count)), position_weight))).reshape(
        3 * row_count, head_count, HD
    )
    content = jnp.einsum("ihd,jhd->hij", content_query, key_rows)
    located = realign(jnp.einsum("ihd,chd->hic", place_query, places))
    scores = low_back(content + located)
    key_index = jnp.arange(3 * row_count).astype(jnp.int32)
    query_index = jnp.arange(row_count).astype(jnp.int32)
    allowed = allowed_keys[None, :] & (key_index[None, :] <= 2 * row_count + query_index[:, None])
    scores = jnp.where(allowed[None], scores, -1e30)
    largest = jnp.max(scores, axis=-1, keepdims=True)
    exp_scores = jnp.exp(scores - largest)
    probability = low(exp_scores / jnp.sum(exp_scores, axis=-1, keepdims=True))
    blended = jnp.einsum("hij,jhd->ihd", probability, value_rows)
    return low(low_back(blended.reshape(row_count, head_count * HD)))


def finish(
    attended,
    residual,
    output_weight,
    output_bias,
    first_gain,
    first_shift,
    up_weight,
    up_bias,
    down_weight,
    down_bias,
    second_gain,
    second_shift,
):
    blended = residual + low_back(matmul(attended, output_weight)) + output_bias
    normed = low(normalize(blended, first_gain, first_shift))
    hidden = low(jax.nn.gelu(low_back(matmul(normed, up_weight) + up_bias), approximate=True))
    return normalize(
        normed + low_back(matmul(hidden, down_weight)) + down_bias, second_gain, second_shift
    )


def body(
    inputs,
    lengths,
    query_weight,
    key_weight,
    value_weight,
    position_weight,
    content_bias,
    position_bias,
    output_weight,
    output_bias,
    first_gain,
    first_shift,
    up_weight,
    up_bias,
    down_weight,
    down_bias,
    second_gain,
    second_shift,
    squeeze_weight,
    squeeze_bias,
    cotangent,
):
    position = lax.axis_index("seq")
    head_index = lax.axis_index("head")
    book_count = inputs.shape[0]
    row_count = inputs.shape[2]
    width = inputs.shape[3]
    segment_count = lengths.shape[1]
    share_rows = row_count // lax.axis_size("head")
    share_start = head_index * share_rows
    gathered = (
        lax.all_gather(query_weight, "seq", axis=0, tiled=True),
        lax.all_gather(key_weight, "seq", axis=0, tiled=True),
        lax.all_gather(value_weight, "seq", axis=0, tiled=True),
        lax.all_gather(position_weight, "seq", axis=0, tiled=True),
        lax.all_gather(content_bias, "seq", axis=0, tiled=True),
        lax.all_gather(position_bias, "seq", axis=0, tiled=True),
        lax.all_gather(output_weight, "seq", axis=0, tiled=True),
        lax.all_gather(output_bias, "seq", axis=0, tiled=True),
        lax.all_gather(first_gain, "seq", axis=0, tiled=True),
        lax.all_gather(first_shift, "seq", axis=0, tiled=True),
        lax.all_gather(up_weight, "seq", axis=1, tiled=True),
        lax.all_gather(up_bias, "seq", axis=0, tiled=True),
        lax.all_gather(down_weight, "seq", axis=0, tiled=True),
        lax.all_gather(down_bias, "seq", axis=0, tiled=True),
        lax.all_gather(second_gain, "seq", axis=0, tiled=True),
        lax.all_gather(second_shift, "seq", axis=0, tiled=True),
        lax.all_gather(squeeze_weight, "seq", axis=1, tiled=True),
        lax.all_gather(squeeze_bias, "seq", axis=0, tiled=True),
    )
    floats = tuple((piece.astype(jnp.float32) for piece in gathered))
    attention_float = floats[:6]
    (
        output_half,
        output_bias_full,
        first_gain_full,
        first_shift_full,
        up_half,
        up_bias_half,
        down_half,
        down_bias_full,
        second_gain_full,
        second_shift_full,
        squeeze_half,
        squeeze_bias_half,
    ) = floats[6:]
    segment = inputs[:, 0]
    earlier = []
    for offset in range(4, 0, -1):
        earlier.append(shifted(segment, "seq", offset))
    window_ids = position - 4 + jnp.arange(5)
    all_ids = jnp.arange(segment_count)
    window_lengths = jnp.sum(
        jnp.where(window_ids[None, :, None] == all_ids[None, None, :], lengths[:, None, :], 0),
        axis=2,
    )
    history_ok = jax.vmap(lambda book_lengths: rows_valid(book_lengths, row_count))(
        window_lengths
    ).astype(jnp.float32)
    allowed_keys = jax.vmap(lambda book_lengths: keys_valid(book_lengths, row_count))(
        window_lengths
    )
    stacked = jnp.concatenate(earlier[:3], axis=1).astype(jnp.float32) * history_ok[:, :, None]
    grouped = stacked.reshape(book_count, row_count, 3 * width)
    squeezed_half, squeeze_pull = jax.vjp(squeeze, grouped, squeeze_half, squeeze_bias_half)
    squeezed = lax.all_gather(
        squeezed_half.astype(jnp.bfloat16), "head", axis=2, tiled=True
    ).astype(jnp.float32)
    memory = earlier[3].astype(jnp.float32)
    current = segment.astype(jnp.float32)

    def attend_book(book_id):
        keys_ok = allowed_keys[book_id]

        def attend_local(squeezed_rows, memory_rows, current_rows, *weights):
            return attend(squeezed_rows, memory_rows, current_rows, keys_ok, *weights)

        return attend_local

    attended = jnp.stack(
        [
            attend_book(book_id)(
                squeezed[book_id], memory[book_id], current[book_id], *attention_float
            )
            for book_id in range(book_count)
        ]
    )
    dense = (
        lax.all_gather(gathered[6], "head", axis=0, tiled=True),
        lax.all_gather(gathered[10], "head", axis=1, tiled=True),
        lax.all_gather(gathered[11], "head", axis=0, tiled=True),
        lax.all_gather(gathered[12], "head", axis=0, tiled=True),
    )
    output_full, up_full, up_bias_full, down_full = tuple(
        (piece.astype(jnp.float32) for piece in dense)
    )
    attended_rows = lax.all_to_all(
        attended.astype(jnp.bfloat16), "head", split_axis=1, concat_axis=2, tiled=True
    ).astype(jnp.float32)
    residual = lax.dynamic_slice_in_dim(current, share_start, share_rows, 1)
    result, finish_pull = jax.vjp(
        finish,
        attended_rows,
        residual,
        output_full,
        output_bias_full,
        first_gain_full,
        first_shift_full,
        up_full,
        up_bias_full,
        down_full,
        down_bias_full,
        second_gain_full,
        second_shift_full,
    )
    cotangent_rows = lax.dynamic_slice_in_dim(cotangent[:, 0], share_start, share_rows, 1).astype(
        jnp.float32
    )
    (
        attended_grad,
        residual_grad,
        output_full_grad,
        output_bias_grad,
        first_gain_grad,
        first_shift_grad,
        up_full_grad,
        up_bias_full_grad,
        down_full_grad,
        down_bias_grad,
        second_gain_grad,
        second_shift_grad,
    ) = finish_pull(cotangent_rows)
    heads_grad = lax.all_to_all(
        attended_grad.astype(jnp.bfloat16), "head", split_axis=2, concat_axis=1, tiled=True
    ).astype(jnp.float32)
    squeezed_grads = []
    memory_grads = []
    current_grads = []
    weight_grads = None
    for book_id in range(book_count):
        unused_value, attend_pull = jax.vjp(
            attend_book(book_id),
            squeezed[book_id],
            memory[book_id],
            current[book_id],
            *attention_float
        )
        pulled = attend_pull(heads_grad[book_id])
        squeezed_grads.append(pulled[0])
        memory_grads.append(pulled[1])
        current_grads.append(pulled[2])
        weight_grads = (
            tuple(pulled[3:])
            if weight_grads is None
            else tuple((total + extra for total, extra in zip(weight_grads, pulled[3:])))
        )
    squeezed_own = lax.psum_scatter(
        jnp.stack(squeezed_grads).astype(jnp.bfloat16), "head", scatter_dimension=2, tiled=True
    ).astype(jnp.float32)
    grouped_grad, squeeze_half_grad, squeeze_bias_half_grad = squeeze_pull(squeezed_own)
    stacked_grad = grouped_grad.reshape(book_count, 3 * row_count, width) * history_ok[:, :, None]
    returned = [
        stacked_grad[:, :row_count],
        stacked_grad[:, row_count : 2 * row_count],
        stacked_grad[:, 2 * row_count :],
        jnp.stack(memory_grads),
    ]
    summed = jnp.stack(current_grads)
    for offset, pieces in zip(range(4, 0, -1), returned):
        summed = summed + shifted(for_sending(pieces), "seq", -offset).astype(pieces.dtype)
    head_sums = (
        lax.psum_scatter(
            summed.astype(jnp.bfloat16), "head", scatter_dimension=1, tiled=True
        ).astype(jnp.float32),
        lax.psum_scatter(
            output_full_grad.astype(jnp.bfloat16), "head", scatter_dimension=0, tiled=True
        ).astype(jnp.float32),
        lax.psum_scatter(
            output_bias_grad.astype(jnp.bfloat16), "head", scatter_dimension=0, tiled=True
        ).astype(jnp.float32),
        lax.psum_scatter(
            first_gain_grad.astype(jnp.bfloat16), "head", scatter_dimension=0, tiled=True
        ).astype(jnp.float32),
        lax.psum_scatter(
            first_shift_grad.astype(jnp.bfloat16), "head", scatter_dimension=0, tiled=True
        ).astype(jnp.float32),
        lax.psum_scatter(
            up_full_grad.astype(jnp.bfloat16), "head", scatter_dimension=1, tiled=True
        ).astype(jnp.float32),
        lax.psum_scatter(
            up_bias_full_grad.astype(jnp.bfloat16), "head", scatter_dimension=0, tiled=True
        ).astype(jnp.float32),
        lax.psum_scatter(
            down_full_grad.astype(jnp.bfloat16), "head", scatter_dimension=0, tiled=True
        ).astype(jnp.float32),
        lax.psum_scatter(
            down_bias_grad.astype(jnp.bfloat16), "head", scatter_dimension=0, tiled=True
        ).astype(jnp.float32),
        lax.psum_scatter(
            second_gain_grad.astype(jnp.bfloat16), "head", scatter_dimension=0, tiled=True
        ).astype(jnp.float32),
        lax.psum_scatter(
            second_shift_grad.astype(jnp.bfloat16), "head", scatter_dimension=0, tiled=True
        ).astype(jnp.float32),
    )
    input_rows = head_sums[0] + residual_grad
    dense_halves = (head_sums[1], head_sums[5], head_sums[6], head_sums[7])
    small_halves = (
        head_sums[2],
        head_sums[3],
        head_sums[4],
        head_sums[8],
        head_sums[9],
        head_sums[10],
    )
    final = (
        lax.psum_scatter(weight_grads[0], "seq", scatter_dimension=0, tiled=True),
        lax.psum_scatter(weight_grads[1], "seq", scatter_dimension=0, tiled=True),
        lax.psum_scatter(weight_grads[2], "seq", scatter_dimension=0, tiled=True),
        lax.psum_scatter(weight_grads[3], "seq", scatter_dimension=0, tiled=True),
        lax.psum_scatter(weight_grads[4], "seq", scatter_dimension=0, tiled=True),
        lax.psum_scatter(weight_grads[5], "seq", scatter_dimension=0, tiled=True),
        lax.psum_scatter(dense_halves[0], "seq", scatter_dimension=0, tiled=True),
        lax.psum_scatter(small_halves[0], "seq", scatter_dimension=0, tiled=True),
        lax.psum_scatter(small_halves[1], "seq", scatter_dimension=0, tiled=True),
        lax.psum_scatter(small_halves[2], "seq", scatter_dimension=0, tiled=True),
        lax.psum_scatter(dense_halves[1], "seq", scatter_dimension=1, tiled=True),
        lax.psum_scatter(dense_halves[2], "seq", scatter_dimension=0, tiled=True),
        lax.psum_scatter(dense_halves[3], "seq", scatter_dimension=0, tiled=True),
        lax.psum_scatter(small_halves[3], "seq", scatter_dimension=0, tiled=True),
        lax.psum_scatter(small_halves[4], "seq", scatter_dimension=0, tiled=True),
        lax.psum_scatter(small_halves[5], "seq", scatter_dimension=0, tiled=True),
        lax.psum_scatter(squeeze_half_grad, "seq", scatter_dimension=1, tiled=True),
        lax.psum_scatter(squeeze_bias_half_grad, "seq", scatter_dimension=0, tiled=True),
    )
    return (
        result.astype(jnp.bfloat16)[:, None],
        input_rows.astype(jnp.bfloat16)[:, None],
        final[0],
        final[1],
        final[2],
        final[3],
        final[4],
        final[5],
        final[6],
        final[7],
        final[8],
        final[9],
        final[10],
        final[11],
        final[12],
        final[13],
        final[14],
        final[15],
        final[16],
        final[17],
    )


def solution(mesh):
    in_specs = (
        P(None, "seq", None, None),
        P(),
        P("seq", "head"),
        P("seq", "head"),
        P("seq", "head"),
        P("seq", "head"),
        P(("head", "seq")),
        P(("head", "seq")),
        P(("head", "seq"), None),
        P("seq"),
        P("seq"),
        P("seq"),
        P(None, ("head", "seq")),
        P(("head", "seq")),
        P(("head", "seq"), None),
        P("seq"),
        P("seq"),
        P("seq"),
        P(None, ("head", "seq")),
        P(("head", "seq")),
        P(None, "seq", None, None),
    )
    out_specs = (
        P(None, "seq", "head", None),
        P(None, "seq", "head", None),
        P("seq", "head"),
        P("seq", "head"),
        P("seq", "head"),
        P("seq", "head"),
        P(("head", "seq")),
        P(("head", "seq")),
        P(("head", "seq"), None),
        P(("head", "seq")),
        P(("head", "seq")),
        P(("head", "seq")),
        P(None, ("head", "seq")),
        P(("head", "seq")),
        P(("head", "seq"), None),
        P(("head", "seq")),
        P(("head", "seq")),
        P(("head", "seq")),
        P(None, ("head", "seq")),
        P(("head", "seq")),
    )
    return jax.shard_map(body, mesh=mesh, in_specs=in_specs, out_specs=out_specs, check_vma=False)
```

profile of v0, /device:TPU:6, one launch (start us, length us, event | category | flops | bytes accessed | tf_op | source)
XLA Modules:
  0.0 1794.4 jit_solution(16465553769211175014)
XLA Ops:
  33.2 211.3 %all-reduce.33 = (bf16[512]{0:T(512)(128)(2,1)S(1)}, bf16[512]{0:T(512)(128)(2,1)S(1)}, bf16[512]{0:T(512)(128)(2,1)S(1)}, bf16[1024]{0:T(1024)(128)(2,1)}, bf16...) all-reduce(bf16[512]{0:T(512)(128)(2,1)S(1)} %dynamic-update-slice., ...), channel_id=1, replica_groups=mesh['head'=2,'seq'=16] {'seq'}, use_global_device_ids=true, to_apply=%add.8 | all-reduce | flops 7680 | bytes 30720
  274.9 11.9 fusion.33
  316.5 13.3 pad_bitcast_fusion
  329.8 19.1 %copy.246 = f32[1,4,512,2048]{3,1,2,0:T(4,128)S(1)} copy(f32[1,4,512,2048]{3,2,1,0:T(8,128)} %pad_bitcast_fusion) | data formatting | bytes 33554432
  348.9 11.7 slice.132
  360.7 47.2 %reshape.564 = f32[4192256]{0:T(1024)} reshape(f32[4,1048064]{1,0:T(4,128)} %slice.132) | data formatting | bytes 33538048
  407.9 24.8 %reshape.478 = f32[4,512,2047]{2,1,0:T(8,128)} reshape(f32[4192256]{0:T(1024)} %reshape.564) | data formatting | bytes 33538048 | tf_op jit(solution)/shard_map/reshape | solution.py:82
  440.8 13.6 pad_bitcast_fusion.1
  454.3 19.0 %copy.245 = f32[1,4,512,2048]{3,1,2,0:T(4,128)S(1)} copy(f32[1,4,512,2048]{3,2,1,0:T(8,128)} %pad_bitcast_fusion.1) | data formatting | bytes 33554432
  473.4 11.6 slice.126
  485.0 48.0 %reshape.566 = f32[4192256]{0:T(1024)} reshape(f32[4,1048064]{1,0:T(4,128)} %slice.126) | data formatting | bytes 33538048
  533.0 24.8 %reshape.472 = f32[4,512,2047]{2,1,0:T(8,128)} reshape(f32[4192256]{0:T(1024)} %reshape.566) | data formatting | bytes 33538048 | tf_op jit(solution)/shard_map/reshape | solution.py:82
  625.7 21.7 %all-gather = bf16[16,1,128]{2,1,0:T(2,128)(2,1)S(1)} all-gather(bf16[1,1,128]{2,1,0:T(2,128)(2,1)S(1)} %bitcast.364), channel_id=1, replica_groups=mesh['head'=2,'seq'=16] {'seq'}, dimensions={0}, use_global_device_ids=true | all-gather | bytes 4352 | tf_op jit(solution)/shard_map/all_gather | solution.py:210
  660.3 14.4 multiply_convert_fusion.1
  674.7 14.4 all-gather.36.cloned.1.call-done
  704.3 12.8 fusion.8
  740.8 11.9 all-to-all-done.1
  798.0 12.1 multiply_reduce_fusion.1
  879.0 16.1 reshape.568
  913.7 11.7 copy.276
  944.0 14.3 reshape.485
  987.8 16.3 reshape.570
  1023.2 12.2 copy.277
  1049.3 18.9 %collective-permute-done.5 = bf16[2,512,1024]{2,1,0:T(8,128)(2,1)} collective-permute-done((bf16[2,512,1024]{2,1,0:T(8,128)(2,1)}, bf16[2,512,1024]{2,1,0:T(8,128)(2,1)}, u32[]{:S(2)}, u32[]{:S(2)}) %collective-permute-start.5) | collective-permute-done | bytes 2097184 | tf_op jit(solution)/shard_map/ppermute | solution.py:15
  1152.3 98.7 %all-reduce.32 = (f32[512]{0:T(512)S(1)}, f32[512]{0:T(512)S(1)}, f32[512]{0:T(512)S(1)}, f32[512]{0:T(512)S(1)}, f32[512]{0:T(512)S(1)}, /*index=5*/f32[2048]{0...) all-reduce(f32[512]{0:T(512)S(1)} %add_bitcast_fusion.2, ...), channel_id=8, replica_groups=mesh['head'=2,'seq'=16] {'seq'}, use_global_device_ids=true, to_apply=%region_28.29.clone | all-reduce | flops 6656 | bytes 53248
  1259.3 24.7 %reduce-scatter.20.cloned.1.call-done = f32[64,512]{1,0:T(8,128)} async-done(((f32[1024,512]{1,0:T(8,128)}), f32[64,512]{1,0:T(8,128)}) %reduce-scatter.20.cloned.1.call-update) | async-done | bytes 131088 | tf_op jit(solution)/shard_map/reduce_scatter | solution.py:405
  1284.1 65.2 %reduce-scatter.22.cloned.1.call-done = f32[64,512]{1,0:T(8,128)} async-done(((f32[1024,512]{1,0:T(8,128)}), f32[64,512]{1,0:T(8,128)}) %reduce-scatter.22.cloned.1.call-update) | async-done | bytes 131088 | tf_op jit(solution)/shard_map/reduce_scatter | solution.py:406
  1349.3 64.9 %reduce-scatter.24.cloned.1.call-done = f32[64,512]{1,0:T(8,128)} async-done(((f32[1024,512]{1,0:T(8,128)}), f32[64,512]{1,0:T(8,128)}) %reduce-scatter.24.cloned.1.call-update) | async-done | bytes 131088 | tf_op jit(solution)/shard_map/reduce_scatter | solution.py:407
  1414.2 65.4 %reduce-scatter.28.cloned.1.call-done = f32[32,1024]{1,0:T(8,128)} async-done(((f32[512,1024]{1,0:T(8,128)}), f32[32,1024]{1,0:T(8,128)}) %reduce-scatter.28.cloned.1.call-update) | async-done | bytes 131088 | tf_op jit(solution)/shard_map/reduce_scatter | solution.py:410
  1479.5 89.0 %reduce-scatter.38.cloned.1.call-done = f32[3072,32]{0,1:T(8,128)} async-done(((f32[3072,512]{0,1:T(8,128)}), f32[3072,32]{0,1:T(8,128)}) %reduce-scatter.38.cloned.1.call-update) | async-done | bytes 393232 | tf_op jit(solution)/shard_map/reduce_scatter | solution.py:420
  1568.5 109.3 %reduce-scatter.32.cloned.1.call-done = f32[1024,128]{1,0:T(8,128)} async-done(((f32[1024,2048]{1,0:T(8,128)}), f32[1024,128]{1,0:T(8,128)}) %reduce-scatter.32.cloned.1.call-update) | async-done | bytes 524304 | tf_op jit(solution)/shard_map/reduce_scatter | solution.py:414
  1677.8 109.5 %reduce-scatter.36.cloned.1.call-done = f32[128,1024]{1,0:T(8,128)} async-done(((f32[2048,1024]{1,0:T(8,128)}), f32[128,1024]{1,0:T(8,128)}) %reduce-scatter.36.cloned.1.call-update) | async-done | bytes 524304 | tf_op jit(solution)/shard_map/reduce_scatter | solution.py:416
  (478 shorter events, 514.2 us)
Async XLA Ops:
  7.2 254.5 %all-gather.14.cloned.1.call-start = ((), (), s32[]{:S(2)}) async-start(), calls=%async_computation.15 | async-start | bytes 3342336 | tf_op jit(solution)/shard_map/all_gather | solution.py:215
  7.9 263.4 %all-gather.26.cloned.1.call-start = ((), (), s32[]{:S(2)}) async-start(), calls=%async_computation.21 | async-start | bytes 1114112 | tf_op jit(solution)/shard_map/all_gather | solution.py:205
  8.7 263.3 %all-gather.30.cloned.1.call-start = ((), (), s32[]{:S(2)}) async-start(), calls=%async_computation.23 | async-start | bytes 4456448 | tf_op jit(solution)/shard_map/all_gather | solution.py:209
  9.4 287.7 %all-gather.20.cloned.1.call-start = ((), (), s32[]{:S(2)}) async-start(), calls=%async_computation.18 | async-start | bytes 1114112 | tf_op jit(solution)/shard_map/all_gather | solution.py:199
  10.0 293.0 %all-gather.24.cloned.1.call-start = ((), (), s32[]{:S(2)}) async-start(), calls=%async_computation.20 | async-start | bytes 1114112 | tf_op jit(solution)/shard_map/all_gather | solution.py:202
  10.6 550.5 %all-gather.34.cloned.1.call-start = ((), (), s32[]{:S(2)}) async-start(), calls=%async_computation.25 | async-start | bytes 4456448 | tf_op jit(solution)/shard_map/all_gather | solution.py:211
  11.1 550.0 %all-gather.16.cloned.1.call-start = ((), (), s32[]{:S(2)}) async-start(), calls=%async_computation.16 | async-start | bytes 3145728 | tf_op jit(solution)/shard_map/all_gather | solution.py:253
  11.2 233.4 %collective-permute-start.2 = (bf16[2,512,1024]{2,1,0:T(8,128)(2,1)}, bf16[2,512,1024]{2,1,0:T(8,128)(2,1)S(1)}, u32[]{:S(2)}, u32[]{:S(2)}) collective-permute-start(bf16[2,512,1024]{2,1,0:T(8,128)(2,1)} %bitcast), channel_id=1, source_target_pairs={{0,2},{1,3},{2,4},{3,5},{4,6},{5,7},{6,8},{7,9},{8,10},{9,11},{10,... | collective-permute-start | bytes 6291464 | tf_op jit(solution)/shard_map/ppermute | solution.py:15
  14.7 230.0 %collective-permute-start.1 = (bf16[2,512,1024]{2,1,0:T(8,128)(2,1)}, bf16[2,512,1024]{2,1,0:T(8,128)(2,1)}, u32[]{:S(2)}, u32[]{:S(2)}) collective-permute-start(bf16[2,512,1024]{2,1,0:T(8,128)(2,1)} %bitcast), channel_id=1, source_target_pairs={{0,3},{1,4},{2,5},{3,6},{4,7},{5,8},{6,9},{7,10},{8,11},{9,12},{10... | collective-permute-start | bytes 6291464 | tf_op jit(solution)/shard_map/ppermute | solution.py:15
  18.7 225.9 %collective-permute-start = (bf16[2,512,1024]{2,1,0:T(8,128)(2,1)}, bf16[2,512,1024]{2,1,0:T(8,128)(2,1)}, u32[]{:S(2)}, u32[]{:S(2)}) collective-permute-start(bf16[2,512,1024]{2,1,0:T(8,128)(2,1)} %bitcast), channel_id=1, source_target_pairs={{0,4},{1,5},{2,6},{3,7},{4,8},{5,9},{6,10},{7,11},{8,12},{9,13},{1... | collective-permute-start | bytes 6291464 | tf_op jit(solution)/shard_map/ppermute | solution.py:15
  269.8 294.5 %all-gather.22.cloned.1.call-start = ((), (), s32[]{:S(2)}) async-start(), calls=%async_computation.19 | async-start | bytes 1114112 | tf_op jit(solution)/shard_map/all_gather | solution.py:200
  270.6 316.3 %all-gather.18.cloned.1.call-start = ((), (), s32[]{:S(2)}) async-start(), calls=%async_computation.17 | async-start | bytes 1114112 | tf_op jit(solution)/shard_map/all_gather | solution.py:201
  271.3 383.3 %all-gather.28.cloned.1.call-start = ((), (), s32[]{:S(2)}) async-start(), calls=%async_computation.22 | async-start | bytes 3145728 | tf_op jit(solution)/shard_map/all_gather | solution.py:276
  271.9 388.4 %all-gather.32.cloned.1.call-start = ((), (), s32[]{:S(2)}) async-start(), calls=%async_computation.24 | async-start | bytes 12582912 | tf_op jit(solution)/shard_map/all_gather | solution.py:277
  272.6 416.5 %all-gather.36.cloned.1.call-start = ((), (), s32[]{:S(2)}) async-start(), calls=%async_computation.26 | async-start | bytes 12582912 | tf_op jit(solution)/shard_map/all_gather | solution.py:279
  272.7 285.4 %collective-permute-start.3 = (bf16[2,512,1024]{2,1,0:T(8,128)(2,1)}, bf16[2,512,1024]{2,1,0:T(8,128)(2,1)}, u32[]{:S(2)}, u32[]{:S(2)}) collective-permute-start(bf16[2,512,1024]{2,1,0:T(8,128)(2,1)} %bitcast), channel_id=1, source_target_pairs={{0,1},{1,2},{2,3},{3,4},{4,5},{5,6},{6,7},{7,8},{8,9},{9,10},{10,1... | collective-permute-start | bytes 6291464 | tf_op jit(solution)/shard_map/ppermute | solution.py:15
  740.6 193.1 %reduce-scatter.16.cloned.1.call-start = ((), (), s32[]{:S(2)}) async-start(), calls=%async_computation.27 | async-start | bytes 3145728 | tf_op jit(solution)/shard_map/reduce_scatter | solution.py:344
  848.6 260.9 %reduce-scatter.26.cloned.1.call-start = ((), (), s32[]{:S(2)}) async-start(), calls=%async_computation.32 | async-start | bytes 3145728 | tf_op jit(solution)/shard_map/reduce_scatter | solution.py:362
  852.0 268.8 %reduce-scatter.30.cloned.1.call-start = ((), (), s32[]{:S(2)}) async-start(), calls=%async_computation.34 | async-start | bytes 12582912 | tf_op jit(solution)/shard_map/reduce_scatter | solution.py:374
  861.2 266.4 %reduce-scatter.34.cloned.1.call-start = ((), (), s32[]{:S(2)}) async-start(), calls=%async_computation.36 | async-start | bytes 12582912 | tf_op jit(solution)/shard_map/reduce_scatter | solution.py:380
  871.6 385.2 %reduce-scatter.18.cloned.1.call-start = ((), (), s32[]{:S(2)}) async-start(), calls=%async_computation.28 | async-start | bytes 3145728 | tf_op jit(solution)/shard_map/reduce_scatter | solution.py:359
  928.7 120.6 %collective-permute-start.7 = (bf16[2,512,1024]{2,1,0:T(8,128)(2,1)}, bf16[2,512,1024]{2,1,0:T(8,128)(2,1)}, u32[]{:S(2)}, u32[]{:S(2)}) collective-permute-start(bf16[2,512,1024]{2,1,0:T(8,128)(2,1)} %pad_maximum_fusion.4), channel_id=1, source_target_pairs={{1,0},{2,1},{3,2},{4,3},{5,4},{6,5},{7,6},{8,7},{9,8},{10,9},{11,1... | collective-permute-start | bytes 6291464 | tf_op jit(solution)/shard_map/ppermute | solution.py:15
  974.4 93.8 %collective-permute-start.5 = (bf16[2,512,1024]{2,1,0:T(8,128)(2,1)}, bf16[2,512,1024]{2,1,0:T(8,128)(2,1)}, u32[]{:S(2)}, u32[]{:S(2)}) collective-permute-start(bf16[2,512,1024]{2,1,0:T(8,128)(2,1)} %get-tuple-element.167), channel_id=1, source_target_pairs={{3,0},{4,1},{5,2},{6,3},{7,4},{8,5},{9,6},{10,7},{11,8},{12,9},{13... | collective-permute-start | bytes 6291464 | tf_op jit(solution)/shard_map/ppermute | solution.py:15
  975.7 92.5 %collective-permute-start.4 = (bf16[2,512,1024]{2,1,0:T(8,128)(2,1)}, bf16[2,512,1024]{2,1,0:T(8,128)(2,1)}, u32[]{:S(2)}, u32[]{:S(2)}) collective-permute-start(bf16[2,512,1024]{2,1,0:T(8,128)(2,1)} %get-tuple-element.165), channel_id=1, source_target_pairs={{4,0},{5,1},{6,2},{7,3},{8,4},{9,5},{10,6},{11,7},{12,8},{13,9},{1... | collective-permute-start | bytes 6291464 | tf_op jit(solution)/shard_map/ppermute | solution.py:15
  1075.4 184.0 %reduce-scatter.40.cloned.1.call-start = ((), (), s32[]{:S(2)}) async-start(), calls=%async_computation.39 | async-start | bytes 2228224
  1081.4 202.7 %reduce-scatter.20.cloned.1.call-start = ((), (), s32[]{:S(2)}) async-start(), calls=%async_computation.29 | async-start | bytes 2228224 | tf_op jit(solution)/shard_map/reduce_scatter | solution.py:405
  1088.8 260.5 %reduce-scatter.22.cloned.1.call-start = ((), (), s32[]{:S(2)}) async-start(), calls=%async_computation.30 | async-start | bytes 2228224 | tf_op jit(solution)/shard_map/reduce_scatter | solution.py:406
  1096.2 317.9 %reduce-scatter.24.cloned.1.call-start = ((), (), s32[]{:S(2)}) async-start(), calls=%async_computation.31 | async-start | bytes 2228224 | tf_op jit(solution)/shard_map/reduce_scatter | solution.py:407
  1109.5 370.1 %reduce-scatter.28.cloned.1.call-start = ((), (), s32[]{:S(2)}) async-start(), calls=%async_computation.33 | async-start | bytes 2228224 | tf_op jit(solution)/shard_map/reduce_scatter | solution.py:410
  1112.5 456.1 %reduce-scatter.38.cloned.1.call-start = ((), (), s32[]{:S(2)}) async-start(), calls=%async_computation.38 | async-start | bytes 6684672 | tf_op jit(solution)/shard_map/reduce_scatter | solution.py:420
  1120.8 557.1 %reduce-scatter.32.cloned.1.call-start = ((), (), s32[]{:S(2)}) async-start(), calls=%async_computation.35 | async-start | bytes 8912896 | tf_op jit(solution)/shard_map/reduce_scatter | solution.py:414
  1127.5 659.9 %reduce-scatter.36.cloned.1.call-start = ((), (), s32[]{:S(2)}) async-start(), calls=%async_computation.37 | async-start | bytes 8912896 | tf_op jit(solution)/shard_map/reduce_scatter | solution.py:416
  (100 other events, 1650.7 us)
Sparse Core Ops, SparseCore 0:
  10.3 57.2 all-gather.13
  69.7 39.9 all-gather.25
  111.9 66.9 all-gather.29
  180.9 40.0 all-gather.19
  223.1 36.9 all-gather.23
  262.1 56.4 all-gather.33
  320.8 33.2 all-gather.15
  356.2 37.9 all-gather.21
  396.4 36.8 all-gather.17
  434.7 32.0 all-gather.27
  468.3 103.9 all-gather.31
  573.7 115.3 all-gather.35
  848.7 32.0 reduce-scatter.15
  883.0 31.8 reduce-scatter.25
  917.0 99.2 reduce-scatter.29
  1018.6 99.2 reduce-scatter.33
  1119.9 32.2 reduce-scatter.17
  1156.8 62.2 reduce-scatter.39
  1223.5 60.5 reduce-scatter.19
  1288.7 60.5 reduce-scatter.21
  1353.6 60.5 reduce-scatter.23
  1418.9 60.5 reduce-scatter.27
  1484.1 84.4 reduce-scatter.37
  1573.6 104.2 reduce-scatter.31
  1683.0 104.3 reduce-scatter.35
where the time goes:
time: 1800 us; the launch traced here: 1790 us
  waiting for transfers between devices  580 us (32%)
  local copies, waits for them, and re-layouts  438 us (24%)
  blocking collectives  345 us (19%)
  matrix products  259 us (14%)
  other arithmetic  122 us (7%)
  starting transfers between devices  30.4 us (2%)
  between operations  20.2 us (1%)
    unnamed x3, blocking collectives  319 us
    unnamed x235, local copies, waits for them, and re-layouts  255 us
    dot_general x33, matrix products, matmul(): return jnp.dot(left, right)  168 us
    reduce_scatter x1, waiting for transfers between devices, body(): lax.psum_scatter(dense_halves[3], 'seq', scatter_dimension=0, tiled=True)  110 us
    reduce_scatter x1, waiting for transfers between devices, body(): lax.psum_scatter(dense_halves[1], 'seq', scatter_dimension=1, tiled=True)  109 us
    reduce_scatter x1, waiting for transfers between devices, body(): lax.psum_scatter(squeeze_half_grad, 'seq', scatter_dimension=1, tiled=True)  89 us
    reshape x4, local copies, waits for them, and re-layouts, realign(): flattened.reshape(head_count, row_count, col_count + row_count - 1)  69.4 us
    reduce_scatter x1, waiting for transfers between devices, body(): lax.psum_scatter(dense_halves[0], 'seq', scatter_dimension=0, tiled=True)  65.4 us
  transfers between devices with their start and end apart: 35, of which 10 were waited for; matrix products, arithmetic and copies ran while one was open for 37% of the time, Pallas kernels for 0%

commit v1 on v0

v1 whole, which is shorter than its diff:
```python
import functools

import jax
import jax.numpy as jnp
import numpy as np
from jax import lax
from jax.experimental import pallas as pl
from jax.experimental.pallas import tpu as pltpu
from jax.sharding import PartitionSpec as P

HD = 128
BF = jnp.bfloat16
F32 = jnp.float32
epsilon = 1e-05
MIB = 1024 * 1024


def mm(left, right, contract=((1,), (0,)), out=F32):
    return lax.dot_general(left, right, (contract, ((), ())), preferred_element_type=F32).astype(out)


def mm_nt(left, right, out=F32):
    return mm(left, right, ((1,), (1,)), out)


def mm_tn(left, right, out=F32):
    return mm(left, right, ((0,), (0,)), out)


def shifted(array, axis, by):
    count = lax.axis_size(axis)
    pairs = [(i, i + by) for i in range(count) if 0 <= i + by < count]
    return lax.ppermute(array, axis, pairs)


def table_rows(width, count):
    distance = np.arange(count - 1, -1, -1).astype(np.float32)[:, None]
    exponent = -np.arange(0, width, 2).astype(np.float32) / np.float32(width)
    frequency = np.power(np.float32(10000.0), exponent).astype(np.float32)
    angles = (distance * frequency[None, :]).astype(np.float32)
    return np.concatenate([np.sin(angles), np.cos(angles)], axis=1).astype(BF)


def squeeze_layout(rows):
    pad = -(-(rows // 3 + 2) // 16) * 16
    taps = np.zeros((3, rows, 3 * pad), np.float32)
    collect = np.zeros((rows, 3 * pad), np.float32)
    biased = np.zeros((3 * pad, 1), np.float32)
    for role in range(3):
        first = role * rows // 3
        for i in range(rows):
            flat = role * rows + i
            taps[flat % 3, i, role * pad + flat // 3 - first] = 1.0
            collect[flat // 3, role * pad + flat // 3 - first] = 1.0
        for c in range(first, ((role + 1) * rows - 1) // 3 + 1):
            if role == 0 or 3 * c >= role * rows:
                biased[role * pad + c - first] = 1.0
    return pad, taps.astype(BF), collect.astype(BF), biased


def attend_forward_kernel(bias_ref, cb_ref, pb_ref, q_ref, k_ref, v_ref, pl_ref, out_ref, p_ref, s_scr, x_scr):
    rows = q_ref.shape[0]
    keys = k_ref.shape[0]
    scale = HD ** (-0.5)
    q = q_ref[...]
    content_query = ((q + cb_ref[...]) * scale).astype(BF)
    place_query = ((q + pb_ref[...]) * scale).astype(BF)
    s_scr[...] = mm_nt(content_query, k_ref[...])
    x_scr[...] = mm_nt(place_query, pl_ref[...])
    step = 32
    bias = bias_ref[...]
    for start in range(0, rows, step):
        here = slice(start, start + step)
        located = pltpu.roll(
            x_scr[here], (start + keys - rows + 1) % keys, 1, stride=1, stride_axis=0
        )
        scores = s_scr[here] + located + bias
        row = start + lax.broadcasted_iota(jnp.int32, scores.shape, 0)
        col = lax.broadcasted_iota(jnp.int32, scores.shape, 1)
        scores = jnp.where(col <= 2 * rows + row, scores, -1e30)
        top = jnp.max(scores, axis=1, keepdims=True)
        weights = jnp.exp(scores - top)
        total = jnp.sum(weights, axis=1, keepdims=True)
        p_ref[0, here] = (weights * (1.0 / total)).astype(BF)
    out_ref[...] = mm(p_ref[0], v_ref[...]).astype(BF)


def attend_backward_kernel(
    cb_ref, pb_ref, q_ref, k_ref, v_ref, pl_ref, p_ref, do_ref,
    dq_ref, dcb_ref, dpb_ref, dk_ref, dv_ref, dpl_ref,
    dp_scr, ds_scr, dx_scr,
):
    rows = q_ref.shape[0]
    keys = k_ref.shape[0]
    scale = HD ** (-0.5)
    q = q_ref[...]
    content_query = ((q + cb_ref[...]) * scale).astype(BF)
    place_query = ((q + pb_ref[...]) * scale).astype(BF)
    block = 128
    flip = (
        lax.broadcasted_iota(jnp.int32, (block, block), 0)
        + lax.broadcasted_iota(jnp.int32, (block, block), 1)
        == block - 1
    ).astype(BF)
    dp_scr[...] = mm_nt(do_ref[...], v_ref[...])
    step = 32
    for start in range(0, rows, step):
        here = slice(start, start + step)
        prob = p_ref[0, here].astype(F32)
        dprob = dp_scr[here]
        delta = jnp.sum(prob * dprob, axis=1, keepdims=True)
        ds_scr[here] = (prob * (dprob - delta)).astype(BF)
    dv_ref[...] = mm_tn(do_ref[...], p_ref[0]).T.astype(BF)
    dk_ref[...] = mm_tn(content_query, ds_scr[...]).T.astype(BF)
    dcq = mm(ds_scr[...], k_ref[...]) * scale
    flipped = []
    for start in range(0, rows, block):
        here = slice(start, start + block)
        dp_scr[here] = mm(flip, ds_scr[here])
        flipped.append(mm(flip, place_query[here]).astype(BF))
        dx_scr[here] = pltpu.roll(
            dp_scr[here], rows - block - start, 1, stride=1, stride_axis=0
        ).astype(BF)
    dpl_ref[...] = mm_tn(jnp.concatenate(flipped, axis=0), dx_scr[...]).T.astype(BF)
    dpq_flipped = mm(dx_scr[...], pl_ref[...]) * scale
    dpq = []
    for start in range(0, rows, block):
        piece = dpq_flipped[start : start + block]
        high = piece.astype(BF)
        dpq.append(mm(flip, high) + mm(flip, (piece - high.astype(F32)).astype(BF)))
    dpq = jnp.concatenate(dpq, axis=0)
    dq_ref[...] = (dcq + dpq).astype(BF)
    dcb_ref[...] = jnp.sum(dcq, axis=0, keepdims=True)
    dpb_ref[...] = jnp.sum(dpq, axis=0, keepdims=True)


def attend_forward(key_bias, content_bias, position_bias, query, keys, values, places):
    rows, width = query.shape
    count = keys.shape[0]
    heads = width // HD
    row_spec = pl.BlockSpec((rows, HD), lambda h: (0, h))
    key_spec = pl.BlockSpec((count, HD), lambda h: (0, h))
    vec_spec = pl.BlockSpec((1, HD), lambda h: (0, h))
    return pl.pallas_call(
        attend_forward_kernel,
        grid=(heads,),
        in_specs=[pl.BlockSpec((1, count), lambda h: (0, 0)), vec_spec, vec_spec, row_spec, key_spec, key_spec, key_spec],
        out_specs=[row_spec, pl.BlockSpec((1, rows, count), lambda h: (h, 0, 0))],
        out_shape=[
            jax.ShapeDtypeStruct((rows, width), BF),
            jax.ShapeDtypeStruct((heads, rows, count), BF),
        ],
        scratch_shapes=[pltpu.VMEM((rows, count), F32), pltpu.VMEM((rows, count), F32)],
        compiler_params=pltpu.CompilerParams(vmem_limit_bytes=48 * MIB),
        cost_estimate=pl.CostEstimate(
            flops=6 * rows * count * width, bytes_accessed=2 * heads * rows * count, transcendentals=heads * rows * count
        ),
        name="attend_forward",
    )(key_bias, content_bias, position_bias, query, keys, values, places)


def attend_backward(content_bias, position_bias, query, keys, values, places, probs, d_out):
    rows, width = query.shape
    count = keys.shape[0]
    heads = width // HD
    row_spec = pl.BlockSpec((rows, HD), lambda h: (0, h))
    key_spec = pl.BlockSpec((count, HD), lambda h: (0, h))
    vec_spec = pl.BlockSpec((1, HD), lambda h: (0, h))
    p_spec = pl.BlockSpec((1, rows, count), lambda h: (h, 0, 0))
    return pl.pallas_call(
        attend_backward_kernel,
        grid=(heads,),
        in_specs=[vec_spec, vec_spec, row_spec, key_spec, key_spec, key_spec, p_spec, row_spec],
        out_specs=[row_spec, vec_spec, vec_spec, key_spec, key_spec, key_spec],
        out_shape=[
            jax.ShapeDtypeStruct((rows, width), BF),
            jax.ShapeDtypeStruct((1, width), F32),
            jax.ShapeDtypeStruct((1, width), F32),
            jax.ShapeDtypeStruct((count, width), BF),
            jax.ShapeDtypeStruct((count, width), BF),
            jax.ShapeDtypeStruct((count, width), BF),
        ],
        scratch_shapes=[
            pltpu.VMEM((rows, count), F32),
            pltpu.VMEM((rows, count), BF),
            pltpu.VMEM((rows, count), BF),
        ],
        compiler_params=pltpu.CompilerParams(vmem_limit_bytes=48 * MIB),
        cost_estimate=pl.CostEstimate(
            flops=12 * rows * count * width, bytes_accessed=2 * heads * rows * count, transcendentals=0
        ),
        name="attend_backward",
    )(content_bias, position_bias, query, keys, values, places, probs, d_out)


MESH = pl.DeviceIdType.MESH
CORE, XFLIP, YFLIP, UP, DOWN = range(5)


class Place:
    def __init__(self, count):
        self.count = count
        self.line_size = count // 4
        self.h = lax.axis_index("head")
        self.s = lax.axis_index("seq")
        self.a = self.s // 4
        self.b = (self.s // 2) % 2
        self.c = self.s % 2

    def seq_of(self, a, b, c):
        return a * 4 + b * 2 + c

    def neighbour(self, kind):
        s, h = self.s, self.h
        if kind == CORE:
            return (h, s + 1 - 2 * self.c)
        if kind == XFLIP:
            return (h, s + 2 - 4 * self.b)
        if kind == YFLIP:
            return (1 - h, s)
        return (h, s + 4) if kind == UP else (h, s - 4)

    def when(self, kind):
        if kind == UP:
            return pl.when(self.a < self.line_size - 1)
        if kind == DOWN:
            return pl.when(self.a > 0)
        return lambda run: run()

    def barrier(self):
        barrier = pltpu.get_barrier_semaphore()
        for kind in range(5):
            @self.when(kind)
            def _(kind=kind):
                pl.semaphore_signal(barrier, inc=1, device_id=self.neighbour(kind), device_id_type=MESH)
        ends = jnp.where(self.a == 0, 1, 0) + jnp.where(self.a == self.line_size - 1, 1, 0)
        pl.semaphore_wait(barrier, 5 - ends)


class Gather:
    def __init__(self, place, shards, fulls, views, orders, local_sem, send_sem, recv_sem):
        self.place, self.shards, self.fulls, self.views, self.orders = place, shards, fulls, views, orders
        self.local_sem, self.send_sem, self.recv_sem = local_sem, send_sem, recv_sem

    def view(self, u, h, s):
        return self.views[u](self.fulls[u], h, s)

    def copy(self, u, kind, h, s, own=False):
        slot = h * self.place.count + s
        line, plane = s // 4, slot // 2
        size = self.place.line_size
        sent = {UP: line, DOWN: size + line, XFLIP: 2 * size + plane, YFLIP: 6 * size + plane, CORE: 10 * size + plane}
        there = self.view(u, h, s)
        return pltpu.make_async_remote_copy(
            src_ref=self.shards[u] if own else there,
            dst_ref=there,
            send_sem=self.send_sem.at[u, sent[kind]],
            recv_sem=self.recv_sem.at[u, slot],
            device_id=self.place.neighbour(kind),
            device_id_type=MESH,
        )

    def local(self, u):
        return pltpu.make_async_copy(self.shards[u], self.view(u, self.place.h, self.place.s), self.local_sem.at[u])

    def sources(self):
        p = self.place
        found = []
        for t in range(p.line_size):
            for sign in ((1, -1) if t else (0,)):
                o = p.a - sign * t
                valid = None if not t else (o >= 0 if sign > 0 else o <= p.line_size - 1)
                for one in (0, 1):
                    for two in (0, 1):
                        if t or one or two:
                            found.append((t + one + two, o, sign, one, two, valid))
        return sorted(found, key=lambda e: e[0])

    def slot_of(self, u, o, one, two):
        p = self.place
        x, y = (one, two) if self.orders[u] == 0 else (two, one)
        h = 1 - p.h if y else p.h
        b = 1 - p.b if x else p.b
        return h, p.seq_of(o, b, p.c)

    def flips(self, u):
        return (XFLIP, YFLIP) if self.orders[u] == 0 else (YFLIP, XFLIP)

    def onward(self, u, sign, one, two):
        first, second = self.flips(u)
        kinds = []
        if not one and not two:
            kinds += [UP] if sign > 0 else [DOWN] if sign < 0 else [UP, DOWN]
            kinds += [first]
        if not two:
            kinds += [second]
        return kinds + [CORE]

    def send(self, u, kind, h, s, own, wait):
        @self.place.when(kind)
        def _():
            copy = self.copy(u, kind, h, s, own)
            if wait:
                copy.wait_send()
            else:
                copy.start()

    def steps(self):
        p = self.place
        units = range(len(self.shards))

        def begin(wait=False):
            for u in units:
                if wait:
                    self.local(u).wait()
                else:
                    self.local(u).start()
                for kind in self.onward(u, 0, 0, 0):
                    self.send(u, kind, p.h, p.s, True, wait)

        def pass_on(entry, wait):
            depth, o, sign, one, two, valid = entry

            def run():
                for u in units:
                    h, s = self.slot_of(u, o, one, two)
                    if not wait:
                        self.copy(u, CORE, h, s).wait_recv()
                    for kind in self.onward(u, sign, one, two):
                        self.send(u, kind, h, s, False, wait)

            if valid is None:
                run()
            else:
                pl.when(valid)(run)

        def finish():
            for h in (0, 1):
                for a in range(p.line_size):
                    for b in (0, 1):
                        for u in units:
                            self.copy(u, CORE, h, p.seq_of(a, b, 1 - p.c)).wait_recv()
            begin(True)
            for entry in self.sources():
                pass_on(entry, True)

        return [begin] + [functools.partial(pass_on, entry, False) for entry in self.sources()] + [finish]


def gather_kernel(count, small_names, *refs):
    (qkvp, sq, o, up, down, small), refs = refs[:6], refs[6:]
    (qkvp_f, sq_f, o_f, up_f, down_f, vec, vec_up), refs = refs[:7], refs[7:]
    small_f, local_sem, send_sem, recv_sem = refs
    place = Place(count)
    place.barrier()
    r, w = qkvp.shape[1:]

    def qkvp_view(ref, h, s):
        return ref.at[:, pl.ds(pl.multiple_of(s * r, r), r), pl.ds(pl.multiple_of(h * w, w), w)]

    def block_view(rows):
        return lambda ref, h, s: ref.at[pl.ds(pl.multiple_of((h * count + s) * rows, rows), rows)]

    shards = [qkvp, sq, up, down, o, small]
    fulls = [qkvp_f, sq_f, up_f, down_f, o_f, small_f]
    views = [qkvp_view] + [block_view(s.shape[0]) for s in shards[1:]]
    gather = Gather(place, shards, fulls, views, (0, 1, 0, 1, 1, 0), local_sem, send_sem, recv_sem)
    for step in gather.steps():
        step()
    for slot in range(2 * count):
        for name, row, at, size, target in small_names:
            if size * 2 * count > vec.shape[1] * (4 if name == "ub" else 1) and slot >= count:
                continue
            ref = vec_up if name == "ub" else vec
            ref[target : target + 1, slot * size : (slot + 1) * size] = small_f[slot * 8 + row : slot * 8 + row + 1, at : at + size]


def small_layout(both, seq):
    names = []
    for i, name in enumerate(("cb", "pb", "sb")):
        names.append((name, 0, i * both, both, i))
    names.append(("ub", 1, 0, 4 * both, 0))
    for i, name in enumerate(("ob", "g1", "s1", "db", "g2", "s2")):
        names.append((name, 2 + i // 2, (i % 2) * seq, seq, 3 + i))
    return names


def gather_all(w):
    count = lax.axis_size("seq")
    both, seq = w["cb"].shape[0], w["ob"].shape[0]
    width = both * 2 * count
    layout = small_layout(both, seq)
    lines = [[] for _ in range(8)]
    for name, row, at, size, target in layout:
        lines[row].append(w[name].astype(F32))
    lines = [jnp.concatenate(parts) if parts else jnp.zeros((128,), F32) for parts in lines]
    small = jnp.stack([jnp.pad(line, (0, 128 - line.shape[0])) for line in lines])
    qkvp = jnp.stack([w["q"], w["k"], w["v"], w["p"]])
    shards = [qkvp, w["sq"], w["o"], w["up"], w["down"], small]
    any_spec = pl.BlockSpec(memory_space=pl.ANY)
    vmem_spec = pl.BlockSpec(memory_space=pltpu.VMEM)
    units = len(shards)
    outs = pl.pallas_call(
        functools.partial(gather_kernel, count, layout),
        in_specs=[any_spec] * 6,
        out_specs=[any_spec] * 5 + [vmem_spec] * 2,
        out_shape=[
            jax.ShapeDtypeStruct((4, qkvp.shape[1] * count, qkvp.shape[2] * 2), BF),
            *[jax.ShapeDtypeStruct((s.shape[0] * 2 * count, s.shape[1]), BF) for s in shards[1:5]],
            jax.ShapeDtypeStruct((16, width), F32),
            jax.ShapeDtypeStruct((1, 4 * width), F32),
        ],
        scratch_shapes=[
            pltpu.VMEM((8 * 2 * count, 128), F32),
            pltpu.SemaphoreType.DMA((units,)),
            pltpu.SemaphoreType.DMA((units, 14 * (count // 4))),
            pltpu.SemaphoreType.DMA((units, 2 * count)),
        ],
        compiler_params=pltpu.CompilerParams(collective_id=0, has_side_effects=True, vmem_limit_bytes=16 * MIB),
        name="gather_weights",
    )(*shards)
    full = dict(zip(("q", "k", "v", "p"), outs[0]))
    full.update(zip(("sq", "o", "up", "down"), outs[1:5]))
    for name, row, at, size, target in layout:
        full[name] = outs[6] if name == "ub" else outs[5][target : target + 1]
    return full


class Scatter:
    def __init__(self, place, view, order, mine, core, first, second, line, local_sem, send_sem, recv_sem):
        self.place, self.view, self.order = place, view, order
        self.mine, self.core, self.first, self.second, self.line = mine, core, first, second, line
        self.local_sem, self.send_sem, self.recv_sem = local_sem, send_sem, recv_sem
        self.f, self.g = (place.h, place.b) if order == 0 else (place.b, place.h)
        self.flips = (YFLIP, XFLIP) if order == 0 else (XFLIP, YFLIP)

    def index(self, f, g, a):
        return (f * 2 + g) * self.place.line_size + a

    def slot(self, f, g, a, c):
        h, b = (f, g) if self.order == 0 else (g, f)
        return h, self.place.seq_of(a, b, c)

    def remote(self, source, target, kind, send_at, recv_at):
        return pltpu.make_async_remote_copy(
            src_ref=source,
            dst_ref=target,
            send_sem=self.send_sem.at[send_at],
            recv_sem=self.recv_sem.at[recv_at],
            device_id=self.place.neighbour(kind),
            device_id_type=MESH,
        )

    def core_copy(self, f, g, a):
        i = self.index(f, g, a)
        return self.remote(self.core.at[i], self.core.at[i], CORE, i, i)

    def first_copy(self, g, a):
        n = self.place.line_size
        to = g * n + a
        return self.remote(self.mine.at[self.index(1 - self.f, g, a)], self.first.at[to], self.flips[0], 4 * n + to, 4 * n + to)

    def second_copy(self, a):
        n = self.place.line_size
        return self.remote(self.mine.at[self.index(self.f, 1 - self.g, a)], self.second.at[a], self.flips[1], 6 * n + a, 6 * n + a)

    def line_copy(self, kind, a):
        n = self.place.line_size
        way = 0 if kind == UP else 1
        at = (7 + way) * n + a
        return self.remote(self.mine.at[self.index(self.f, self.g, a)], self.line.at[way * n + a], kind, at, at)

    def start(self, f, g, a):
        p = self.place
        i = self.index(f, g, a)
        for source, target in self.view(*self.slot(f, g, a, 1 - p.c), self.core.at[i]):
            self.remote(source, target, CORE, i, i).start()
        for source, target in self.view(*self.slot(f, g, a, p.c), self.mine.at[i]):
            pltpu.make_async_copy(source, target, self.local_sem.at[i]).start()

    def arrive(self, f, g, a):
        i = self.index(f, g, a)
        pltpu.make_async_copy(self.mine.at[i], self.mine.at[i], self.local_sem.at[i]).wait()
        self.core_copy(f, g, a).wait_recv()

    def add(self, i, *refs):
        total = self.mine[i].astype(F32)
        for ref, at in refs:
            total = total + ref[at].astype(F32)
        self.mine[i] = total.astype(self.mine.dtype)

    def loop(self, count, run):
        def body(i, carry):
            run(i)
            return carry

        lax.fori_loop(0, count, body, 0)

    def begin(self):
        n = self.place.line_size
        self.loop(2 * n, lambda i: self.start(1 - self.f, i // n, i % n))
        self.loop(n, lambda i: self.start(self.f, 1 - self.g, i))
        self.loop(n, lambda i: self.start(self.f, self.g, i))

    def flip_first(self):
        n = self.place.line_size

        def run(i):
            g, a = i // n, i % n
            self.arrive(1 - self.f, g, a)
            at = self.index(1 - self.f, g, a)
            self.add(at, (self.core, at))
            self.first_copy(g, a).start()

        self.loop(2 * n, run)

    def flip_second(self):
        n = self.place.line_size

        def run(a):
            self.arrive(self.f, 1 - self.g, a)
            self.first_copy(1 - self.g, a).wait_recv()
            at = self.index(self.f, 1 - self.g, a)
            self.add(at, (self.core, at), (self.first, (1 - self.g) * n + a))
            self.second_copy(a).start()

        self.loop(n, run)

    def settle(self, a):
        n = self.place.line_size
        self.arrive(self.f, self.g, a)
        self.first_copy(self.g, a).wait_recv()
        self.second_copy(a).wait_recv()
        at = self.index(self.f, self.g, a)
        return at, [(self.core, at), (self.first, self.g * n + a), (self.second, a)]

    def along(self):
        p = self.place
        n = p.line_size
        for d in range(n - 1, 0, -1):
            for kind, way, a, inside, fed in (
                (UP, 0, p.a + d, p.a + d <= n - 1, p.a > 0),
                (DOWN, 1, p.a - d, p.a - d >= 0, p.a < n - 1),
            ):
                @pl.when(inside)
                def _(kind=kind, way=way, a=a, fed=fed):
                    at, refs = self.settle(a)

                    @pl.when(fed)
                    def _():
                        self.line_copy(kind, a).wait_recv()
                        self.add(at, *refs, (self.line, way * n + a))

                    @pl.when(jnp.logical_not(fed))
                    def _():
                        self.add(at, *refs)

                    self.line_copy(kind, a).start()

    def finish(self, store):
        p = self.place
        n = p.line_size
        at, refs = self.settle(p.a)
        self.add(at, *refs)
        for kind, way, fed in ((UP, 0, p.a > 0), (DOWN, 1, p.a < n - 1)):
            @pl.when(fed)
            def _(kind=kind, way=way):
                self.line_copy(kind, p.a).wait_recv()
                self.add(at, (self.line, way * n + p.a))
        store(self.mine[at].astype(F32))
        self.loop(4 * n, lambda i: self.core_copy(i // (2 * n), (i // n) % 2, i % n).wait_send())
        self.loop(2 * n, lambda i: self.first_copy(i // n, i % n).wait_send())
        self.loop(n, lambda a: self.second_copy(a).wait_send())

        def line_done(a):
            for kind, inside in ((UP, a > p.a), (DOWN, a < p.a)):
                @pl.when(inside)
                def _(kind=kind):
                    self.line_copy(kind, a).wait_send()

        self.loop(n, line_done)


def scatter_scratch(count, shape, dtype=BF):
    n = count // 4
    return [
        *[pltpu.VMEM((k * n, *shape), dtype) for k in (4, 4, 2, 1, 2)],
        pltpu.SemaphoreType.DMA((4 * n,)),
        pltpu.SemaphoreType.DMA((9 * n,)),
        pltpu.SemaphoreType.DMA((9 * n,)),
    ]


def block_pairs(ref, rows, count):
    def view(h, s, target):
        return [(ref.at[pl.ds(pl.multiple_of((h * count + s) * rows, rows), rows)], target)]

    return view


def square_pairs(refs, r, w):
    def view(h, s, target):
        here = (pl.ds(pl.multiple_of(s * r, r), r), pl.ds(pl.multiple_of(h * w, w), w))
        return [(ref.at[here], target.at[i]) for i, ref in enumerate(refs)]

    return view


def run_scatters(units, stores, between=lambda at: None):
    for unit in units:
        unit.begin()
    between(0)
    for unit in units:
        unit.flip_first()
    between(1)
    for unit in units:
        unit.flip_second()
    between(2)
    for unit in units:
        unit.along()
    between(3)
    for unit, store in zip(units, stores):
        unit.finish(store)
    between(4)


def scatter_dense_kernel(count, up, down, o, up_out, down_out, o_out, *scratch):
    place = Place(count)
    place.barrier()
    units, stores = [], []
    for i, (ref, out, order) in enumerate(((up, up_out, 0), (down, down_out, 1), (o, o_out, 1))):
        units.append(Scatter(place, block_pairs(ref, out.shape[0], count), order, *scratch[8 * i : 8 * i + 8]))

        def store(value, out=out):
            out[...] = value

        stores.append(store)
    run_scatters(units, stores)


def scatter_attention_kernel(
    count, q, k, v, p, sq, vec, q_out, k_out, v_out, p_out, sq_out, vec_out, ub_out, sums, parts, vec_send, vec_recv, *scratch
):
    place = Place(count)
    place.barrier()
    r, w = q_out.shape
    units = [
        Scatter(place, square_pairs((q, k, v, p), r, w), 0, *scratch[:8]),
        Scatter(place, block_pairs(sq, sq_out.shape[0], count), 1, *scratch[8:]),
    ]

    def store_square(value):
        for i, out in enumerate((q_out, k_out, v_out, p_out)):
            out[...] = value[i]

    def store_sq(value):
        sq_out[...] = value

    def vec_copy(kind):
        return pltpu.make_async_remote_copy(
            src_ref=sums.at[kind],
            dst_ref=parts.at[kind],
            send_sem=vec_send.at[kind],
            recv_sem=vec_recv.at[kind],
            device_id=place.neighbour(kind),
            device_id_type=MESH,
        )

    def between(at):
        kinds = (CORE, XFLIP, YFLIP)
        if at == 0:
            sums[CORE] = vec[...]
            vec_copy(CORE).start()
        elif at < 3:
            vec_copy(kinds[at - 1]).wait_recv()
            sums[kinds[at]] = sums[kinds[at - 1]] + parts[kinds[at - 1]]
            vec_copy(kinds[at]).start()
        elif at == 3:
            vec_copy(YFLIP).wait_recv()
            total = sums[YFLIP] + parts[YFLIP]
            ends = (place.a > 0, place.a < place.line_size - 1)
            sums[UP] = total
            sums[DOWN] = total
            for kind, fed in ((UP, ends[0]), (DOWN, ends[1])):
                @pl.when(fed)
                def _(kind=kind):
                    vec_copy(kind).wait_recv()
                    sums[kind] = sums[kind] + parts[kind]

                @place.when(kind)
                def _(kind=kind):
                    vec_copy(kind).start()
        else:
            total = sums[UP] + sums[DOWN] - (sums[YFLIP] + parts[YFLIP])
            width = total.shape[1]
            both = vec_out.shape[1]
            k = place.h * count + place.s
            mine = pltpu.roll(total, lax.rem(width - k * both, width), 1)
            vec_out[...] = mine[:, :both]
            wide = ub_out.shape[1]
            flat = k * wide
            lanes = lax.rem(flat, width)
            mine = pltpu.roll(total, lax.rem(width - lanes, width), 1)[:, :wide]
            row = lax.broadcasted_iota(jnp.int32, mine.shape, 0)
            ub_out[...] = jnp.sum(jnp.where(row == 12 + flat // width, mine, 0.0), axis=0, keepdims=True)
            for kind in range(5):
                @place.when(kind)
                def _(kind=kind):
                    vec_copy(kind).wait_send()

    run_scatters(units, (store_square, store_sq), between)


def scatter_dense(g):
    count = lax.axis_size("seq")
    names = ("up", "down", "o")
    shapes = [(g[n].shape[0] // (2 * count), g[n].shape[1]) for n in names]
    scratch = []
    for shape in shapes:
        scratch += scatter_scratch(count, shape)
    outs = pl.pallas_call(
        functools.partial(scatter_dense_kernel, count),
        in_specs=[pl.BlockSpec(memory_space=pl.ANY)] * 3,
        out_specs=[pl.BlockSpec(memory_space=pltpu.VMEM)] * 3,
        out_shape=[jax.ShapeDtypeStruct(shape, F32) for shape in shapes],
        scratch_shapes=scratch,
        compiler_params=pltpu.CompilerParams(collective_id=1, has_side_effects=True, vmem_limit_bytes=48 * MIB),
        name="scatter_dense",
    )(*[g[n] for n in names])
    return dict(zip(names, outs))


VECTORS = ("cb", "pb", "sb", "ob", "g1", "s1", "db", "g2", "s2")


def scatter_attention(g):
    count = lax.axis_size("seq")
    width = g["q"].shape[0]
    both = width // (2 * count)
    lines = [g[n].reshape(1, width) for n in VECTORS]
    vec = jnp.concatenate(lines + [jnp.zeros((12 - len(lines), width), F32), g["ub"].reshape(-1, width)], axis=0)
    square = (width // count, width // 2)
    narrow = (both, g["sq"].shape[1])
    vmem = pl.BlockSpec(memory_space=pltpu.VMEM)
    outs = pl.pallas_call(
        functools.partial(scatter_attention_kernel, count),
        in_specs=[pl.BlockSpec(memory_space=pl.ANY)] * 5 + [vmem],
        out_specs=[vmem] * 7,
        out_shape=[jax.ShapeDtypeStruct(square, F32)] * 4
        + [jax.ShapeDtypeStruct(s, F32) for s in (narrow, (16, both), (1, 4 * both))],
        scratch_shapes=[
            pltpu.VMEM((5, 16, width), F32),
            pltpu.VMEM((5, 16, width), F32),
            pltpu.SemaphoreType.DMA((5,)),
            pltpu.SemaphoreType.DMA((5,)),
            *scatter_scratch(count, (4, *square)),
            *scatter_scratch(count, narrow),
        ],
        compiler_params=pltpu.CompilerParams(collective_id=2, has_side_effects=True, vmem_limit_bytes=48 * MIB),
        name="scatter_attention",
    )(g["q"], g["k"], g["v"], g["p"], g["sq"], vec)
    final = dict(zip(("q", "k", "v", "p", "sq"), outs[:5]))
    final.update({n: outs[5][i] for i, n in enumerate(VECTORS)})
    final["ub"] = outs[6].reshape(4 * both)
    return final


def normalize(values):
    centre = values - jnp.mean(values, axis=-1, keepdims=True)
    spread = jnp.mean(centre * centre, axis=-1, keepdims=True)
    scale = lax.rsqrt(spread + epsilon)
    return centre * scale, scale


def normalize_back(grad, gain, unit, scale):
    pulled = grad * gain
    return scale * (
        pulled
        - jnp.mean(pulled, axis=-1, keepdims=True)
        - unit * jnp.mean(pulled * unit, axis=-1, keepdims=True)
    )


def gelu_parts(u):
    root = np.float32(np.sqrt(2.0 / np.pi))
    inner = root * (u + 0.044715 * u * u * u)
    tanh = jnp.tanh(inner)
    value = 0.5 * u * (1.0 + tanh)
    slope = 0.5 * (1.0 + tanh) + 0.5 * u * (1.0 - tanh * tanh) * root * (1.0 + 3 * 0.044715 * u * u)
    return value, slope


def exchange_rows(array, head):
    half = array.shape[0] // 2
    mine = lax.dynamic_slice_in_dim(array, head * half, half, 0)
    theirs = lax.dynamic_slice_in_dim(array, (1 - head) * half, half, 0)
    other = lax.ppermute(theirs, "head", [(0, 1), (1, 0)])
    first = jnp.where(head == 0, mine, other)
    second = jnp.where(head == 0, other, mine)
    return jnp.stack([first, second])[:, None]


def body(
    inputs, lengths,
    query_weight, key_weight, value_weight, position_weight, content_bias, position_bias,
    output_weight, output_bias, first_gain, first_shift, up_weight, up_bias, down_weight, down_bias,
    second_gain, second_shift, squeeze_weight, squeeze_bias, cotangent,
):
    seq = lax.axis_index("seq")
    head = lax.axis_index("head")
    rows, width = inputs.shape[2:]

    x = lax.dynamic_index_in_dim(inputs[:, 0], head, 0, keepdims=False)
    book_lengths = lax.dynamic_index_in_dim(lengths, head, 0, keepdims=False)
    padded_lengths = jnp.concatenate([jnp.zeros((4,), jnp.int32), book_lengths])
    window = lax.dynamic_slice_in_dim(padded_lengths, seq, 5, 0)
    own_length = window[4]

    memory = shifted(x, "seq", 1)
    w = gather_all(
        dict(
            q=query_weight, k=key_weight, v=value_weight, p=position_weight,
            o=output_weight, up=up_weight.T, down=down_weight, sq=squeeze_weight.T,
            cb=content_bias, pb=position_bias, ob=output_bias, g1=first_gain, s1=first_shift, ub=up_bias,
            db=down_bias, g2=second_gain, s2=second_shift, sb=squeeze_bias,
        )
    )
    cb, pb, ob, g1, s1, ub, db, g2, s2, sb = (
        w[n] for n in ("cb", "pb", "ob", "g1", "s1", "ub", "db", "g2", "s2", "sb")
    )

    pad, taps, collect, biased = squeeze_layout(rows)
    row_ids = jnp.arange(rows)
    kept = (row_ids < own_length)[:, None]
    masked = jnp.where(kept, x, jnp.zeros_like(x))
    made = biased * sb
    for tap in range(3):
        made = made + mm_nt(mm_tn(taps[tap], masked, BF), w["sq"][:, tap * width : (tap + 1) * width])
    made = made.astype(BF)
    arrived = jnp.concatenate(
        [shifted(made[role * pad : (role + 1) * pad], "seq", 4 - role) for role in range(3)], axis=0
    )
    squeezed = mm(collect, arrived, out=BF)
    keys_in = jnp.concatenate([squeezed, memory, x], axis=0)

    flat = np.arange(0, 3 * rows, 3)
    history_ok = jnp.asarray(flat % rows) < window[:3][flat // rows]
    valid = jnp.concatenate([history_ok, row_ids < window[3], row_ids < window[4]])
    key_bias = jnp.where(valid, 0.0, -1e30).astype(F32)[None]

    query = mm(x, w["q"])
    keys = mm(keys_in, w["k"], out=BF)
    values = mm(keys_in, w["v"], out=BF)
    table = jnp.asarray(table_rows(width, 3 * rows))
    places = mm(table, w["p"], out=BF)
    attended, probs = attend_forward(key_bias, cb, pb, query, keys, values, places)

    blended = x.astype(F32) + mm(attended, w["o"]) + ob
    unit1, scale1 = normalize(blended)
    normed = (unit1 * g1 + s1).astype(BF)
    u = mm_nt(normed, w["up"]) + ub
    hidden_f, slope = gelu_parts(u)
    hidden = hidden_f.astype(BF)
    unit2, scale2 = normalize(normed.astype(F32) + mm(hidden, w["down"]) + db)
    outputs = (unit2 * g2 + s2).astype(BF)

    grads = {}
    ct = lax.dynamic_index_in_dim(cotangent[:, 0], head, 0, keepdims=False).astype(F32)
    grads["g2"] = jnp.sum(ct * unit2, axis=0)
    grads["s2"] = jnp.sum(ct, axis=0)
    dy = normalize_back(ct, g2, unit2, scale2)
    grads["db"] = jnp.sum(dy, axis=0)
    dy_b = dy.astype(BF)
    grads["down"] = mm_tn(hidden, dy_b, BF)
    du = (mm_nt(dy_b, w["down"]) * slope).astype(BF)
    grads["ub"] = jnp.sum(du.astype(F32), axis=0)
    grads["up"] = mm_tn(du, normed, BF)
    dnormed = dy + mm(du, w["up"])
    grads["g1"] = jnp.sum(dnormed * unit1, axis=0)
    grads["s1"] = jnp.sum(dnormed, axis=0)
    dblended = normalize_back(dnormed, g1, unit1, scale1)
    grads["ob"] = jnp.sum(dblended, axis=0)
    dblended_b = dblended.astype(BF)
    grads["o"] = mm_tn(attended, dblended_b, BF)
    dattended = mm_nt(dblended_b, w["o"], BF)

    dq, dcb, dpb, dk, dv, dplaces = attend_backward(cb, pb, query, keys, values, places, probs, dattended)
    grads["cb"] = dcb[0]
    grads["pb"] = dpb[0]
    dkeys_in = mm_nt(dk, w["k"]) + mm_nt(dv, w["v"])
    dsqueezed = dkeys_in[:rows].astype(BF)
    grads["sb"] = jnp.sum(dsqueezed.astype(F32), axis=0)
    dmade = mm_tn(collect, dsqueezed, BF)
    returned = jnp.concatenate(
        [shifted(dmade[role * pad : (role + 1) * pad], "seq", role - 4) for role in range(3)], axis=0
    )
    from_next = shifted(dkeys_in[rows : 2 * rows].astype(BF), "seq", -1)
    grads["q"] = mm_tn(x, dq, BF)
    grads["k"] = mm_tn(keys_in, dk, BF)
    grads["v"] = mm_tn(keys_in, dv, BF)
    grads["p"] = mm_tn(table, dplaces, BF)
    dx = dblended + mm_nt(dq, w["q"]) + dkeys_in[2 * rows :] + from_next.astype(F32)
    dmasked = jnp.zeros((rows, width), F32)
    sq_grads = []
    for tap in range(3):
        spread = mm(taps[tap], returned, out=BF)
        dmasked = dmasked + mm(spread, w["sq"][:, tap * width : (tap + 1) * width])
        sq_grads.append(mm_tn(spread, masked, BF))
    grads["sq"] = jnp.concatenate(sq_grads, axis=1)
    dx = dx + jnp.where(kept, dmasked, 0.0)

    final = {**scatter_dense(grads), **scatter_attention(grads)}
    return (
        exchange_rows(outputs, head),
        exchange_rows(dx.astype(BF), head),
        final["q"], final["k"], final["v"], final["p"], final["cb"], final["pb"],
        final["o"], final["ob"], final["g1"], final["s1"], final["up"].T, final["ub"],
        final["down"], final["db"], final["g2"], final["s2"], final["sq"].T, final["sb"],
    )


def solution(mesh):
    both = ("head", "seq")
    matrix = P("seq", "head")
    in_specs = (
        P(None, "seq", None, None), P(), matrix, matrix, matrix, matrix, P(both), P(both),
        P(both, None), P("seq"), P("seq"), P("seq"), P(None, both), P(both), P(both, None), P("seq"),
        P("seq"), P("seq"), P(None, both), P(both), P(None, "seq", None, None),
    )
    rows = P(None, "seq", "head", None)
    out_specs = (
        rows, rows, matrix, matrix, matrix, matrix, P(both), P(both),
        P(both, None), P(both), P(both), P(both), P(None, both), P(both), P(both, None), P(both),
        P(both), P(both), P(None, both), P(both),
    )
    return jax.shard_map(body, mesh=mesh, in_specs=in_specs, out_specs=out_specs, check_vma=False)
```

time: 1800 us -> 751 us (0.42)
  waiting for transfers between devices: 580 us -> 8.1 us
  Pallas kernels: 0 us -> 474 us
  local copies, waits for them, and re-layouts: 438 us -> 32.8 us
  blocking collectives: 345 us -> 0 us
  other arithmetic: 122 us -> 19.3 us
  matrix products: 259 us -> 181 us
  between operations: 20.2 us -> 2.07 us
    reduce_scatter x12 -> x0, waiting for transfers between devices: 528 us -> none  [the longest x1 110 us: body(): lax.psum_scatter(dense_halves[3], 'seq', scatter_dimension=0, tiled=True)]
    pallas_call x0 -> x5, Pallas kernels: none -> 474 us  [the longest x1 155 us: gather_all(): pl.pallas_call(functools.partial(gather_kernel, count, layout), in_specs=...]
    unnamed x3 -> x0, blocking collectives: 319 us -> none
    unnamed x235 -> x156, local copies, waits for them, and re-layouts: 255 us -> 24.5 us
    reshape x14 -> x1, local copies, waits for them, and re-layouts: 92.5 us -> 0.62 us  [scatter_attention(): g['ub'].reshape(-1, width)]
    dot_general x51 -> x42, matrix products: 259 us -> 181 us  [mm(): lax.dot_general(left, right, (contract, ((), ())), preferred_element_type...]
    convert_element_type x29 -> x0, other arithmetic: 51.5 us -> none  [the longest x2 17.2 us: low_back(): return make_rounders()[1](value)]
    slice x9 -> x4, local copies, waits for them, and re-layouts: 33 us -> 2.89 us  [the longest x1 1.06 us: body(): from_next = shifted(dkeys_in[rows:2 * rows].astype(BF), 'seq', -1)]
  transfers between devices with their start and end apart: 35 -> 10, of which waited for: 10 -> 1; matrix products, arithmetic and copies ran while one was open for 37% -> 13% of each run, Pallas kernels for 0% -> 55%
where the time goes in v1:
time: 751 us; the launch traced here: 745 us
  Pallas kernels  474 us (63%)
  matrix products  181 us (24%)
  local copies, waits for them, and re-layouts  32.8 us (4%)
  starting transfers between devices  27.3 us (4%)
  other arithmetic  19.3 us (3%)
  waiting for transfers between devices  8.1 us (1%)
    dot_general x42, matrix products, mm(): lax.dot_general(left, right, (contract, ((), ())), preferred_element_type...  181 us
    pallas_call x1, Pallas kernels, gather_all(): pl.pallas_call(functools.partial(gather_kernel, count, layout), in_specs=...  155 us
    pallas_call x1, Pallas kernels, scatter_dense(): pl.pallas_call(functools.partial(scatter_dense_kernel, count), in_specs=[...  139 us
    pallas_call x1, Pallas kernels, scatter_attention(): pl.pallas_call(functools.partial(scatter_attention_kernel, count), in_spe...  118 us
    pallas_call x1, Pallas kernels, attend_backward(): pl.pallas_call(attend_backward_kernel, grid=(heads,), in_specs=[vec_spec,...  33.7 us
    pallas_call x1, Pallas kernels, attend_forward(): pl.pallas_call(attend_forward_kernel, grid=(heads,), in_specs=[pl.BlockSp...  28.6 us
    ppermute x8, starting transfers between devices, shifted(): return lax.ppermute(array, axis, pairs)  25.5 us
    unnamed x156, local copies, waits for them, and re-layouts  24.5 us
  transfers between devices with their start and end apart: 10, of which 1 were waited for; matrix products, arithmetic and copies ran while one was open for 13% of the time, Pallas kernels for 55%

profile of v1, /device:TPU:6, one launch (start us, length us, event | category | flops | bytes accessed | tf_op | source)
XLA Modules:
  0.0 744.9 jit_solution(7089612344841713813)
XLA Ops:
  5.8 155.4 %gather_weights.1 = (bf16[4,1024,1024]{2,1,0:T(8,128)(2,1)S(1)}, bf16[1024,3072]{1,0:T(8,128)(2,1)S(1)}, bf16[1024,1024]{1,0:T(8,128)(2,1)S(1)}, bf16[4096,1024]...) custom-call(bf16[4,64,512]{2,1,0:T(8,128)(2,1)S(1)} %pad_maximum_fusion.2.refs, ...), custom_call_target="tpu_custom_call" | custom-call | tf_op jit(solution)/shard_map/gather_weights/pallas_call | solution.py:403
  163.9 3.3 copy-done.8
  167.2 3.2 copy-done.9
  174.4 5.7 fusion.37
  180.1 5.7 fusion.41
  185.8 5.6 add_convert_fusion
  192.2 8.8 %collective-permute-start = (bf16[176,1024]{1,0:T(8,128)(2,1)}, bf16[176,1024]{1,0:T(8,128)(2,1)}, u32[]{:S(2)}, u32[]{:S(2)}) collective-permute-start(bf16[176,1024]{1,0:T(8,128)(2,1)} %get-tuple-element.111), channel_id=1, source_target_pairs={{0,4},{1,5},{2,6},{3,7},{4,8},{5,9},{6,10},{7,11},{8,12},{9,13},{1... | collective-permute-start | bytes 1081352 | tf_op jit(solution)/shard_map/ppermute | solution.py:33
  201.0 4.0 collective-permute-start.1
  207.4 3.3 fusion.28.q_ref
  210.8 6.6 fusion.7.pl_ref
  225.6 7.9 %convolution_convert_fusion.4.k_ref = bf16[1536,1024]{1,0:T(8,128)(2,1)} fusion(bf16[4,1024,1024]{2,1,0:T(8,128)(2,1)} %copy-done.8, bf16[512,1024]{1,0:T(8,128)(2,1)} %dynamic-slice_bitcast_fusion, bf16[512,1024]{1,0:T(8,128)(2,1)} %collective-permute-done.3, bf16[512,1024]{1,0:T(8,128)(2,1)S(1)} %fusion.54), kind=kOutput, calls=%fused_computation.17 | convolution fusion | flops 3232235520 | bytes 8388608 | tf_op jit(solution)/shard_map/dot_general | solution.py:19
  233.5 6.6 convolution_convert_fusion.3.v_ref
  240.2 28.6 %attend_forward.1 = (bf16[512,1024]{1,0:T(8,128)(2,1)S(1)}, bf16[8,512,1536]{2,1,0:T(8,128)(2,1)}) custom-call(f32[1,1536]{1,0:T(1,128)S(1)} %add_select_fusion.bias_ref, f32[1,1024]{1,0:T(1,128)S(1)} %get-tuple-element.120.cb_ref, f32[1,1024]{1,0:T(1,128)S(1)} %get-tuple-element.119.pb_ref, f32[512,1024]{1,0:T(8,128)S(1)} %fusion.28.q_ref, ...), custom_call_target="tpu_custom_call" | custom-call | flops 4831838208 | bytes 12582912 | tf_op jit(solution)/shard_map/attend_forward/pallas_call | solution.py:144
  272.1 10.9 %fusion.76 = f32[512,4096]{1,0:T(8,128)} fusion(bf16[4096,1024]{1,0:T(8,128)(2,1)} %copy-done.9, f32[512,1024]{1,0:T(8,128)S(1)} %get-tuple-element.136, f32[1024]{0:T(1024)S(1)} %bitcast.223, f32[1024]{0:T(1024)S(1)} %bitcast.212, f32[512]{0:T(512)S(1)} %add_rsqrt_fusion.1, f32[512]{0:T(512)S(1)} %broadcast_multiply_fusion.5), kind=kOutput, calls=%fused_computation.159 | convolution fusion | flops 4297588736 | bytes 18886656 | tf_op jit(solution)/shard_map/dot_general | solution.py:19
  283.0 10.7 %fusion.74 = (f32[512]{0:T(512)S(1)}, f32[512,1024]{1,0:T(8,128)S(1)}) fusion(f32[1024]{0:T(1024)S(1)} %bitcast.226, bf16[4096,1024]{1,0:T(8,128)(2,1)} %copy-done.10, f32[512,4096]{1,0:T(8,128)} %fusion.76, f32[4096]{0:T(1024)S(1)} %bitcast.202, f32[1024]{0:T(1024)S(1)} %bitcast.224, f32[1024]{0:T(1024)S(1)} %bitcast.213, f32[512]{0:T(512)S(1)} %add_rsqrt_fusion.1, ...), kind=kOutput, calls=%fused_computation.157 | convolution fusion | flops 4320656896 | bytes 21006336 | tf_op jit(solution)/shard_map/dot_general | solution.py:19
  299.4 14.7 %convert_reduce_fusion = (f32[4096]{0:T(1024)S(1)}, bf16[512,4096]{1,0:T(8,128)(2,1)}) fusion(f32[512,4096]{1,0:T(8,128)} %fusion.76, f32[4096]{0:T(1024)S(1)} %bitcast.203, bf16[4096,1024]{1,0:T(8,128)(2,1)} %copy-done.10, f32[512,1024]{1,0:T(8,128)} %get-tuple-element.98), kind=kOutput, calls=%fused_computation.9 | convolution fusion | flops 4341624832 | bytes 23101440 | tf_op jit(solution)/shard_map/dot_general | solution.py:19
  314.1 11.1 %multiply_reduce_fusion = (f32[1024]{0:T(1024)}, f32[512]{0:T(512)S(1)}, f32[512]{0:T(512)S(1)}, f32[1024]{0:T(1024)}, f32[512,1024]{1,0:T(8,128)S(1)}) fusion(f32[512,1024]{1,0:T(8,128)S(1)} %get-tuple-element.136, f32[512]{0:T(512)S(1)} %add_rsqrt_fusion.1, f32[512]{0:T(512)S(1)} %broadcast_multiply_fusion.5, f32[1024]{0:T(1024)S(1)} %bitcast.214, ...), kind=kOutput, calls=%fused_computation.50 | convolution fusion | flops 4300207104 | bytes 18894848 | tf_op jit(solution)/shard_map/dot_general | solution.py:19
  327.8 33.7 %attend_backward.1 = (bf16[512,1024]{1,0:T(8,128)(2,1)S(1)}, f32[1,1024]{1,0:T(1,128)S(1)}, f32[1,1024]{1,0:T(1,128)S(1)}, bf16[1536,1024]{1,0:T(8,128)(2,1)}, b...) custom-call(f32[1,1024]{1,0:T(1,128)S(1)} %get-tuple-element.120.cb_ref, f32[1,1024]{1,0:T(1,128)S(1)} %get-tuple-element.119.pb_ref, ...), custom_call_target="tpu_custom_call" | custom-call | flops 9663676416 | bytes 12582912 | tf_op jit(solution)/shard_map/attend_backward/pallas_call | solution.py:170
  364.2 4.0 convolution_convert_fusion.11.q
  368.2 3.5 fusion.23
  371.7 5.7 fusion.75
  379.4 7.7 %convolution_convert_fusion.1.up = bf16[4096,1024]{1,0:T(8,128)(2,1)} fusion(bf16[512,4096]{1,0:T(8,128)(2,1)S(1)} %copy-done.68, f32[512,1024]{1,0:T(8,128)S(1)} %copy-done.19, f32[1024]{0:T(1024)S(1)} %bitcast.225, f32[1024]{0:T(1024)S(1)} %bitcast.216, f32[512]{0:T(512)S(1)} %add_rsqrt_fusion.1, f32[512]{0:T(512)S(1)} %broadcast_multiply_fusion.5), kind=kOutput, calls=%fused_computation.12 | convolution fusion | flops 4301783040 | bytes 14692352 | tf_op jit(solution)/shard_map/dot_general | solution.py:19
  387.1 13.4 %convolution_convert_fusion.down = bf16[4096,1024]{1,0:T(8,128)(2,1)} fusion(f32[512,1024]{1,0:T(8,128)S(1)} %copy-done.29, f32[512,4096]{1,0:T(8,128)} %fusion.76, f32[4096]{0:T(1024)S(1)} %bitcast.204), kind=kOutput, calls=%fused_computation.11 | convolution fusion | flops 4320657408 | bytes 18890752 | tf_op jit(solution)/shard_map/dot_general | solution.py:19
  408.0 3.9 collective-permute-start.8
  413.9 4.9 convert_bitcast_fusion.1.p
  418.9 6.5 convolution_convert_fusion.10.k
  425.3 6.2 convolution_convert_fusion.9.v
  432.2 138.5 %scatter_dense.1 = (f32[128,1024]{1,0:T(8,128)S(1)}, f32[128,1024]{1,0:T(8,128)S(1)}, f32[32,1024]{1,0:T(8,128)S(1)}) custom-call(bf16[4096,1024]{1,0:T(8,128)(2,1)} %convolution_convert_fusion.1.up, bf16[4096,1024]{1,0:T(8,128)(2,1)} %convolution_convert_fusion.down, bf16[1024,1024]{1,0:T(8,128)(2,1)S(1)} %convolution_convert_fusion.5.o), custom_call_target="tpu_custom_call" | custom-call | tf_op jit(solution)/shard_map/scatter_dense/pallas_call | solution.py:721
  596.2 3.3 pad_maximum_fusion.sq
  600.6 117.9 %scatter_attention.1 = (f32[64,512]{1,0:T(8,128)S(1)}, f32[64,512]{1,0:T(8,128)S(1)}, f32[64,512]{1,0:T(8,128)S(1)}, f32[64,512]{1,0:T(8,128)S(1)}, f32[32,3072]...) custom-call(bf16[1024,1024]{1,0:T(8,128)(2,1)S(1)} %copy-done.3, bf16[1024,1024]{1,0:T(8,128)(2,1)S(1)} %copy-done.4, ...), custom_call_target="tpu_custom_call" | custom-call | tf_op jit(solution)/shard_map/scatter_attention/pallas_call | solution.py:745
  722.4 3.8 fusion.19
  729.9 8.1 %collective-permute-done.9 = bf16[256,1024]{1,0:T(8,128)(2,1)S(1)} collective-permute-done((bf16[256,1024]{1,0:T(8,128)(2,1)S(1)}, bf16[256,1024]{1,0:T(8,128)(2,1)S(1)}, u32[]{:S(2)}, u32[]{:S(2)}) %collective-permute-start.9) | collective-permute-done | bytes 524320 | tf_op jit(solution)/shard_map/ppermute | solution.py:797
  (240 shorter events, 89.5 us)
Async XLA Ops:
  0.9 172.2 %copy-start.57 = (s32[2,16]{1,0:T(2,128)S(1)}, s32[2,16]{1,0:T(2,128)}, u32[]{:S(2)}) copy-start(s32[2,16]{1,0:T(2,128)} %param.34) | copy-start | bytes 388
  3.3 222.3 %collective-permute-start.3 = (bf16[512,1024]{1,0:T(8,128)(2,1)}, bf16[512,1024]{1,0:T(8,128)(2,1)}, u32[]{:S(2)}, u32[]{:S(2)}) collective-permute-start(bf16[512,1024]{1,0:T(8,128)(2,1)} %dynamic-slice_bitcast_fusion), channel_id=1, source_target_pairs={{0,1},{1,2},{2,3},{3,4},{4,5},{5,6},{6,7},{7,8},{8,9},{9,10},{10,1... | collective-permute-start | bytes 3145736 | tf_op jit(solution)/shard_map/ppermute | solution.py:33
  167.2 12.9 %copy-start.11 = (bf16[1024,1024]{1,0:T(8,128)(2,1)}, bf16[1024,1024]{1,0:T(8,128)(2,1)S(1)}, u32[]{:S(2)}) copy-start(bf16[1024,1024]{1,0:T(8,128)(2,1)S(1)} %get-tuple-element.49) | copy-start | bytes 6291460
  174.4 33.0 %copy-start.42 = (pred[512]{0:T(512)(128)(4,1)}, pred[512]{0:T(512)(128)(4,1)S(1)}, u32[]{:S(2)}) copy-start(pred[512]{0:T(512)(128)(4,1)S(1)} %iota_compare_fusion) | copy-start | bytes 1540
  192.2 29.8 %collective-permute-start = (bf16[176,1024]{1,0:T(8,128)(2,1)}, bf16[176,1024]{1,0:T(8,128)(2,1)}, u32[]{:S(2)}, u32[]{:S(2)}) collective-permute-start(bf16[176,1024]{1,0:T(8,128)(2,1)} %get-tuple-element.111), channel_id=1, source_target_pairs={{0,4},{1,5},{2,6},{3,7},{4,8},{5,9},{6,10},{7,11},{8,12},{9,13},{1... | collective-permute-start | bytes 1081352 | tf_op jit(solution)/shard_map/ppermute | solution.py:33
  201.0 22.6 %collective-permute-start.1 = (bf16[176,1024]{1,0:T(8,128)(2,1)S(1)}, bf16[176,1024]{1,0:T(8,128)(2,1)}, u32[]{:S(2)}, u32[]{:S(2)}) collective-permute-start(bf16[176,1024]{1,0:T(8,128)(2,1)S(1)} %get-tuple-element.109), channel_id=1, source_target_pairs={{0,3},{1,4},{2,5},{3,6},{4,7},{5,8},{6,9},{7,10},{8,11},{9,12},{10... | collective-permute-start | bytes 1081352 | tf_op jit(solution)/shard_map/ppermute | solution.py:33
  205.1 20.1 %collective-permute-start.2 = (bf16[176,1024]{1,0:T(8,128)(2,1)S(1)}, bf16[176,1024]{1,0:T(8,128)(2,1)S(1)}, u32[]{:S(2)}, u32[]{:S(2)}) collective-permute-start(bf16[176,1024]{1,0:T(8,128)(2,1)S(1)} %get-tuple-element.110), channel_id=1, source_target_pairs={{0,2},{1,3},{2,4},{3,5},{4,6},{5,7},{6,8},{7,9},{8,10},{9,11},{10,... | collective-permute-start | bytes 1081352 | tf_op jit(solution)/shard_map/ppermute | solution.py:33
  210.8 6.6 copy-start.44
  210.8 6.6 copy-start.48
  210.8 6.6 copy-start.49
  225.1 8.4 %slice-start.2 = ((s8[8388608]{0:T(1024)(128)(4,1)}), s8[4194304]{0:T(1024)(128)(4,1)S(1)}, s32[]{:S(2)}) async-start(s8[8388608]{0:T(1024)(128)(4,1)} %bitcast.200), calls=%async_computation.2 | async-start | bytes 8388608
  225.6 7.9 %copy-start.30 = (bf16[512,1024]{1,0:T(8,128)(2,1)}, bf16[512,1024]{1,0:T(8,128)(2,1)S(1)}, u32[]{:S(2)}) copy-start(bf16[512,1024]{1,0:T(8,128)(2,1)S(1)} %fusion.54) | copy-start | bytes 3145732
  225.6 7.9 %slice-start.3 = ((s8[8388608]{0:T(1024)(128)(4,1)}), s8[4194304]{0:T(1024)(128)(4,1)S(1)}, s32[]{:S(2)}) async-start(s8[8388608]{0:T(1024)(128)(4,1)} %bitcast.200), calls=%async_computation.3 | async-start | bytes 8388608
  240.2 28.6 %copy-start.12 = (bf16[1024,1024]{1,0:T(8,128)(2,1)S(1)}, bf16[1024,1024]{1,0:T(8,128)(2,1)}, u32[]{:S(2)}) copy-start(bf16[1024,1024]{1,0:T(8,128)(2,1)} %copy-done.11) | copy-start | bytes 6291460
  271.8 53.4 %copy-start.18 = (f32[512,1024]{1,0:T(8,128)}, f32[512,1024]{1,0:T(8,128)S(1)}, u32[]{:S(2)}) copy-start(f32[512,1024]{1,0:T(8,128)S(1)} %get-tuple-element.136) | copy-start | bytes 6291460
  371.7 7.5 %copy-start.68 = (bf16[512,4096]{1,0:T(8,128)(2,1)S(1)}, bf16[512,4096]{1,0:T(8,128)(2,1)}, u32[]{:S(2)}) copy-start(bf16[512,4096]{1,0:T(8,128)(2,1)} %get-tuple-element.143) | copy-start | bytes 12582916
  379.4 7.7 %copy-start.29 = (f32[512,1024]{1,0:T(8,128)S(1)}, f32[512,1024]{1,0:T(8,128)}, u32[]{:S(2)}) copy-start(f32[512,1024]{1,0:T(8,128)} %get-tuple-element.98) | copy-start | bytes 6291460
  387.1 13.4 %copy-start.14 = (bf16[512,1024]{1,0:T(8,128)(2,1)S(1)}, bf16[512,1024]{1,0:T(8,128)(2,1)}, u32[]{:S(2)}) copy-start(bf16[512,1024]{1,0:T(8,128)(2,1)} %copy-done.13) | copy-start | bytes 3145732
  387.1 13.4 %copy-start.16 = (f32[512,1024]{1,0:T(8,128)S(1)}, f32[512,1024]{1,0:T(8,128)}, u32[]{:S(2)}) copy-start(f32[512,1024]{1,0:T(8,128)} %copy-done.15) | copy-start | bytes 6291460
  401.8 12.1 %copy-start.67 = (bf16[1536,1024]{1,0:T(8,128)(2,1)S(1)}, bf16[1536,1024]{1,0:T(8,128)(2,1)}, u32[]{:S(2)}) copy-start(bf16[1536,1024]{1,0:T(8,128)(2,1)} %get-tuple-element.57) | copy-start | bytes 9437188
  402.6 11.3 %copy-start.59 = (bf16[1536,1024]{1,0:T(8,128)(2,1)S(1)}, bf16[1536,1024]{1,0:T(8,128)(2,1)}, u32[]{:S(2)}) copy-start(bf16[1536,1024]{1,0:T(8,128)(2,1)} %constant.93.clone) | copy-start | bytes 9437188
  402.6 324.9 %collective-permute-start.4 = (bf16[256,1024]{1,0:T(8,128)(2,1)}, bf16[256,1024]{1,0:T(8,128)(2,1)}, u32[]{:S(2)}, u32[]{:S(2)}) collective-permute-start(bf16[256,1024]{1,0:T(8,128)(2,1)} %constant_dynamic-slice_fusion.1), channel_id=1, source_target_pairs={{0,16},{16,0},{1,17},{17,1},{2,18},{18,2},{3,19},{19,3},{4,20},{20... | collective-permute-start | bytes 1572872 | tf_op jit(solution)/shard_map/ppermute | solution.py:797
  405.4 167.9 %collective-permute-start.6 = (bf16[176,1024]{1,0:T(8,128)(2,1)}, bf16[176,1024]{1,0:T(8,128)(2,1)}, u32[]{:S(2)}, u32[]{:S(2)}) collective-permute-start(bf16[176,1024]{1,0:T(8,128)(2,1)} %get-tuple-element.108), channel_id=1, source_target_pairs={{4,0},{5,1},{6,2},{7,3},{8,4},{9,5},{10,6},{11,7},{12,8},{13,9},{1... | collective-permute-start | bytes 1081352 | tf_op jit(solution)/shard_map/ppermute | solution.py:33
  406.7 168.2 %collective-permute-start.7 = (bf16[176,1024]{1,0:T(8,128)(2,1)}, bf16[176,1024]{1,0:T(8,128)(2,1)}, u32[]{:S(2)}, u32[]{:S(2)}) collective-permute-start(bf16[176,1024]{1,0:T(8,128)(2,1)} %get-tuple-element.106), channel_id=1, source_target_pairs={{3,0},{4,1},{5,2},{6,3},{7,4},{8,5},{9,6},{10,7},{11,8},{12,9},{13... | collective-permute-start | bytes 1081352 | tf_op jit(solution)/shard_map/ppermute | solution.py:33
  408.0 168.4 %collective-permute-start.8 = (bf16[176,1024]{1,0:T(8,128)(2,1)}, bf16[176,1024]{1,0:T(8,128)(2,1)}, u32[]{:S(2)}, u32[]{:S(2)}) collective-permute-start(bf16[176,1024]{1,0:T(8,128)(2,1)} %get-tuple-element.107), channel_id=1, source_target_pairs={{2,0},{3,1},{4,2},{5,3},{6,4},{7,5},{8,6},{9,7},{10,8},{11,9},{12,... | collective-permute-start | bytes 1081352 | tf_op jit(solution)/shard_map/ppermute | solution.py:33
  412.0 309.2 %collective-permute-start.5 = (bf16[512,1024]{1,0:T(8,128)(2,1)}, bf16[512,1024]{1,0:T(8,128)(2,1)}, u32[]{:S(2)}, u32[]{:S(2)}) collective-permute-start(bf16[512,1024]{1,0:T(8,128)(2,1)} %slice.162), channel_id=1, source_target_pairs={{1,0},{2,1},{3,2},{4,3},{5,4},{6,5},{7,6},{8,7},{9,8},{10,9},{11,1... | collective-permute-start | bytes 3145736 | tf_op jit(solution)/shard_map/ppermute | solution.py:33
  418.9 6.5 copy-start.64
  432.2 139.5 %copy-start.41 = (f32[1024]{0:T(1024)S(1)}, f32[1024]{0:T(1024)}, u32[]{:S(2)}) copy-start(f32[1024]{0:T(1024)} %convert_reduce_fusion.1) | copy-start | bytes 12292
  596.2 122.3 %slice-start = ((s8[6291456]{0:T(1024)(128)(4,1)}), s8[4194304]{0:T(1024)(128)(4,1)S(1)}, s32[]{:S(2)}) async-start(s8[6291456]{0:T(1024)(128)(4,1)} %bitcast.194), calls=%async_computation | async-start | bytes 8388608
  600.6 117.9 %slice-start.1 = ((s8[6291456]{0:T(1024)(128)(4,1)}), s8[2097152]{0:T(1024)(128)(4,1)S(1)}, s32[]{:S(2)}) async-start(s8[6291456]{0:T(1024)(128)(4,1)} %bitcast.194), calls=%async_computation.1 | async-start | bytes 4194304
  726.2 11.8 %collective-permute-start.9 = (bf16[256,1024]{1,0:T(8,128)(2,1)S(1)}, bf16[256,1024]{1,0:T(8,128)(2,1)S(1)}, u32[]{:S(2)}, u32[]{:S(2)}) collective-permute-start(bf16[256,1024]{1,0:T(8,128)(2,1)S(1)} %constant_dynamic-slice_fusion), channel_id=1, source_target_pairs={{0,16},{16,0},{1,17},{17,1},{2,18},{18,2},{3,19},{19,3},{4,20},{20... | collective-permute-start | bytes 1572872 | tf_op jit(solution)/shard_map/ppermute | solution.py:797
  738.2 6.4 copy-start.1
  (51 other events, 186.7 us)

commit v2 on v1

--- a/solution.py
+++ b/solution.py
@@ -197,10 +197,18 @@
 CORE, XFLIP, YFLIP, UP, DOWN = range(5)
 
 
+def repeat(count, run):
+    def body(i, carry):
+        run(i)
+        return carry
+
+    lax.fori_loop(0, count, body, 0)
+
+
 class Place:
     def __init__(self, count):
         self.count = count
-        self.line_size = count // 4
+        self.n = count // 4
         self.h = lax.axis_index("head")
         self.s = lax.axis_index("seq")
         self.a = self.s // 4
@@ -222,7 +230,7 @@
 
     def when(self, kind):
         if kind == UP:
-            return pl.when(self.a < self.line_size - 1)
+            return pl.when(self.a < self.n - 1)
         if kind == DOWN:
             return pl.when(self.a > 0)
         return lambda run: run()
@@ -233,67 +241,66 @@
             @self.when(kind)
             def _(kind=kind):
                 pl.semaphore_signal(barrier, inc=1, device_id=self.neighbour(kind), device_id_type=MESH)
-        ends = jnp.where(self.a == 0, 1, 0) + jnp.where(self.a == self.line_size - 1, 1, 0)
+        ends = jnp.where(self.a == 0, 1, 0) + jnp.where(self.a == self.n - 1, 1, 0)
         pl.semaphore_wait(barrier, 5 - ends)
 
+    def along(self, i):
+        return (self.a + self.n // 2 + i) % self.n
+
 
 class Gather:
-    def __init__(self, place, shards, fulls, views, orders, local_sem, send_sem, recv_sem):
-        self.place, self.shards, self.fulls, self.views, self.orders = place, shards, fulls, views, orders
+    def __init__(self, place, units, local_sem, send_sem, recv_sem):
+        self.place, self.units = place, units
         self.local_sem, self.send_sem, self.recv_sem = local_sem, send_sem, recv_sem
 
     def view(self, u, h, s):
-        return self.views[u](self.fulls[u], h, s)
+        shard, full, view, order = self.units[u]
+        return view(full, h, s)
 
     def copy(self, u, kind, h, s, own=False):
-        slot = h * self.place.count + s
-        line, plane = s // 4, slot // 2
-        size = self.place.line_size
-        sent = {UP: line, DOWN: size + line, XFLIP: 2 * size + plane, YFLIP: 6 * size + plane, CORE: 10 * size + plane}
+        n = self.place.n
+        a, b = s // 4, (s // 2) % 2
+        order = self.units[u][3]
+        other = b if order.index("x") < order.index("z") else h
+        sent = {
+            UP: other * n + a,
+            DOWN: (2 + other) * n + a,
+            XFLIP: (4 + h) * n + a,
+            YFLIP: (6 + b) * n + a,
+            CORE: (8 + h * 2 + b) * n + a,
+        }[kind]
         there = self.view(u, h, s)
         return pltpu.make_async_remote_copy(
-            src_ref=self.shards[u] if own else there,
+            src_ref=self.units[u][0] if own else there,
             dst_ref=there,
-            send_sem=self.send_sem.at[u, sent[kind]],
-            recv_sem=self.recv_sem.at[u, slot],
+            send_sem=self.send_sem.at[u, sent],
+            recv_sem=self.recv_sem.at[u, h * self.place.count + s],
             device_id=self.place.neighbour(kind),
             device_id_type=MESH,
         )
 
     def local(self, u):
-        return pltpu.make_async_copy(self.shards[u], self.view(u, self.place.h, self.place.s), self.local_sem.at[u])
+        return pltpu.make_async_copy(self.units[u][0], self.view(u, self.place.h, self.place.s), self.local_sem.at[u])
 
     def sources(self):
-        p = self.place
         found = []
-        for t in range(p.line_size):
+        for t in range(self.place.n):
             for sign in ((1, -1) if t else (0,)):
-                o = p.a - sign * t
-                valid = None if not t else (o >= 0 if sign > 0 else o <= p.line_size - 1)
-                for one in (0, 1):
-                    for two in (0, 1):
-                        if t or one or two:
-                            found.append((t + one + two, o, sign, one, two, valid))
-        return sorted(found, key=lambda e: e[0])
-
-    def slot_of(self, u, o, one, two):
-        p = self.place
-        x, y = (one, two) if self.orders[u] == 0 else (two, one)
-        h = 1 - p.h if y else p.h
-        b = 1 - p.b if x else p.b
-        return h, p.seq_of(o, b, p.c)
-
-    def flips(self, u):
-        return (XFLIP, YFLIP) if self.orders[u] == 0 else (YFLIP, XFLIP)
-
-    def onward(self, u, sign, one, two):
-        first, second = self.flips(u)
+                for x in (0, 1):
+                    for y in (0, 1):
+                        if t or x or y:
+                            found.append((t, sign, x, y))
+        return sorted(found, key=lambda e: e[0] + e[2] + e[3])
+
+    def onward(self, u, sign, x, y):
+        order = self.units[u][3]
+        moved = {"x": x, "y": y, "z": sign}
+        last = max([i for i in range(3) if moved[order[i]]], default=-1)
         kinds = []
-        if not one and not two:
-            kinds += [UP] if sign > 0 else [DOWN] if sign < 0 else [UP, DOWN]
-            kinds += [first]
-        if not two:
-            kinds += [second]
+        if last >= 0 and order[last] == "z":
+            kinds.append(UP if sign > 0 else DOWN)
+        for dim in order[last + 1 :]:
+            kinds += {"x": [XFLIP], "y": [YFLIP], "z": [UP, DOWN]}[dim]
         return kinds + [CORE]
 
     def send(self, u, kind, h, s, own, wait):
@@ -305,66 +312,94 @@
             else:
                 copy.start()
 
+    def begin(self, wait=False):
+        p = self.place
+        for u in range(len(self.units)):
+            for kind in self.onward(u, 0, 0, 0):
+                self.send(u, kind, p.h, p.s, True, wait)
+        for u in range(len(self.units)):
+            if wait:
+                self.local(u).wait()
+            else:
+                self.local(u).start()
+
+    def pass_on(self, entry, wait=False):
+        p = self.place
+        t, sign, x, y = entry
+        a = p.a - sign * t
+        h = 1 - p.h if y else p.h
+        s = p.seq_of(a, 1 - p.b if x else p.b, p.c)
+
+        def run():
+            for u in range(len(self.units)):
+                if not wait:
+                    self.copy(u, CORE, h, s).wait_recv()
+                for kind in self.onward(u, sign, x, y):
+                    self.send(u, kind, h, s, False, wait)
+
+        if t:
+            pl.when(jnp.logical_and(a >= 0, a <= p.n - 1))(run)
+        else:
+            run()
+
+    def finish(self):
+        p = self.place
+
+        def core(i):
+            h, a, b = i // (2 * p.n), i // 2 % p.n, i % 2
+            for u in range(len(self.units)):
+                self.copy(u, CORE, h, p.seq_of(a, b, 1 - p.c)).wait_recv()
+
+        repeat(4 * p.n, core)
+        self.begin(True)
+        for entry in self.sources():
+            self.pass_on(entry, True)
+
     def steps(self):
-        p = self.place
-        units = range(len(self.shards))
-
-        def begin(wait=False):
-            for u in units:
-                if wait:
-                    self.local(u).wait()
-                else:
-                    self.local(u).start()
-                for kind in self.onward(u, 0, 0, 0):
-                    self.send(u, kind, p.h, p.s, True, wait)
-
-        def pass_on(entry, wait):
-            depth, o, sign, one, two, valid = entry
-
-            def run():
-                for u in units:
-                    h, s = self.slot_of(u, o, one, two)
-                    if not wait:
-                        self.copy(u, CORE, h, s).wait_recv()
-                    for kind in self.onward(u, sign, one, two):
-                        self.send(u, kind, h, s, False, wait)
-
-            if valid is None:
-                run()
-            else:
-                pl.when(valid)(run)
-
-        def finish():
-            for h in (0, 1):
-                for a in range(p.line_size):
-                    for b in (0, 1):
-                        for u in units:
-                            self.copy(u, CORE, h, p.seq_of(a, b, 1 - p.c)).wait_recv()
-            begin(True)
-            for entry in self.sources():
-                pass_on(entry, True)
-
-        return [begin] + [functools.partial(pass_on, entry, False) for entry in self.sources()] + [finish]
-
-
-def gather_kernel(count, small_names, *refs):
-    (qkvp, sq, o, up, down, small), refs = refs[:6], refs[6:]
-    (qkvp_f, sq_f, o_f, up_f, down_f, vec, vec_up), refs = refs[:7], refs[7:]
-    small_f, local_sem, send_sem, recv_sem = refs
+        return [self.begin] + [functools.partial(self.pass_on, entry) for entry in self.sources()] + [self.finish]
+
+
+GATHER_ORDERS = ("yzx", "xzy", "zxy", "zyx")
+
+
+def halves(rows):
+    return [(0, rows // 2), (rows // 2, rows // 2)] if rows % 32 == 0 else [(0, rows)]
+
+
+def block_units(shard, full, count, first):
+    rows = shard.shape[0]
+    units = []
+    for i, (at, size) in enumerate(halves(rows)):
+        def view(ref, h, s, at=at, size=size):
+            return ref.at[pl.ds(pl.multiple_of((h * count + s) * rows + at, size), size)]
+
+        units.append((shard.at[pl.ds(at, size)], full, view, GATHER_ORDERS[(first + i) % 4]))
+    return units
+
+
+def square_unit(shard, full, order):
+    r, w = shard.shape
+
+    def view(ref, h, s):
+        return ref.at[pl.ds(pl.multiple_of(s * r, r), r), pl.ds(pl.multiple_of(h * w, w), w)]
+
+    return (shard, full, view, order)
+
+
+def gather_attention_kernel(count, small_names, *refs):
+    shards, (vec, vec_up) = refs[:6], refs[11:13]
+    fulls = refs[6:11] + refs[13:14]
     place = Place(count)
     place.barrier()
-    r, w = qkvp.shape[1:]
-
-    def qkvp_view(ref, h, s):
-        return ref.at[:, pl.ds(pl.multiple_of(s * r, r), r), pl.ds(pl.multiple_of(h * w, w), w)]
-
-    def block_view(rows):
-        return lambda ref, h, s: ref.at[pl.ds(pl.multiple_of((h * count + s) * rows, rows), rows)]
-
-    shards = [qkvp, sq, up, down, o, small]
-    fulls = [qkvp_f, sq_f, up_f, down_f, o_f, small_f]
-    views = [qkvp_view] + [block_view(s.shape[0]) for s in shards[1:]]
-    gather = Gather(place, shards, fulls, views, (0, 1, 0, 1, 1, 0), local_sem, send_sem, recv_sem)
+    units = [square_unit(shards[i], fulls[i], GATHER_ORDERS[i]) for i in range(4)]
+    units += block_units(shards[4], fulls[4], count, 0)
+    small, small_f = shards[5], fulls[5]
+
+    def small_view(ref, h, s):
+        return ref.at[pl.ds(pl.multiple_of((h * count + s) * 8, 8), 8)]
+
+    units.append((small, small_f, small_view, "zxy"))
+    gather = Gather(place, units, *refs[14:])
     for step in gather.steps():
         step()
     for slot in range(2 * count):
@@ -375,6 +410,25 @@
             ref[target : target + 1, slot * size : (slot + 1) * size] = small_f[slot * 8 + row : slot * 8 + row + 1, at : at + size]
 
 
+def gather_dense_kernel(count, *refs):
+    place = Place(count)
+    place.barrier()
+    units = []
+    for i in range(3):
+        units += block_units(refs[i], refs[3 + i], count, (0, 2, 1)[i])
+    gather = Gather(place, units, *refs[6:])
+    for step in gather.steps():
+        step()
+
+
+def gather_semaphores(count, units):
+    return [
+        pltpu.SemaphoreType.DMA((units,)),
+        pltpu.SemaphoreType.DMA((units, 12 * (count // 4))),
+        pltpu.SemaphoreType.DMA((units, 2 * count)),
+    ]
+
+
 def small_layout(both, seq):
     names = []
     for i, name in enumerate(("cb", "pb", "sb")):
@@ -385,7 +439,7 @@
     return names
 
 
-def gather_all(w):
+def gather_attention(w):
     count = lax.axis_size("seq")
     both, seq = w["cb"].shape[0], w["ob"].shape[0]
     width = both * 2 * count
@@ -395,50 +449,63 @@
         lines[row].append(w[name].astype(F32))
     lines = [jnp.concatenate(parts) if parts else jnp.zeros((128,), F32) for parts in lines]
     small = jnp.stack([jnp.pad(line, (0, 128 - line.shape[0])) for line in lines])
-    qkvp = jnp.stack([w["q"], w["k"], w["v"], w["p"]])
-    shards = [qkvp, w["sq"], w["o"], w["up"], w["down"], small]
+    names = ("q", "k", "v", "p", "sq")
     any_spec = pl.BlockSpec(memory_space=pl.ANY)
     vmem_spec = pl.BlockSpec(memory_space=pltpu.VMEM)
-    units = len(shards)
     outs = pl.pallas_call(
-        functools.partial(gather_kernel, count, layout),
+        functools.partial(gather_attention_kernel, count, layout),
         in_specs=[any_spec] * 6,
         out_specs=[any_spec] * 5 + [vmem_spec] * 2,
         out_shape=[
-            jax.ShapeDtypeStruct((4, qkvp.shape[1] * count, qkvp.shape[2] * 2), BF),
-            *[jax.ShapeDtypeStruct((s.shape[0] * 2 * count, s.shape[1]), BF) for s in shards[1:5]],
+            *[jax.ShapeDtypeStruct((width, width), BF) for _ in range(4)],
+            jax.ShapeDtypeStruct((width, w["sq"].shape[1]), BF),
             jax.ShapeDtypeStruct((16, width), F32),
             jax.ShapeDtypeStruct((1, 4 * width), F32),
         ],
         scratch_shapes=[
             pltpu.VMEM((8 * 2 * count, 128), F32),
-            pltpu.SemaphoreType.DMA((units,)),
-            pltpu.SemaphoreType.DMA((units, 14 * (count // 4))),
-            pltpu.SemaphoreType.DMA((units, 2 * count)),
+            *gather_semaphores(count, 5 + len(halves(w["sq"].shape[0]))),
         ],
         compiler_params=pltpu.CompilerParams(collective_id=0, has_side_effects=True, vmem_limit_bytes=16 * MIB),
-        name="gather_weights",
-    )(*shards)
-    full = dict(zip(("q", "k", "v", "p"), outs[0]))
-    full.update(zip(("sq", "o", "up", "down"), outs[1:5]))
+        name="gather_attention",
+    )(*[w[n] for n in names], small)
+    full = dict(zip(names, outs))
     for name, row, at, size, target in layout:
         full[name] = outs[6] if name == "ub" else outs[5][target : target + 1]
     return full
 
 
+def gather_dense(w):
+    count = lax.axis_size("seq")
+    names = ("up", "down", "o")
+    any_spec = pl.BlockSpec(memory_space=pl.ANY)
+    outs = pl.pallas_call(
+        functools.partial(gather_dense_kernel, count),
+        in_specs=[any_spec] * 3,
+        out_specs=[any_spec] * 3,
+        out_shape=[jax.ShapeDtypeStruct((w[n].shape[0] * 2 * count, w[n].shape[1]), BF) for n in names],
+        scratch_shapes=gather_semaphores(count, sum(len(halves(w[n].shape[0])) for n in names)),
+        compiler_params=pltpu.CompilerParams(collective_id=3, has_side_effects=True, vmem_limit_bytes=16 * MIB),
+        name="gather_dense",
+    )(*[w[n] for n in names])
+    return dict(zip(names, outs))
+
+
 class Scatter:
     def __init__(self, place, view, order, mine, core, first, second, line, local_sem, send_sem, recv_sem):
-        self.place, self.view, self.order = place, view, order
+        self.place, self.view = place, view
+        self.by_y = order[0] == "y"
+        self.late = order[2] == "z"
         self.mine, self.core, self.first, self.second, self.line = mine, core, first, second, line
         self.local_sem, self.send_sem, self.recv_sem = local_sem, send_sem, recv_sem
-        self.f, self.g = (place.h, place.b) if order == 0 else (place.b, place.h)
-        self.flips = (YFLIP, XFLIP) if order == 0 else (XFLIP, YFLIP)
+        self.f, self.g = (place.h, place.b) if self.by_y else (place.b, place.h)
+        self.flips = (YFLIP, XFLIP) if self.by_y else (XFLIP, YFLIP)
 
     def index(self, f, g, a):
-        return (f * 2 + g) * self.place.line_size + a
+        return (f * 2 + g) * self.place.n + a
 
     def slot(self, f, g, a, c):
-        h, b = (f, g) if self.order == 0 else (g, f)
+        h, b = (f, g) if self.by_y else (g, f)
         return h, self.place.seq_of(a, b, c)
 
     def remote(self, source, target, kind, send_at, recv_at):
@@ -451,24 +518,31 @@
             device_id_type=MESH,
         )
 
-    def core_copy(self, f, g, a):
-        i = self.index(f, g, a)
+    def core_copy(self, i):
         return self.remote(self.core.at[i], self.core.at[i], CORE, i, i)
 
     def first_copy(self, g, a):
-        n = self.place.line_size
+        n = self.place.n
         to = g * n + a
         return self.remote(self.mine.at[self.index(1 - self.f, g, a)], self.first.at[to], self.flips[0], 4 * n + to, 4 * n + to)
 
     def second_copy(self, a):
-        n = self.place.line_size
-        return self.remote(self.mine.at[self.index(self.f, 1 - self.g, a)], self.second.at[a], self.flips[1], 6 * n + a, 6 * n + a)
-
-    def line_copy(self, kind, a):
-        n = self.place.line_size
-        way = 0 if kind == UP else 1
-        at = (7 + way) * n + a
-        return self.remote(self.mine.at[self.index(self.f, self.g, a)], self.line.at[way * n + a], kind, at, at)
+        n = self.place.n
+        to = a if self.late else 0
+        return self.remote(self.mine.at[self.index(self.f, 1 - self.g, a)], self.second.at[to], self.flips[1], 6 * n + to, 6 * n + to)
+
+    def line_at(self, g, at):
+        return at if self.late else g * (self.place.n + 1) + at
+
+    def line_copy(self, kind, g, a):
+        n = self.place.n
+        to = self.line_at(g, a if kind == UP else jnp.where(a == self.place.a - 1, n, a))
+        sent = 7 * n + (a if self.late else g * n + a)
+        return self.remote(self.mine.at[self.index(self.f, g, a)], self.line.at[to], kind, sent, 7 * n + to)
+
+    def line_wait(self, at):
+        n = self.place.n
+        self.remote(self.line.at[at], self.line.at[at], CORE, 7 * n, 7 * n + at).wait_recv()
 
     def start(self, f, g, a):
         p = self.place
@@ -478,164 +552,218 @@
         for source, target in self.view(*self.slot(f, g, a, p.c), self.mine.at[i]):
             pltpu.make_async_copy(source, target, self.local_sem.at[i]).start()
 
-    def arrive(self, f, g, a):
+    def gather(self, f, g, a, more=()):
         i = self.index(f, g, a)
         pltpu.make_async_copy(self.mine.at[i], self.mine.at[i], self.local_sem.at[i]).wait()
-        self.core_copy(f, g, a).wait_recv()
-
-    def add(self, i, *refs):
+        self.core_copy(i).wait_recv()
+        return i, [(self.core, i), *more]
+
+    def after_first(self, g, a):
+        self.first_copy(g, a).wait_recv()
+        return self.gather(self.f, g, a, [(self.first, g * self.place.n + a)])
+
+    def add(self, i, refs):
         total = self.mine[i].astype(F32)
         for ref, at in refs:
             total = total + ref[at].astype(F32)
         self.mine[i] = total.astype(self.mine.dtype)
 
-    def loop(self, count, run):
-        def body(i, carry):
-            run(i)
-            return carry
-
-        lax.fori_loop(0, count, body, 0)
-
-    def begin(self):
-        n = self.place.line_size
-        self.loop(2 * n, lambda i: self.start(1 - self.f, i // n, i % n))
-        self.loop(n, lambda i: self.start(self.f, 1 - self.g, i))
-        self.loop(n, lambda i: self.start(self.f, self.g, i))
-
-    def flip_first(self):
-        n = self.place.line_size
-
-        def run(i):
-            g, a = i // n, i % n
-            self.arrive(1 - self.f, g, a)
-            at = self.index(1 - self.f, g, a)
-            self.add(at, (self.core, at))
-            self.first_copy(g, a).start()
-
-        self.loop(2 * n, run)
-
-    def flip_second(self):
-        n = self.place.line_size
-
-        def run(a):
-            self.arrive(self.f, 1 - self.g, a)
-            self.first_copy(1 - self.g, a).wait_recv()
-            at = self.index(self.f, 1 - self.g, a)
-            self.add(at, (self.core, at), (self.first, (1 - self.g) * n + a))
-            self.second_copy(a).start()
-
-        self.loop(n, run)
-
-    def settle(self, a):
-        n = self.place.line_size
-        self.arrive(self.f, self.g, a)
-        self.first_copy(self.g, a).wait_recv()
-        self.second_copy(a).wait_recv()
-        at = self.index(self.f, self.g, a)
-        return at, [(self.core, at), (self.first, self.g * n + a), (self.second, a)]
-
-    def along(self):
+    def add_line(self, i, g):
         p = self.place
-        n = p.line_size
-        for d in range(n - 1, 0, -1):
-            for kind, way, a, inside, fed in (
-                (UP, 0, p.a + d, p.a + d <= n - 1, p.a > 0),
-                (DOWN, 1, p.a - d, p.a - d >= 0, p.a < n - 1),
-            ):
-                @pl.when(inside)
-                def _(kind=kind, way=way, a=a, fed=fed):
-                    at, refs = self.settle(a)
-
-                    @pl.when(fed)
-                    def _():
-                        self.line_copy(kind, a).wait_recv()
-                        self.add(at, *refs, (self.line, way * n + a))
-
-                    @pl.when(jnp.logical_not(fed))
-                    def _():
-                        self.add(at, *refs)
-
-                    self.line_copy(kind, a).start()
+        for fed, at in ((p.a > 0, p.a), (p.a < p.n - 1, p.n)):
+            @pl.when(fed)
+            def _(at=self.line_at(g, at)):
+                self.line_wait(at)
+                self.add(i, [(self.line, at)])
+
+    def flip_first(self, g, a):
+        self.add(*self.gather(1 - self.f, g, a))
+        self.first_copy(g, a).start()
+
+    def flip_second(self, a):
+        i, refs = self.after_first(1 - self.g, a)
+        self.add(i, refs)
+        if not self.late:
+            self.add_line(i, 1 - self.g)
+        self.second_copy(a).start()
+
+    def move(self, g, d):
+        p = self.place
+        for kind, a, inside, fed in (
+            (UP, p.a + d, p.a + d <= p.n - 1, p.a > 0),
+            (DOWN, p.a - d, p.a - d >= 0, p.a < p.n - 1),
+        ):
+            @pl.when(inside)
+            def _(kind=kind, a=a, fed=fed):
+                i, refs = self.after_first(g, a)
+                if self.late:
+                    self.second_copy(a).wait_recv()
+                    refs.append((self.second, a))
+                self.add(i, refs)
+
+                @pl.when(fed)
+                def _():
+                    at = self.line_at(g, a)
+                    self.line_wait(at)
+                    self.add(i, [(self.line, at)])
+
+                self.line_copy(kind, g, a).start()
 
     def finish(self, store):
         p = self.place
-        n = p.line_size
-        at, refs = self.settle(p.a)
-        self.add(at, *refs)
-        for kind, way, fed in ((UP, 0, p.a > 0), (DOWN, 1, p.a < n - 1)):
-            @pl.when(fed)
-            def _(kind=kind, way=way):
-                self.line_copy(kind, p.a).wait_recv()
-                self.add(at, (self.line, way * n + p.a))
-        store(self.mine[at].astype(F32))
-        self.loop(4 * n, lambda i: self.core_copy(i // (2 * n), (i // n) % 2, i % n).wait_send())
-        self.loop(2 * n, lambda i: self.first_copy(i // n, i % n).wait_send())
-        self.loop(n, lambda a: self.second_copy(a).wait_send())
+        n = p.n
+        i, refs = self.after_first(self.g, p.a)
+        to = p.a if self.late else 0
+        self.second_copy(p.a).wait_recv()
+        self.add(i, refs + [(self.second, to)])
+        self.add_line(i, self.g)
+        store(self.mine[i].astype(F32))
+        repeat(4 * n, lambda i: self.core_copy(i).wait_send())
+        repeat(2 * n, lambda i: self.first_copy(i // n, i % n).wait_send())
+        if self.late:
+            repeat(n, lambda a: self.second_copy(a).wait_send())
+        else:
+            self.second_copy(p.a).wait_send()
 
         def line_done(a):
             for kind, inside in ((UP, a > p.a), (DOWN, a < p.a)):
                 @pl.when(inside)
                 def _(kind=kind):
-                    self.line_copy(kind, a).wait_send()
-
-        self.loop(n, line_done)
-
-
-def scatter_scratch(count, shape, dtype=BF):
+                    for g in (self.g,) if self.late else (0, 1):
+                        self.line_copy(kind, g, a).wait_send()
+
+        repeat(n, line_done)
+
+
+def scatter_scratch(count, shape, order):
     n = count // 4
+    late = order[2] == "z"
+    lines = n + 1 if late else 2 * n + 2
     return [
-        *[pltpu.VMEM((k * n, *shape), dtype) for k in (4, 4, 2, 1, 2)],
+        *[pltpu.VMEM((k, *shape), BF) for k in (4 * n, 4 * n, 2 * n, n if late else 1, lines)],
         pltpu.SemaphoreType.DMA((4 * n,)),
         pltpu.SemaphoreType.DMA((9 * n,)),
-        pltpu.SemaphoreType.DMA((9 * n,)),
+        pltpu.SemaphoreType.DMA((7 * n + lines,)),
     ]
 
 
-def block_pairs(ref, rows, count):
+SCATTER_ORDERS = ("yzx", "xzy", "yxz", "xyz")
+
+
+def block_scatters(rows, first):
+    return [(at, size, SCATTER_ORDERS[(first + i) % 4]) for i, (at, size) in enumerate(halves(rows))]
+
+
+def block_pairs(ref, rows, at, size, count):
     def view(h, s, target):
-        return [(ref.at[pl.ds(pl.multiple_of((h * count + s) * rows, rows), rows)], target)]
+        return [(ref.at[pl.ds(pl.multiple_of((h * count + s) * rows + at, size), size)], target)]
 
     return view
 
 
-def square_pairs(refs, r, w):
+def square_pairs(ref, r, w):
     def view(h, s, target):
-        here = (pl.ds(pl.multiple_of(s * r, r), r), pl.ds(pl.multiple_of(h * w, w), w))
-        return [(ref.at[here], target.at[i]) for i, ref in enumerate(refs)]
+        return [(ref.at[pl.ds(pl.multiple_of(s * r, r), r), pl.ds(pl.multiple_of(h * w, w), w)], target)]
 
     return view
 
 
-def run_scatters(units, stores, between=lambda at: None):
-    for unit in units:
-        unit.begin()
-    between(0)
-    for unit in units:
-        unit.flip_first()
-    between(1)
-    for unit in units:
-        unit.flip_second()
-    between(2)
-    for unit in units:
-        unit.along()
-    between(3)
-    for unit, store in zip(units, stores):
-        unit.finish(store)
-    between(4)
+def scatter_steps(place, units, stores, between=lambda at: None):
+    n = place.n
+    middle = [u for u in units if not u.late]
+    late = [u for u in units if u.late]
+
+    def each(run, some=units):
+        def one(i):
+            for unit in some:
+                run(unit, i)
+
+        return one
+
+    def begin():
+        repeat(n, each(lambda u, i: u.start(1 - u.f, 1 - u.g, place.along(i))))
+        repeat(n, each(lambda u, i: u.start(1 - u.f, u.g, place.along(i))))
+        repeat(n, each(lambda u, i: u.start(u.f, 1 - u.g, place.along(i))))
+        repeat(n, each(lambda u, i: u.start(u.f, u.g, place.along(i))))
+        between(0)
+
+    def flips():
+        repeat(n, each(lambda u, i: u.flip_first(1 - u.g, place.along(i)), middle))
+        repeat(n, each(lambda u, i: u.flip_first(1 - u.g, place.along(i)), late))
+        repeat(n, each(lambda u, i: u.flip_first(u.g, place.along(i)), middle))
+        repeat(n, each(lambda u, i: u.flip_first(u.g, place.along(i)), late))
+        between(1)
+
+    def second(d):
+        for u in middle:
+            u.move(1 - u.g, d)
+        for u in late:
+            u.flip_second(place.along(n - 1 - d))
+
+    def third(d):
+        for u in middle:
+            u.move(u.g, d)
+
+    def fourth():
+        for u in late:
+            u.flip_second(place.along(n - 1))
+        for u in middle:
+            u.flip_second(place.a)
+        between(2)
+
+    def fifth(d):
+        for u in late:
+            u.move(u.g, d)
+
+    def finish():
+        between(3)
+        for unit, store in zip(units, stores):
+            unit.finish(store)
+        between(4)
+
+    far = range(n - 1, 0, -1)
+    return (
+        [begin, flips]
+        + [functools.partial(second, d) for d in far]
+        + [functools.partial(third, d) for d in far]
+        + [fourth]
+        + [functools.partial(fifth, d) for d in far]
+        + [finish]
+    )
+
+
+def store_into(out):
+    def store(value):
+        out[...] = value
+
+    return store
+
+
+def scatter_dense_units(place, count, grads, outs, scratch):
+    units, stores = [], []
+    for ref, out, first in zip(grads, outs, (0, 2, 1)):
+        rows = out.shape[0]
+        for at, size, order in block_scatters(rows, first):
+            units.append(Scatter(place, block_pairs(ref, rows, at, size, count), order, *scratch[:8]))
+            stores.append(store_into(out.at[pl.ds(at, size)]))
+            scratch = scratch[8:]
+    return units, stores
+
+
+def scatter_dense_scratch(count, shapes):
+    scratch = []
+    for (rows, width), first in zip(shapes, (0, 2, 1)):
+        for at, size, order in block_scatters(rows, first):
+            scratch += scatter_scratch(count, (size, width), order)
+    return scratch
 
 
 def scatter_dense_kernel(count, up, down, o, up_out, down_out, o_out, *scratch):
     place = Place(count)
     place.barrier()
-    units, stores = [], []
-    for i, (ref, out, order) in enumerate(((up, up_out, 0), (down, down_out, 1), (o, o_out, 1))):
-        units.append(Scatter(place, block_pairs(ref, out.shape[0], count), order, *scratch[8 * i : 8 * i + 8]))
-
-        def store(value, out=out):
-            out[...] = value
-
-        stores.append(store)
-    run_scatters(units, stores)
+    units, stores = scatter_dense_units(place, count, (up, down, o), (up_out, down_out, o_out), scratch)
+    for step in scatter_steps(place, units, stores):
+        step()
 
 
 def scatter_attention_kernel(
@@ -644,17 +772,16 @@
     place = Place(count)
     place.barrier()
     r, w = q_out.shape
-    units = [
-        Scatter(place, square_pairs((q, k, v, p), r, w), 0, *scratch[:8]),
-        Scatter(place, block_pairs(sq, sq_out.shape[0], count), 1, *scratch[8:]),
-    ]
-
-    def store_square(value):
-        for i, out in enumerate((q_out, k_out, v_out, p_out)):
-            out[...] = value[i]
-
-    def store_sq(value):
-        sq_out[...] = value
+    units, stores = [], []
+    for ref, out, order in zip((q, k, v, p), (q_out, k_out, v_out, p_out), SCATTER_ORDERS):
+        units.append(Scatter(place, square_pairs(ref, r, w), order, *scratch[:8]))
+        stores.append(store_into(out))
+        scratch = scratch[8:]
+    rows = sq_out.shape[0]
+    for at, size, order in block_scatters(rows, 0):
+        units.append(Scatter(place, block_pairs(sq, rows, at, size, count), order, *scratch[:8]))
+        stores.append(store_into(sq_out.at[pl.ds(at, size)]))
+        scratch = scratch[8:]
 
     def vec_copy(kind):
         return pltpu.make_async_remote_copy(
@@ -678,7 +805,7 @@
         elif at == 3:
             vec_copy(YFLIP).wait_recv()
             total = sums[YFLIP] + parts[YFLIP]
-            ends = (place.a > 0, place.a < place.line_size - 1)
+            ends = (place.a > 0, place.a < place.n - 1)
             sums[UP] = total
             sums[DOWN] = total
             for kind, fed in ((UP, ends[0]), (DOWN, ends[1])):
@@ -708,22 +835,20 @@
                 def _(kind=kind):
                     vec_copy(kind).wait_send()
 
-    run_scatters(units, (store_square, store_sq), between)
+    for step in scatter_steps(place, units, stores, between):
+        step()
 
 
 def scatter_dense(g):
     count = lax.axis_size("seq")
     names = ("up", "down", "o")
     shapes = [(g[n].shape[0] // (2 * count), g[n].shape[1]) for n in names]
-    scratch = []
-    for shape in shapes:
-        scratch += scatter_scratch(count, shape)
     outs = pl.pallas_call(
         functools.partial(scatter_dense_kernel, count),
         in_specs=[pl.BlockSpec(memory_space=pl.ANY)] * 3,
         out_specs=[pl.BlockSpec(memory_space=pltpu.VMEM)] * 3,
         out_shape=[jax.ShapeDtypeStruct(shape, F32) for shape in shapes],
-        scratch_shapes=scratch,
+        scratch_shapes=scatter_dense_scratch(count, shapes),
         compiler_params=pltpu.CompilerParams(collective_id=1, has_side_effects=True, vmem_limit_bytes=48 * MIB),
         name="scatter_dense",
     )(*[g[n] for n in names])
@@ -741,6 +866,11 @@
     vec = jnp.concatenate(lines + [jnp.zeros((12 - len(lines), width), F32), g["ub"].reshape(-1, width)], axis=0)
     square = (width // count, width // 2)
     narrow = (both, g["sq"].shape[1])
+    scratch = []
+    for order in SCATTER_ORDERS:
+        scratch += scatter_scratch(count, square, order)
+    for at, size, order in block_scatters(both, 0):
+        scratch += scatter_scratch(count, (size, narrow[1]), order)
     vmem = pl.BlockSpec(memory_space=pltpu.VMEM)
     outs = pl.pallas_call(
         functools.partial(scatter_attention_kernel, count),
@@ -753,8 +883,7 @@
             pltpu.VMEM((5, 16, width), F32),
             pltpu.SemaphoreType.DMA((5,)),
             pltpu.SemaphoreType.DMA((5,)),
-            *scatter_scratch(count, (4, *square)),
-            *scatter_scratch(count, narrow),
+            *scratch,
         ],
         compiler_params=pltpu.CompilerParams(collective_id=2, has_side_effects=True, vmem_limit_bytes=48 * MIB),
         name="scatter_attention",
@@ -817,14 +946,14 @@
     own_length = window[4]
 
     memory = shifted(x, "seq", 1)
-    w = gather_all(
-        dict(
+    shards = dict(
             q=query_weight, k=key_weight, v=value_weight, p=position_weight,
             o=output_weight, up=up_weight.T, down=down_weight, sq=squeeze_weight.T,
             cb=content_bias, pb=position_bias, ob=output_bias, g1=first_gain, s1=first_shift, ub=up_bias,
             db=down_bias, g2=second_gain, s2=second_shift, sb=squeeze_bias,
-        )
     )
+    w = gather_attention(shards)
+    w.update(gather_dense(shards))
     cb, pb, ob, g1, s1, ub, db, g2, s2, sb = (
         w[n] for n in ("cb", "pb", "ob", "g1", "s1", "ub", "db", "g2", "s2", "sb")
     )

time: 751 us -> 677 us (0.901)
  Pallas kernels: 474 us -> 414 us
    pallas_call x1, Pallas kernels: 139 us -> 97.9 us  [scatter_dense(): pl.pallas_call(functools.partial(scatter_dense_kernel, count), in_specs=[...]
    pallas_call x1, Pallas kernels: 118 us -> 92.9 us  [scatter_attention(): pl.pallas_call(functools.partial(scatter_attention_kernel, count), in_spe...]
    ppermute x8, starting transfers between devices: 25.5 us -> 16.9 us  [shifted(): return lax.ppermute(array, axis, pairs)]
    pallas_call x1 -> x2, Pallas kernels: 155 us -> 161 us  [the longest x1 88.3 us: gather_dense(): pl.pallas_call(functools.partial(gather_dense_kernel, count), in_specs=[a...]
    unnamed x156 -> x164, local copies, waits for them, and re-layouts: 24.5 us -> 25.9 us
  transfers between devices with their start and end apart: 10 -> 10, of which waited for: 1 -> 1; matrix products, arithmetic and copies ran while one was open for 13% -> 15% of each run, Pallas kernels for 55% -> 52%
where the time goes in v2:
time: 677 us; the launch traced here: 670 us
  Pallas kernels  414 us (61%)
  matrix products  176 us (26%)
  local copies, waits for them, and re-layouts  33.4 us (5%)
  starting transfers between devices  21.9 us (3%)
  other arithmetic  18.3 us (3%)
    dot_general x42, matrix products, mm(): lax.dot_general(left, right, (contract, ((), ())), preferred_element_type...  176 us
    pallas_call x1, Pallas kernels, scatter_dense(): pl.pallas_call(functools.partial(scatter_dense_kernel, count), in_specs=[...  97.9 us
    pallas_call x1, Pallas kernels, scatter_attention(): pl.pallas_call(functools.partial(scatter_attention_kernel, count), in_spe...  92.9 us
    pallas_call x1, Pallas kernels, gather_dense(): pl.pallas_call(functools.partial(gather_dense_kernel, count), in_specs=[a...  88.3 us
    pallas_call x1, Pallas kernels, gather_attention(): pl.pallas_call(functools.partial(gather_attention_kernel, count, layout),...  72.5 us
    pallas_call x1, Pallas kernels, attend_backward(): pl.pallas_call(attend_backward_kernel, grid=(heads,), in_specs=[vec_spec,...  33.9 us
    pallas_call x1, Pallas kernels, attend_forward(): pl.pallas_call(attend_forward_kernel, grid=(heads,), in_specs=[pl.BlockSp...  28.1 us
    unnamed x164, local copies, waits for them, and re-layouts  25.9 us
  transfers between devices with their start and end apart: 10, of which 1 were waited for; matrix products, arithmetic and copies ran while one was open for 15% of the time, Pallas kernels for 52%

profile of v2, /device:TPU:6, one launch (start us, length us, event | category | flops | bytes accessed | tf_op | source)
XLA Modules:
  0.0 670.1 jit_solution(12345473845071467599)
XLA Ops:
  5.6 72.5 %gather_attention.1 = (bf16[1024,1024]{1,0:T(8,128)(2,1)S(1)}, bf16[1024,1024]{1,0:T(8,128)(2,1)S(1)}, bf16[1024,1024]{1,0:T(8,128)(2,1)S(1)}, bf16[1024,1024]{1...) custom-call(bf16[64,512]{1,0:T(8,128)(2,1)S(1)} %copy-done.12, ...), custom_call_target="tpu_custom_call" | custom-call | tf_op jit(solution)/shard_map/gather_attention/pallas_call | solution.py:455
  86.3 5.7 fusion.22
  92.0 5.7 fusion.26
  97.7 6.6 add_convert_fusion
  108.3 4.4 collective-permute-start.1
  114.7 4.0 fusion.58.q_ref
  118.7 4.8 fusion.7.pl_ref
  126.4 88.3 %gather_dense.1 = (bf16[4096,1024]{1,0:T(8,128)(2,1)S(1)}, bf16[4096,1024]{1,0:T(8,128)(2,1)S(1)}, bf16[1024,1024]{1,0:T(8,128)(2,1)S(1)}) custom-call(bf16[128,1024]{1,0:T(8,128)(2,1)S(1)} %bitcast.179, bf16[128,1024]{1,0:T(8,128)(2,1)S(1)} %copy-done.10, bf16[32,1024]{1,0:T(8,128)(2,1)S(1)} %copy-done.16), custom_call_target="tpu_custom_call" | custom-call | tf_op jit(solution)/shard_map/gather_dense/pallas_call | solution.py:482
  214.6 3.3 copy-done.17
  225.4 6.7 %convolution_convert_fusion.4.k_ref = bf16[1536,1024]{1,0:T(8,128)(2,1)} fusion(bf16[1024,1024]{1,0:T(8,128)(2,1)S(1)} %copy-done.21, bf16[512,1024]{1,0:T(8,128)(2,1)} %dynamic-slice_bitcast_fusion, bf16[512,1024]{1,0:T(8,128)(2,1)} %collective-permute-done.3, bf16[512,1024]{1,0:T(8,128)(2,1)S(1)} %fusion.35), kind=kOutput, calls=%fused_computation.17 | convolution fusion | flops 3232235520 | bytes 8388608 | tf_op jit(solution)/shard_map/dot_general | solution.py:19
  232.1 6.6 convolution_convert_fusion.3.v_ref
  238.7 28.1 %attend_forward.1 = (bf16[512,1024]{1,0:T(8,128)(2,1)S(1)}, bf16[8,512,1536]{2,1,0:T(8,128)(2,1)}) custom-call(f32[1,1536]{1,0:T(1,128)S(1)} %add_select_fusion.bias_ref, f32[1,1024]{1,0:T(1,128)S(1)} %get-tuple-element.126.cb_ref, f32[1,1024]{1,0:T(1,128)S(1)} %get-tuple-element.125.pb_ref, f32[512,1024]{1,0:T(8,128)S(1)} %copy-done.27, ...), custom_call_target="tpu_custom_call" | custom-call | flops 4831838208 | bytes 12582912 | tf_op jit(solution)/shard_map/attend_forward/pallas_call | solution.py:144
  266.9 3.0 fusion.54
  270.2 7.1 %fusion.57 = f32[512,4096]{1,0:T(8,128)} fusion(bf16[4096,1024]{1,0:T(8,128)(2,1)S(1)} %get-tuple-element.56, f32[512,1024]{1,0:T(8,128)S(1)} %get-tuple-element.142, f32[1024]{0:T(1024)S(1)} %bitcast.200, f32[1024]{0:T(1024)S(1)} %bitcast.189, f32[512]{0:T(512)S(1)} %add_rsqrt_fusion.1, f32[512]{0:T(512)S(1)} %broadcast_multiply_fusion.5), kind=kOutput, calls=%fused_computation.141 | convolution fusion | flops 4297588736 | bytes 18886656 | tf_op jit(solution)/shard_map/dot_general | solution.py:19
  277.3 10.8 %fusion.55 = (f32[512]{0:T(512)S(1)}, f32[512,1024]{1,0:T(8,128)S(1)}) fusion(f32[1024]{0:T(1024)S(1)} %bitcast.203, bf16[4096,1024]{1,0:T(8,128)(2,1)} %copy-done.17, f32[512,4096]{1,0:T(8,128)} %fusion.57, f32[4096]{0:T(1024)S(1)} %bitcast.183, f32[1024]{0:T(1024)S(1)} %bitcast.201, f32[1024]{0:T(1024)S(1)} %bitcast.190, f32[512]{0:T(512)S(1)} %add_rsqrt_fusion.1, ...), kind=kOutput, calls=%fused_computation.139 | convolution fusion | flops 4320656896 | bytes 21006336 | tf_op jit(solution)/shard_map/dot_general | solution.py:19
  293.2 14.9 %convert_reduce_fusion = (f32[4096]{0:T(1024)S(1)}, bf16[512,4096]{1,0:T(8,128)(2,1)}) fusion(f32[512,4096]{1,0:T(8,128)} %fusion.57, f32[4096]{0:T(1024)S(1)} %bitcast.184, bf16[4096,1024]{1,0:T(8,128)(2,1)} %copy-done.17, f32[512,1024]{1,0:T(8,128)} %get-tuple-element.104), kind=kOutput, calls=%fused_computation.9 | convolution fusion | flops 4341624832 | bytes 23101440 | tf_op jit(solution)/shard_map/dot_general | solution.py:19
  308.0 8.0 %multiply_reduce_fusion = (f32[1024]{0:T(1024)S(1)}, f32[512]{0:T(512)S(1)}, f32[512]{0:T(512)S(1)}, f32[1024]{0:T(1024)S(1)}, f32[512,1024]{1,0:T(8,128)S(1)}) fusion(f32[512,1024]{1,0:T(8,128)S(1)} %get-tuple-element.142, f32[512]{0:T(512)S(1)} %add_rsqrt_fusion.1, f32[512]{0:T(512)S(1)} %broadcast_multiply_fusion.5, f32[1024]{0:T(1024)S(1)} %bitcast.191, ...), kind=kOutput, calls=%fused_computation.40 | convolution fusion | flops 4300207104 | bytes 18894848 | tf_op jit(solution)/shard_map/dot_general | solution.py:19
  318.1 33.9 %attend_backward.1 = (bf16[512,1024]{1,0:T(8,128)(2,1)S(1)}, f32[1,1024]{1,0:T(1,128)S(1)}, f32[1,1024]{1,0:T(1,128)S(1)}, bf16[1536,1024]{1,0:T(8,128)(2,1)}, b...) custom-call(f32[1,1024]{1,0:T(1,128)S(1)} %get-tuple-element.126.cb_ref, f32[1,1024]{1,0:T(1,128)S(1)} %get-tuple-element.125.pb_ref, ...), custom_call_target="tpu_custom_call" | custom-call | flops 9663676416 | bytes 12582912 | tf_op jit(solution)/shard_map/attend_backward/pallas_call | solution.py:170
  352.1 5.6 fusion.59
  357.7 5.7 fusion.56
  366.4 7.7 %convolution_convert_fusion.1.up = bf16[4096,1024]{1,0:T(8,128)(2,1)} fusion(bf16[512,4096]{1,0:T(8,128)(2,1)S(1)} %copy-done.74, f32[512,1024]{1,0:T(8,128)S(1)} %copy-done.33, f32[1024]{0:T(1024)S(1)} %bitcast.202, f32[1024]{0:T(1024)S(1)} %bitcast.193, f32[512]{0:T(512)S(1)} %add_rsqrt_fusion.1, f32[512]{0:T(512)S(1)} %broadcast_multiply_fusion.5), kind=kOutput, calls=%fused_computation.12 | convolution fusion | flops 4301783040 | bytes 14692352 | tf_op jit(solution)/shard_map/dot_general | solution.py:19
  374.1 13.4 %convolution_convert_fusion.down = bf16[4096,1024]{1,0:T(8,128)(2,1)} fusion(f32[512,1024]{1,0:T(8,128)S(1)} %copy-done.38, f32[512,4096]{1,0:T(8,128)} %fusion.57, f32[4096]{0:T(1024)S(1)} %bitcast.185), kind=kOutput, calls=%fused_computation.11 | convolution fusion | flops 4320657408 | bytes 18890752 | tf_op jit(solution)/shard_map/dot_general | solution.py:19
  389.7 3.3 collective-permute-start.4
  402.8 4.9 convert_bitcast_fusion.1.p
  407.8 6.4 convolution_convert_fusion.10.k
  414.2 6.3 convolution_convert_fusion.9.v
  420.5 3.9 convolution_convert_fusion.11.q
  424.4 97.9 %scatter_dense.1 = (f32[128,1024]{1,0:T(8,128)S(1)}, f32[128,1024]{1,0:T(8,128)S(1)}, f32[32,1024]{1,0:T(8,128)S(1)}) custom-call(bf16[4096,1024]{1,0:T(8,128)(2,1)} %convolution_convert_fusion.1.up, bf16[4096,1024]{1,0:T(8,128)(2,1)} %convolution_convert_fusion.down, bf16[1024,1024]{1,0:T(8,128)(2,1)S(1)} %convolution_convert_fusion.5.o), custom_call_target="tpu_custom_call" | custom-call | tf_op jit(solution)/shard_map/scatter_dense/pallas_call | solution.py:846
  547.7 3.3 pad_maximum_fusion.sq
  552.1 92.9 %scatter_attention.1 = (f32[64,512]{1,0:T(8,128)S(1)}, f32[64,512]{1,0:T(8,128)S(1)}, f32[64,512]{1,0:T(8,128)S(1)}, f32[64,512]{1,0:T(8,128)S(1)}, f32[32,3072]...) custom-call(bf16[1024,1024]{1,0:T(8,128)(2,1)S(1)} %copy-done.6, bf16[1024,1024]{1,0:T(8,128)(2,1)S(1)} %copy-done.5, ...), custom_call_target="tpu_custom_call" | custom-call | tf_op jit(solution)/shard_map/scatter_attention/pallas_call | solution.py:875
  649.8 3.8 fusion.19
  658.3 4.7 collective-permute-done.9
  (247 shorter events, 93.6 us)
Async XLA Ops:
  0.8 83.9 %copy-start.64 = (s32[2,16]{1,0:T(2,128)S(1)}, s32[2,16]{1,0:T(2,128)}, u32[]{:S(2)}) copy-start(s32[2,16]{1,0:T(2,128)} %param.34) | copy-start | bytes 388
  3.3 222.0 %collective-permute-start.3 = (bf16[512,1024]{1,0:T(8,128)(2,1)}, bf16[512,1024]{1,0:T(8,128)(2,1)}, u32[]{:S(2)}, u32[]{:S(2)}) collective-permute-start(bf16[512,1024]{1,0:T(8,128)(2,1)} %dynamic-slice_bitcast_fusion), channel_id=1, source_target_pairs={{0,1},{1,2},{2,3},{3,4},{4,5},{5,6},{6,7},{7,8},{8,9},{9,10},{10,1... | collective-permute-start | bytes 3145736 | tf_op jit(solution)/shard_map/ppermute | solution.py:33
  84.7 29.9 %copy-start.3 = (bf16[1024,1024]{1,0:T(8,128)(2,1)}, bf16[1024,1024]{1,0:T(8,128)(2,1)S(1)}, u32[]{:S(2)}) copy-start(bf16[1024,1024]{1,0:T(8,128)(2,1)S(1)} %get-tuple-element.49) | copy-start | bytes 6291460
  86.3 28.3 %copy-start.49 = (pred[512]{0:T(512)(128)(4,1)}, pred[512]{0:T(512)(128)(4,1)S(1)}, u32[]{:S(2)}) copy-start(pred[512]{0:T(512)(128)(4,1)S(1)} %iota_compare_fusion) | copy-start | bytes 1540
  106.3 114.4 %collective-permute-start = (bf16[176,1024]{1,0:T(8,128)(2,1)}, bf16[176,1024]{1,0:T(8,128)(2,1)}, u32[]{:S(2)}, u32[]{:S(2)}) collective-permute-start(bf16[176,1024]{1,0:T(8,128)(2,1)} %get-tuple-element.117), channel_id=1, source_target_pairs={{0,4},{1,5},{2,6},{3,7},{4,8},{5,9},{6,10},{7,11},{8,12},{9,13},{1... | collective-permute-start | bytes 1081352 | tf_op jit(solution)/shard_map/ppermute | solution.py:33
  108.3 113.9 %collective-permute-start.1 = (bf16[176,1024]{1,0:T(8,128)(2,1)S(1)}, bf16[176,1024]{1,0:T(8,128)(2,1)}, u32[]{:S(2)}, u32[]{:S(2)}) collective-permute-start(bf16[176,1024]{1,0:T(8,128)(2,1)S(1)} %get-tuple-element.115), channel_id=1, source_target_pairs={{0,3},{1,4},{2,5},{3,6},{4,7},{5,8},{6,9},{7,10},{8,11},{9,12},{10... | collective-permute-start | bytes 1081352 | tf_op jit(solution)/shard_map/ppermute | solution.py:33
  112.7 111.0 %collective-permute-start.2 = (bf16[176,1024]{1,0:T(8,128)(2,1)S(1)}, bf16[176,1024]{1,0:T(8,128)(2,1)}, u32[]{:S(2)}, u32[]{:S(2)}) collective-permute-start(bf16[176,1024]{1,0:T(8,128)(2,1)S(1)} %get-tuple-element.116), channel_id=1, source_target_pairs={{0,2},{1,3},{2,4},{3,5},{4,6},{5,7},{6,8},{7,9},{8,10},{9,11},{10,... | collective-permute-start | bytes 1081352 | tf_op jit(solution)/shard_map/ppermute | solution.py:33
  118.7 7.5 %copy-start.45 = (bf16[1024,128]{1,0:T(8,128)(2,1)S(1)}, bf16[1024,128]{1,0:T(8,128)(2,1)}, u32[]{:S(2)}) copy-start(bf16[1024,128]{1,0:T(8,128)(2,1)} %param.45) | copy-start | bytes 786436
  118.7 7.6 %copy-start.10 = (bf16[128,1024]{1,0:T(8,128)(2,1)S(1)}, bf16[128,1024]{1,0:T(8,128)(2,1)}, u32[]{:S(2)}) copy-start(bf16[128,1024]{1,0:T(8,128)(2,1)} %refs_1_.3) | copy-start | bytes 786436
  118.7 7.6 %copy-start.16 = (bf16[32,1024]{1,0:T(8,128)(2,1)S(1)}, bf16[32,1024]{1,0:T(8,128)(2,1)}, u32[]{:S(2)}) copy-start(bf16[32,1024]{1,0:T(8,128)(2,1)} %refs_2_.3) | copy-start | bytes 196612
  126.3 95.9 %copy-start.47 = (bf16[512,176]{1,0:T(8,128)(2,1)S(1)}, bf16[512,176]{1,0:T(8,128)(2,1)}, u32[]{:S(2)}) copy-start(bf16[512,176]{1,0:T(8,128)(2,1)} %constant.103) | copy-start | bytes 540676
  225.3 6.8 %copy-start.40 = (bf16[512,1024]{1,0:T(8,128)(2,1)}, bf16[512,1024]{1,0:T(8,128)(2,1)S(1)}, u32[]{:S(2)}) copy-start(bf16[512,1024]{1,0:T(8,128)(2,1)S(1)} %fusion.35) | copy-start | bytes 3145732
  225.4 6.7 %copy-start.19 = (bf16[1024,1024]{1,0:T(8,128)(2,1)S(1)}, bf16[1024,1024]{1,0:T(8,128)(2,1)}, u32[]{:S(2)}) copy-start(bf16[1024,1024]{1,0:T(8,128)(2,1)} %copy-done.18) | copy-start | bytes 6291460
  232.1 6.6 copy-start.27
  238.7 28.1 %copy-start.24 = (bf16[1024,1024]{1,0:T(8,128)(2,1)S(1)}, bf16[1024,1024]{1,0:T(8,128)(2,1)}, u32[]{:S(2)}) copy-start(bf16[1024,1024]{1,0:T(8,128)(2,1)} %copy-done.23) | copy-start | bytes 6291460
  269.8 46.3 %copy-start.32 = (f32[512,1024]{1,0:T(8,128)}, f32[512,1024]{1,0:T(8,128)S(1)}, u32[]{:S(2)}) copy-start(f32[512,1024]{1,0:T(8,128)S(1)} %get-tuple-element.142) | copy-start | bytes 6291460
  316.8 70.7 %copy-start.30 = (f32[512,1024]{1,0:T(8,128)}, f32[512,1024]{1,0:T(8,128)S(1)}, u32[]{:S(2)}) copy-start(f32[512,1024]{1,0:T(8,128)S(1)} %get-tuple-element.106) | copy-start | bytes 6291460
  318.1 33.9 %copy-start.22 = (bf16[1024,1024]{1,0:T(8,128)(2,1)S(1)}, bf16[1024,1024]{1,0:T(8,128)(2,1)}, u32[]{:S(2)}) copy-start(bf16[1024,1024]{1,0:T(8,128)(2,1)} %copy-done.20) | copy-start | bytes 6291460
  357.6 8.0 %copy-start.74 = (bf16[512,4096]{1,0:T(8,128)(2,1)S(1)}, bf16[512,4096]{1,0:T(8,128)(2,1)}, u32[]{:S(2)}) copy-start(bf16[512,4096]{1,0:T(8,128)(2,1)} %get-tuple-element.149) | copy-start | bytes 12582916
  366.4 7.7 %copy-start.38 = (f32[512,1024]{1,0:T(8,128)S(1)}, f32[512,1024]{1,0:T(8,128)}, u32[]{:S(2)}) copy-start(f32[512,1024]{1,0:T(8,128)} %get-tuple-element.104) | copy-start | bytes 6291460
  374.1 13.4 %copy-start.29 = (bf16[512,1024]{1,0:T(8,128)(2,1)S(1)}, bf16[512,1024]{1,0:T(8,128)(2,1)}, u32[]{:S(2)}) copy-start(bf16[512,1024]{1,0:T(8,128)(2,1)} %copy-done.28) | copy-start | bytes 3145732
  388.8 13.9 %copy-start.73 = (bf16[1536,1024]{1,0:T(8,128)(2,1)S(1)}, bf16[1536,1024]{1,0:T(8,128)(2,1)}, u32[]{:S(2)}) copy-start(bf16[1536,1024]{1,0:T(8,128)(2,1)} %get-tuple-element.63) | copy-start | bytes 9437188
  389.7 13.1 %copy-start.66 = (bf16[1536,1024]{1,0:T(8,128)(2,1)S(1)}, bf16[1536,1024]{1,0:T(8,128)(2,1)}, u32[]{:S(2)}) copy-start(bf16[1536,1024]{1,0:T(8,128)(2,1)} %constant.93.clone) | copy-start | bytes 9437188
  389.7 266.2 %collective-permute-start.4 = (bf16[256,1024]{1,0:T(8,128)(2,1)}, bf16[256,1024]{1,0:T(8,128)(2,1)}, u32[]{:S(2)}, u32[]{:S(2)}) collective-permute-start(bf16[256,1024]{1,0:T(8,128)(2,1)} %constant_dynamic-slice_fusion.1), channel_id=1, source_target_pairs={{0,16},{16,0},{1,17},{17,1},{2,18},{18,2},{3,19},{19,3},{4,20},{20... | collective-permute-start | bytes 1572872 | tf_op jit(solution)/shard_map/ppermute | solution.py:926
  396.0 130.0 %collective-permute-start.6 = (bf16[176,1024]{1,0:T(8,128)(2,1)}, bf16[176,1024]{1,0:T(8,128)(2,1)}, u32[]{:S(2)}, u32[]{:S(2)}) collective-permute-start(bf16[176,1024]{1,0:T(8,128)(2,1)} %get-tuple-element.114), channel_id=1, source_target_pairs={{4,0},{5,1},{6,2},{7,3},{8,4},{9,5},{10,6},{11,7},{12,8},{13,9},{1... | collective-permute-start | bytes 1081352 | tf_op jit(solution)/shard_map/ppermute | solution.py:33
  397.3 130.3 %collective-permute-start.7 = (bf16[176,1024]{1,0:T(8,128)(2,1)}, bf16[176,1024]{1,0:T(8,128)(2,1)}, u32[]{:S(2)}, u32[]{:S(2)}) collective-permute-start(bf16[176,1024]{1,0:T(8,128)(2,1)} %get-tuple-element.112), channel_id=1, source_target_pairs={{3,0},{4,1},{5,2},{6,3},{7,4},{8,5},{9,6},{10,7},{11,8},{12,9},{13... | collective-permute-start | bytes 1081352 | tf_op jit(solution)/shard_map/ppermute | solution.py:33
  398.6 130.6 %collective-permute-start.8 = (bf16[176,1024]{1,0:T(8,128)(2,1)}, bf16[176,1024]{1,0:T(8,128)(2,1)}, u32[]{:S(2)}, u32[]{:S(2)}) collective-permute-start(bf16[176,1024]{1,0:T(8,128)(2,1)} %get-tuple-element.113), channel_id=1, source_target_pairs={{2,0},{3,1},{4,2},{5,3},{6,4},{7,5},{8,6},{9,7},{10,8},{11,9},{12,... | collective-permute-start | bytes 1081352 | tf_op jit(solution)/shard_map/ppermute | solution.py:33
  400.9 248.0 %collective-permute-start.5 = (bf16[512,1024]{1,0:T(8,128)(2,1)}, bf16[512,1024]{1,0:T(8,128)(2,1)}, u32[]{:S(2)}, u32[]{:S(2)}) collective-permute-start(bf16[512,1024]{1,0:T(8,128)(2,1)} %slice.162), channel_id=1, source_target_pairs={{1,0},{2,1},{3,2},{4,3},{5,4},{6,5},{7,6},{8,7},{9,8},{10,9},{11,1... | collective-permute-start | bytes 3145736 | tf_op jit(solution)/shard_map/ppermute | solution.py:33
  424.4 101.6 %copy-start.48 = (f32[1024]{0:T(1024)S(1)}, f32[1024]{0:T(1024)}, u32[]{:S(2)}) copy-start(f32[1024]{0:T(1024)} %convert_reduce_fusion.1) | copy-start | bytes 12292
  547.7 97.4 %slice-start = ((s8[6291456]{0:T(1024)(128)(4,1)}), s8[4194304]{0:T(1024)(128)(4,1)S(1)}, s32[]{:S(2)}) async-start(s8[6291456]{0:T(1024)(128)(4,1)} %bitcast.177), calls=%async_computation | async-start | bytes 8388608
  552.1 92.9 %slice-start.1 = ((s8[6291456]{0:T(1024)(128)(4,1)}), s8[2097152]{0:T(1024)(128)(4,1)S(1)}, s32[]{:S(2)}) async-start(s8[6291456]{0:T(1024)(128)(4,1)} %bitcast.177), calls=%async_computation.1 | async-start | bytes 4194304
  653.7 9.2 %collective-permute-start.9 = (bf16[256,1024]{1,0:T(8,128)(2,1)S(1)}, bf16[256,1024]{1,0:T(8,128)(2,1)S(1)}, u32[]{:S(2)}, u32[]{:S(2)}) collective-permute-start(bf16[256,1024]{1,0:T(8,128)(2,1)S(1)} %constant_dynamic-slice_fusion), channel_id=1, source_target_pairs={{0,16},{16,0},{1,17},{17,1},{2,18},{18,2},{3,19},{19,3},{4,20},{20... | collective-permute-start | bytes 1572872 | tf_op jit(solution)/shard_map/ppermute | solution.py:926
  (55 other events, 204.4 us)

commit v3 on v2

--- a/solution.py
+++ b/solution.py
@@ -56,141 +56,6 @@
             if role == 0 or 3 * c >= role * rows:
                 biased[role * pad + c - first] = 1.0
     return pad, taps.astype(BF), collect.astype(BF), biased
-
-
-def attend_forward_kernel(bias_ref, cb_ref, pb_ref, q_ref, k_ref, v_ref, pl_ref, out_ref, p_ref, s_scr, x_scr):
-    rows = q_ref.shape[0]
-    keys = k_ref.shape[0]
-    scale = HD ** (-0.5)
-    q = q_ref[...]
-    content_query = ((q + cb_ref[...]) * scale).astype(BF)
-    place_query = ((q + pb_ref[...]) * scale).astype(BF)
-    s_scr[...] = mm_nt(content_query, k_ref[...])
-    x_scr[...] = mm_nt(place_query, pl_ref[...])
-    step = 32
-    bias = bias_ref[...]
-    for start in range(0, rows, step):
-        here = slice(start, start + step)
-        located = pltpu.roll(
-            x_scr[here], (start + keys - rows + 1) % keys, 1, stride=1, stride_axis=0
-        )
-        scores = s_scr[here] + located + bias
-        row = start + lax.broadcasted_iota(jnp.int32, scores.shape, 0)
-        col = lax.broadcasted_iota(jnp.int32, scores.shape, 1)
-        scores = jnp.where(col <= 2 * rows + row, scores, -1e30)
-        top = jnp.max(scores, axis=1, keepdims=True)
-        weights = jnp.exp(scores - top)
-        total = jnp.sum(weights, axis=1, keepdims=True)
-        p_ref[0, here] = (weights * (1.0 / total)).astype(BF)
-    out_ref[...] = mm(p_ref[0], v_ref[...]).astype(BF)
-
-
-def attend_backward_kernel(
-    cb_ref, pb_ref, q_ref, k_ref, v_ref, pl_ref, p_ref, do_ref,
-    dq_ref, dcb_ref, dpb_ref, dk_ref, dv_ref, dpl_ref,
-    dp_scr, ds_scr, dx_scr,
-):
-    rows = q_ref.shape[0]
-    keys = k_ref.shape[0]
-    scale = HD ** (-0.5)
-    q = q_ref[...]
-    content_query = ((q + cb_ref[...]) * scale).astype(BF)
-    place_query = ((q + pb_ref[...]) * scale).astype(BF)
-    block = 128
-    flip = (
-        lax.broadcasted_iota(jnp.int32, (block, block), 0)
-        + lax.broadcasted_iota(jnp.int32, (block, block), 1)
-        == block - 1
-    ).astype(BF)
-    dp_scr[...] = mm_nt(do_ref[...], v_ref[...])
-    step = 32
-    for start in range(0, rows, step):
-        here = slice(start, start + step)
-        prob = p_ref[0, here].astype(F32)
-        dprob = dp_scr[here]
-        delta = jnp.sum(prob * dprob, axis=1, keepdims=True)
-        ds_scr[here] = (prob * (dprob - delta)).astype(BF)
-    dv_ref[...] = mm_tn(do_ref[...], p_ref[0]).T.astype(BF)
-    dk_ref[...] = mm_tn(content_query, ds_scr[...]).T.astype(BF)
-    dcq = mm(ds_scr[...], k_ref[...]) * scale
-    flipped = []
-    for start in range(0, rows, block):
-        here = slice(start, start + block)
-        dp_scr[here] = mm(flip, ds_scr[here])
-        flipped.append(mm(flip, place_query[here]).astype(BF))
-        dx_scr[here] = pltpu.roll(
-            dp_scr[here], rows - block - start, 1, stride=1, stride_axis=0
-        ).astype(BF)
-    dpl_ref[...] = mm_tn(jnp.concatenate(flipped, axis=0), dx_scr[...]).T.astype(BF)
-    dpq_flipped = mm(dx_scr[...], pl_ref[...]) * scale
-    dpq = []
-    for start in range(0, rows, block):
-        piece = dpq_flipped[start : start + block]
-        high = piece.astype(BF)
-        dpq.append(mm(flip, high) + mm(flip, (piece - high.astype(F32)).astype(BF)))
-    dpq = jnp.concatenate(dpq, axis=0)
-    dq_ref[...] = (dcq + dpq).astype(BF)
-    dcb_ref[...] = jnp.sum(dcq, axis=0, keepdims=True)
-    dpb_ref[...] = jnp.sum(dpq, axis=0, keepdims=True)
-
-
-def attend_forward(key_bias, content_bias, position_bias, query, keys, values, places):
-    rows, width = query.shape
-    count = keys.shape[0]
-    heads = width // HD
-    row_spec = pl.BlockSpec((rows, HD), lambda h: (0, h))
-    key_spec = pl.BlockSpec((count, HD), lambda h: (0, h))
-    vec_spec = pl.BlockSpec((1, HD), lambda h: (0, h))
-    return pl.pallas_call(
-        attend_forward_kernel,
-        grid=(heads,),
-        in_specs=[pl.BlockSpec((1, count), lambda h: (0, 0)), vec_spec, vec_spec, row_spec, key_spec, key_spec, key_spec],
-        out_specs=[row_spec, pl.BlockSpec((1, rows, count), lambda h: (h, 0, 0))],
-        out_shape=[
-            jax.ShapeDtypeStruct((rows, width), BF),
-            jax.ShapeDtypeStruct((heads, rows, count), BF),
-        ],
-        scratch_shapes=[pltpu.VMEM((rows, count), F32), pltpu.VMEM((rows, count), F32)],
-        compiler_params=pltpu.CompilerParams(vmem_limit_bytes=48 * MIB),
-        cost_estimate=pl.CostEstimate(
-            flops=6 * rows * count * width, bytes_accessed=2 * heads * rows * count, transcendentals=heads * rows * count
-        ),
-        name="attend_forward",
-    )(key_bias, content_bias, position_bias, query, keys, values, places)
-
-
-def attend_backward(content_bias, position_bias, query, keys, values, places, probs, d_out):
-    rows, width = query.shape
-    count = keys.shape[0]
-    heads = width // HD
-    row_spec = pl.BlockSpec((rows, HD), lambda h: (0, h))
-    key_spec = pl.BlockSpec((count, HD), lambda h: (0, h))
-    vec_spec = pl.BlockSpec((1, HD), lambda h: (0, h))
-    p_spec = pl.BlockSpec((1, rows, count), lambda h: (h, 0, 0))
-    return pl.pallas_call(
-        attend_backward_kernel,
-        grid=(heads,),
-        in_specs=[vec_spec, vec_spec, row_spec, key_spec, key_spec, key_spec, p_spec, row_spec],
-        out_specs=[row_spec, vec_spec, vec_spec, key_spec, key_spec, key_spec],
-        out_shape=[
-            jax.ShapeDtypeStruct((rows, width), BF),
-            jax.ShapeDtypeStruct((1, width), F32),
-            jax.ShapeDtypeStruct((1, width), F32),
-            jax.ShapeDtypeStruct((count, width), BF),
-            jax.ShapeDtypeStruct((count, width), BF),
-            jax.ShapeDtypeStruct((count, width), BF),
-        ],
-        scratch_shapes=[
-            pltpu.VMEM((rows, count), F32),
-            pltpu.VMEM((rows, count), BF),
-            pltpu.VMEM((rows, count), BF),
-        ],
-        compiler_params=pltpu.CompilerParams(vmem_limit_bytes=48 * MIB),
-        cost_estimate=pl.CostEstimate(
-            flops=12 * rows * count * width, bytes_accessed=2 * heads * rows * count, transcendentals=0
-        ),
-        name="attend_backward",
-    )(content_bias, position_bias, query, keys, values, places, probs, d_out)
 
 
 MESH = pl.DeviceIdType.MESH
@@ -408,17 +273,6 @@
                 continue
             ref = vec_up if name == "ub" else vec
             ref[target : target + 1, slot * size : (slot + 1) * size] = small_f[slot * 8 + row : slot * 8 + row + 1, at : at + size]
-
-
-def gather_dense_kernel(count, *refs):
-    place = Place(count)
-    place.barrier()
-    units = []
-    for i in range(3):
-        units += block_units(refs[i], refs[3 + i], count, (0, 2, 1)[i])
-    gather = Gather(place, units, *refs[6:])
-    for step in gather.steps():
-        step()
 
 
 def gather_semaphores(count, units):
@@ -475,28 +329,12 @@
     return full
 
 
-def gather_dense(w):
-    count = lax.axis_size("seq")
-    names = ("up", "down", "o")
-    any_spec = pl.BlockSpec(memory_space=pl.ANY)
-    outs = pl.pallas_call(
-        functools.partial(gather_dense_kernel, count),
-        in_specs=[any_spec] * 3,
-        out_specs=[any_spec] * 3,
-        out_shape=[jax.ShapeDtypeStruct((w[n].shape[0] * 2 * count, w[n].shape[1]), BF) for n in names],
-        scratch_shapes=gather_semaphores(count, sum(len(halves(w[n].shape[0])) for n in names)),
-        compiler_params=pltpu.CompilerParams(collective_id=3, has_side_effects=True, vmem_limit_bytes=16 * MIB),
-        name="gather_dense",
-    )(*[w[n] for n in names])
-    return dict(zip(names, outs))
-
-
 class Scatter:
-    def __init__(self, place, view, order, mine, core, first, second, line, local_sem, send_sem, recv_sem):
+    def __init__(self, place, view, order, sums, own, first, second, line, local_sem, send_sem, recv_sem):
         self.place, self.view = place, view
         self.by_y = order[0] == "y"
         self.late = order[2] == "z"
-        self.mine, self.core, self.first, self.second, self.line = mine, core, first, second, line
+        self.sums, self.own, self.first, self.second, self.line = sums, own, first, second, line
         self.local_sem, self.send_sem, self.recv_sem = local_sem, send_sem, recv_sem
         self.f, self.g = (place.h, place.b) if self.by_y else (place.b, place.h)
         self.flips = (YFLIP, XFLIP) if self.by_y else (XFLIP, YFLIP)
@@ -519,17 +357,17 @@
         )
 
     def core_copy(self, i):
-        return self.remote(self.core.at[i], self.core.at[i], CORE, i, i)
+        return self.remote(self.sums.at[i], self.sums.at[i], CORE, i, i)
 
     def first_copy(self, g, a):
         n = self.place.n
         to = g * n + a
-        return self.remote(self.mine.at[self.index(1 - self.f, g, a)], self.first.at[to], self.flips[0], 4 * n + to, 4 * n + to)
+        return self.remote(self.sums.at[self.index(1 - self.f, g, a)], self.first.at[to], self.flips[0], 4 * n + to, 4 * n + to)
 
     def second_copy(self, a):
         n = self.place.n
         to = a if self.late else 0
-        return self.remote(self.mine.at[self.index(self.f, 1 - self.g, a)], self.second.at[to], self.flips[1], 6 * n + to, 6 * n + to)
+        return self.remote(self.sums.at[self.index(self.f, 1 - self.g, a)], self.second.at[to], self.flips[1], 6 * n + to, 6 * n + to)
 
     def line_at(self, g, at):
         return at if self.late else g * (self.place.n + 1) + at
@@ -538,35 +376,54 @@
         n = self.place.n
         to = self.line_at(g, a if kind == UP else jnp.where(a == self.place.a - 1, n, a))
         sent = 7 * n + (a if self.late else g * n + a)
-        return self.remote(self.mine.at[self.index(self.f, g, a)], self.line.at[to], kind, sent, 7 * n + to)
+        return self.remote(self.sums.at[self.index(self.f, g, a)], self.line.at[to], kind, sent, 7 * n + to)
 
     def line_wait(self, at):
         n = self.place.n
         self.remote(self.line.at[at], self.line.at[at], CORE, 7 * n, 7 * n + at).wait_recv()
 
-    def start(self, f, g, a):
-        p = self.place
-        i = self.index(f, g, a)
-        for source, target in self.view(*self.slot(f, g, a, 1 - p.c), self.core.at[i]):
-            self.remote(source, target, CORE, i, i).start()
-        for source, target in self.view(*self.slot(f, g, a, p.c), self.mine.at[i]):
-            pltpu.make_async_copy(source, target, self.local_sem.at[i]).start()
-
-    def gather(self, f, g, a, more=()):
-        i = self.index(f, g, a)
-        pltpu.make_async_copy(self.mine.at[i], self.mine.at[i], self.local_sem.at[i]).wait()
-        self.core_copy(i).wait_recv()
-        return i, [(self.core, i), *more]
+    def piece(self, part, i):
+        return (self.f if part >= 2 else 1 - self.f, self.g if part % 2 else 1 - self.g, self.place.along(i))
+
+    def trade(self, part, i):
+        f, g, a = self.piece(part, i)
+        at = self.index(f, g, a)
+        source = self.view(*self.slot(f, g, a, 1 - self.place.c))
+        self.remote(source, self.sums.at[at], CORE, at, at).start()
+
+    def load(self, part, i):
+        source = self.view(*self.slot(*self.piece(part, i), self.place.c))
+        return pltpu.make_async_copy(source, self.own.at[i % 4], self.local_sem.at[i % 4])
+
+    def absorb(self, part, i):
+        n = self.place.n
+        f, g, a = self.piece(part, i)
+        at = self.index(f, g, a)
+        self.load(part, i).wait()
+        self.core_copy(at).wait_recv()
+        self.add(at, [(self.own, i % 4)])
+
+        @pl.when(i + 4 < n)
+        def _():
+            self.load(part, i + 4).start()
+
+        if part < 3:
+            @pl.when(i + 4 >= n)
+            def _():
+                self.load(part + 1, i + 4 - n).start()
+
+        if part < 2:
+            self.first_copy(g, a).start()
 
     def after_first(self, g, a):
         self.first_copy(g, a).wait_recv()
-        return self.gather(self.f, g, a, [(self.first, g * self.place.n + a)])
+        return self.index(self.f, g, a), [(self.first, g * self.place.n + a)]
 
     def add(self, i, refs):
-        total = self.mine[i].astype(F32)
+        total = self.sums[i].astype(F32)
         for ref, at in refs:
             total = total + ref[at].astype(F32)
-        self.mine[i] = total.astype(self.mine.dtype)
+        self.sums[i] = total.astype(BF)
 
     def add_line(self, i, g):
         p = self.place
@@ -575,10 +432,6 @@
             def _(at=self.line_at(g, at)):
                 self.line_wait(at)
                 self.add(i, [(self.line, at)])
-
-    def flip_first(self, g, a):
-        self.add(*self.gather(1 - self.f, g, a))
-        self.first_copy(g, a).start()
 
     def flip_second(self, a):
         i, refs = self.after_first(1 - self.g, a)
@@ -617,7 +470,7 @@
         self.second_copy(p.a).wait_recv()
         self.add(i, refs + [(self.second, to)])
         self.add_line(i, self.g)
-        store(self.mine[i].astype(F32))
+        store(self.sums[i].astype(F32))
         repeat(4 * n, lambda i: self.core_copy(i).wait_send())
         repeat(2 * n, lambda i: self.first_copy(i // n, i % n).wait_send())
         if self.late:
@@ -640,8 +493,8 @@
     late = order[2] == "z"
     lines = n + 1 if late else 2 * n + 2
     return [
-        *[pltpu.VMEM((k, *shape), BF) for k in (4 * n, 4 * n, 2 * n, n if late else 1, lines)],
-        pltpu.SemaphoreType.DMA((4 * n,)),
+        *[pltpu.VMEM((k, *shape), BF) for k in (4 * n, 4, 2 * n, n if late else 1, lines)],
+        pltpu.SemaphoreType.DMA((4,)),
         pltpu.SemaphoreType.DMA((9 * n,)),
         pltpu.SemaphoreType.DMA((7 * n + lines,)),
     ]
@@ -655,15 +508,15 @@
 
 
 def block_pairs(ref, rows, at, size, count):
-    def view(h, s, target):
-        return [(ref.at[pl.ds(pl.multiple_of((h * count + s) * rows + at, size), size)], target)]
+    def view(h, s):
+        return ref.at[pl.ds(pl.multiple_of((h * count + s) * rows + at, size), size)]
 
     return view
 
 
 def square_pairs(ref, r, w):
-    def view(h, s, target):
-        return [(ref.at[pl.ds(pl.multiple_of(s * r, r), r), pl.ds(pl.multiple_of(h * w, w), w)], target)]
+    def view(h, s):
+        return ref.at[pl.ds(pl.multiple_of(s * r, r), r), pl.ds(pl.multiple_of(h * w, w), w)]
 
     return view
 
@@ -681,18 +534,14 @@
         return one
 
     def begin():
-        repeat(n, each(lambda u, i: u.start(1 - u.f, 1 - u.g, place.along(i))))
-        repeat(n, each(lambda u, i: u.start(1 - u.f, u.g, place.along(i))))
-        repeat(n, each(lambda u, i: u.start(u.f, 1 - u.g, place.along(i))))
-        repeat(n, each(lambda u, i: u.start(u.f, u.g, place.along(i))))
+        for part in range(4):
+            repeat(n, each(lambda u, i, part=part: u.trade(part, i)))
+            if part == 0:
+                repeat(4, each(lambda u, i: u.load(0, i).start()))
         between(0)
 
-    def flips():
-        repeat(n, each(lambda u, i: u.flip_first(1 - u.g, place.along(i)), middle))
-        repeat(n, each(lambda u, i: u.flip_first(1 - u.g, place.along(i)), late))
-        repeat(n, each(lambda u, i: u.flip_first(u.g, place.along(i)), middle))
-        repeat(n, each(lambda u, i: u.flip_first(u.g, place.along(i)), late))
-        between(1)
+    def absorb(part):
+        repeat(n, each(lambda u, i: u.absorb(part, i), middle + late))
 
     def second(d):
         for u in middle:
@@ -705,6 +554,7 @@
             u.move(u.g, d)
 
     def fourth():
+        between(1)
         for u in late:
             u.flip_second(place.along(n - 1))
         for u in middle:
@@ -723,7 +573,8 @@
 
     far = range(n - 1, 0, -1)
     return (
-        [begin, flips]
+        [begin]
+        + [functools.partial(absorb, part) for part in range(4)]
         + [functools.partial(second, d) for d in far]
         + [functools.partial(third, d) for d in far]
         + [fourth]
@@ -756,14 +607,6 @@
         for at, size, order in block_scatters(rows, first):
             scratch += scatter_scratch(count, (size, width), order)
     return scratch
-
-
-def scatter_dense_kernel(count, up, down, o, up_out, down_out, o_out, *scratch):
-    place = Place(count)
-    place.barrier()
-    units, stores = scatter_dense_units(place, count, (up, down, o), (up_out, down_out, o_out), scratch)
-    for step in scatter_steps(place, units, stores):
-        step()
 
 
 def scatter_attention_kernel(
@@ -837,22 +680,6 @@
 
     for step in scatter_steps(place, units, stores, between):
         step()
-
-
-def scatter_dense(g):
-    count = lax.axis_size("seq")
-    names = ("up", "down", "o")
-    shapes = [(g[n].shape[0] // (2 * count), g[n].shape[1]) for n in names]
-    outs = pl.pallas_call(
-        functools.partial(scatter_dense_kernel, count),
-        in_specs=[pl.BlockSpec(memory_space=pl.ANY)] * 3,
-        out_specs=[pl.BlockSpec(memory_space=pltpu.VMEM)] * 3,
-        out_shape=[jax.ShapeDtypeStruct(shape, F32) for shape in shapes],
-        scratch_shapes=scatter_dense_scratch(count, shapes),
-        compiler_params=pltpu.CompilerParams(collective_id=1, has_side_effects=True, vmem_limit_bytes=48 * MIB),
-        name="scatter_dense",
-    )(*[g[n] for n in names])
-    return dict(zip(names, outs))
 
 
 VECTORS = ("cb", "pb", "sb", "ob", "g1", "s1", "db", "g2", "s2")
@@ -894,6 +721,279 @@
     return final
 
 
+def spread_steps(steps, points):
+    out = [[] for _ in range(points)]
+    for i, step in enumerate(steps):
+        out[i * points // len(steps)].append(step)
+    return out
+
+
+def attend_forward_kernel(
+    count, bias_ref, cb_ref, pb_ref, in_ref, table_ref, wq_ref, wk_ref, wv_ref, wp_ref, up, down, o,
+    out_ref, p_ref, cq_ref, pq_ref, k_ref, v_ref, pl_ref, up_f, down_f, o_f,
+    s_scr, x_scr, *sems,
+):
+    turn, turns = pl.program_id(0), pl.num_programs(0)
+    place = Place(count)
+    units = []
+    for shard, full, first in ((up, up_f, 0), (down, down_f, 2), (o, o_f, 1)):
+        units += block_units(shard, full, count, first)
+    gather = Gather(place, units, *sems)
+    first, *steps, last = gather.steps()
+    heads = cq_ref.shape[1] // HD
+    points = 2 + heads
+    plan = spread_steps(steps, turns * points - 1)
+
+    def point(k):
+        for t in range(turns):
+            chosen = plan[t * points + k - 1] if t or k else [place.barrier, first]
+            if chosen:
+                @pl.when(turn == t)
+                def _(chosen=chosen):
+                    for step in chosen:
+                        step()
+
+    rows, keys = cq_ref.shape[0], k_ref.shape[0]
+    scale = HD ** (-0.5)
+    point(0)
+    query = mm(in_ref[2 * rows :], wq_ref[...])
+    cq_ref[...] = ((query + cb_ref[...]) * scale).astype(BF)
+    pq_ref[...] = ((query + pb_ref[...]) * scale).astype(BF)
+
+    def project(source, weight, target):
+        def one(i):
+            here = pl.ds(pl.multiple_of(i * rows, rows), rows)
+            target[here] = mm(source[here], weight[...]).astype(BF)
+
+        repeat(keys // rows, one)
+
+    project(in_ref, wk_ref, k_ref)
+    point(1)
+    project(in_ref, wv_ref, v_ref)
+    project(table_ref, wp_ref, pl_ref)
+    step = 32
+    for head in range(heads):
+        point(2 + head)
+        cols = slice(head * HD, (head + 1) * HD)
+        s_scr[...] = mm_nt(cq_ref[:, cols], k_ref[:, cols])
+        x_scr[...] = mm_nt(pq_ref[:, cols], pl_ref[:, cols])
+        for start in range(0, rows, step):
+            here = slice(start, start + step)
+            located = pltpu.roll(x_scr[here], (start + keys - rows + 1) % keys, 1, stride=1, stride_axis=0)
+            scores = s_scr[here] + located + bias_ref[...]
+            early, own = scores[:, : 2 * rows], scores[:, 2 * rows :]
+            row = start + lax.broadcasted_iota(jnp.int32, own.shape, 0)
+            col = lax.broadcasted_iota(jnp.int32, own.shape, 1)
+            own = jnp.where(col <= row, own, -1e30)
+            top = jnp.maximum(jnp.max(early, axis=1, keepdims=True), jnp.max(own, axis=1, keepdims=True))
+            early, own = jnp.exp(early - top), jnp.exp(own - top)
+            total = jnp.sum(early, axis=1, keepdims=True) + jnp.sum(own, axis=1, keepdims=True)
+            share = 1.0 / total
+            p_ref[head, here, : 2 * rows] = (early * share).astype(BF)
+            p_ref[head, here, 2 * rows :] = (own * share).astype(BF)
+        out_ref[:, cols] = mm(p_ref[head], v_ref[:, cols]).astype(BF)
+
+    @pl.when(turn == turns - 1)
+    def _():
+        last()
+
+
+def attend_forward(key_bias, content_bias, position_bias, keys_in, table, w, shards):
+    count = lax.axis_size("seq")
+    keys, width = keys_in.shape
+    rows = keys // 3
+    pair = 2 * HD
+    names = ("up", "down", "o")
+
+    def whole(shape):
+        return pl.BlockSpec(shape, lambda t: (0,) * len(shape), pipeline_mode=pl.Buffered(1))
+
+    def columns(height):
+        return pl.BlockSpec((height, pair), lambda t: (0, t))
+
+    any_spec = pl.BlockSpec(memory_space=pl.ANY)
+    outs = pl.pallas_call(
+        functools.partial(attend_forward_kernel, count),
+        grid=(width // pair,),
+        in_specs=[whole((1, keys)), columns(1), columns(1), whole((keys, width)), whole((keys, width))]
+        + [columns(width)] * 4
+        + [any_spec] * 3,
+        out_specs=[columns(rows), pl.BlockSpec((2, rows, keys), lambda t: (t, 0, 0))]
+        + [columns(rows)] * 2
+        + [columns(keys)] * 3
+        + [any_spec] * 3,
+        out_shape=[
+            jax.ShapeDtypeStruct((rows, width), BF),
+            jax.ShapeDtypeStruct((width // HD, rows, keys), BF),
+            *[jax.ShapeDtypeStruct((rows, width), BF)] * 2,
+            *[jax.ShapeDtypeStruct((keys, width), BF)] * 3,
+            *[jax.ShapeDtypeStruct((shards[n].shape[0] * 2 * count, width), BF) for n in names],
+        ],
+        scratch_shapes=[
+            pltpu.VMEM((rows, keys), F32),
+            pltpu.VMEM((rows, keys), F32),
+            *gather_semaphores(count, sum(len(halves(shards[n].shape[0])) for n in names)),
+        ],
+        compiler_params=pltpu.CompilerParams(collective_id=3, has_side_effects=True, vmem_limit_bytes=56 * MIB),
+        name="attend_forward",
+    )(key_bias, content_bias, position_bias, keys_in, table, w["q"], w["k"], w["v"], w["p"], *[shards[n] for n in names])
+    return outs[:7], dict(zip(names, outs[7:]))
+
+
+BACKWARD_PLAN = (
+    (0, 0), (0, 1), (0, 2), (1, 1), (1, 2),
+    (3, 3), (4, 1), (4, 2),
+    (5, 0), (5, 1), (5, 2),
+    (5, 3),
+    (6, 1), (7, 0), (7, 2),
+)
+
+
+def attend_backward_kernel(
+    count, cq_ref, pq_ref, k_ref, v_ref, pl_ref, p_ref, do_ref, in_t_ref, table_t_ref, wq_ref, wk_ref, wv_ref, up, down, o,
+    dcb_ref, dpb_ref, gq_ref, gk_ref, gv_ref, gp_ref, up_out, down_out, o_out, dsq_out, dmem_out, dcur_out,
+    dp_scr, ds_scr, dq_scr, dk_scr, dv_scr, dpl_scr, total, out_sem, *scratch,
+):
+    head, heads = pl.program_id(0), pl.num_programs(0)
+    place = Place(count)
+    units, stores = scatter_dense_units(place, count, (up, down, o), (up_out, down_out, o_out), scratch)
+    first, *steps, last = scatter_steps(place, units, stores)
+    plan = {at: [] for at in BACKWARD_PLAN}
+    plan[BACKWARD_PLAN[0]] = [place.barrier, first]
+    for i, step in enumerate(steps):
+        plan[BACKWARD_PLAN[min(1 + i * (len(BACKWARD_PLAN) - 1) // len(steps), len(BACKWARD_PLAN) - 1)]].append(step)
+
+    def point(k):
+        for (t, at), chosen in plan.items():
+            if at == k:
+                @pl.when(head == t)
+                def _(chosen=chosen):
+                    for step in chosen:
+                        step()
+
+    rows, keys = cq_ref.shape[0], k_ref.shape[0]
+    scale = HD ** (-0.5)
+    block = 128
+    flip = (
+        lax.broadcasted_iota(jnp.int32, (block, block), 0)
+        + lax.broadcasted_iota(jnp.int32, (block, block), 1)
+        == block - 1
+    ).astype(BF)
+    point(0)
+    dp_scr[...] = mm_nt(do_ref[...], v_ref[...])
+    step = 32
+    for start in range(0, rows, step):
+        here = slice(start, start + step)
+        prob = p_ref[0, here].astype(F32)
+        dprob = dp_scr[here]
+        delta = jnp.sum(prob * dprob, axis=1, keepdims=True)
+        ds_scr[here] = (prob * (dprob - delta)).astype(BF)
+    point(1)
+    side = head % 2
+    dv_scr[side] = mm_tn(do_ref[...], p_ref[0]).T.astype(BF)
+    dk_scr[side] = mm_tn(cq_ref[...], ds_scr[...]).T.astype(BF)
+    dcq = mm(ds_scr[...], k_ref[...]) * scale
+    flipped = []
+    for start in range(0, rows, block):
+        here = slice(start, start + block)
+        dp_scr[here] = mm(flip, ds_scr[here])
+        flipped.append(mm(flip, pq_ref[here]).astype(BF))
+        ds_scr[here] = pltpu.roll(dp_scr[here], rows - block - start, 1, stride=1, stride_axis=0).astype(BF)
+    dpl_scr[side] = mm_tn(jnp.concatenate(flipped, axis=0), ds_scr[...]).T.astype(BF)
+    dpq_flipped = mm(ds_scr[...], pl_ref[...]) * scale
+    dpq = []
+    for start in range(0, rows, block):
+        piece = dpq_flipped[start : start + block]
+        high = piece.astype(BF)
+        dpq.append(mm(flip, high) + mm(flip, (piece - high.astype(F32)).astype(BF)))
+    dpq = jnp.concatenate(dpq, axis=0)
+    dq_scr[side] = (dcq + dpq).astype(BF)
+    dcb_ref[...] = jnp.sum(dcq, axis=0, keepdims=True)
+    dpb_ref[...] = jnp.sum(dpq, axis=0, keepdims=True)
+    point(2)
+
+    @pl.when(side == 1)
+    def _():
+        dq, dk, dv, dpl = (jnp.concatenate([ref[0], ref[1]], axis=1) for ref in (dq_scr, dk_scr, dv_scr, dpl_scr))
+        gk_ref[...] = mm(in_t_ref[...], dk).astype(BF)
+        gv_ref[...] = mm(in_t_ref[...], dv).astype(BF)
+        gp_ref[...] = mm(table_t_ref[...], dpl).astype(BF)
+        gq_ref[...] = mm(in_t_ref[:, 2 * rows :], dq).astype(BF)
+        point(3)
+
+        @pl.when(head == 1)
+        def _():
+            total[...] = jnp.zeros_like(total)
+
+        for start in range(0, keys, rows):
+            here = slice(start, start + rows)
+            more = mm_nt(dk[here], wk_ref[...]) + mm_nt(dv[here], wv_ref[...])
+            if start == 2 * rows:
+                more = more + mm_nt(dq, wq_ref[...])
+            total[here] += more
+
+    @pl.when(head == heads - 1)
+    def _():
+        width = total.shape[1]
+        own = pltpu.make_async_copy(total.at[pl.ds(2 * rows, rows)], dcur_out, out_sem.at[0])
+        own.start()
+        for i, out in enumerate((dsq_out, dmem_out)):
+            ds_scr[:, :width] = total[i * rows : (i + 1) * rows].astype(BF)
+            copy = pltpu.make_async_copy(ds_scr.at[:, pl.ds(0, width)], out, out_sem.at[1 + i])
+            copy.start()
+            copy.wait()
+        own.wait()
+        last()
+
+
+def attend_backward(saved, probs, d_out, inputs_t, table_t, w, dense):
+    count = lax.axis_size("seq")
+    rows, width = d_out.shape
+    keys = inputs_t.shape[1]
+    heads = width // HD
+    names = ("up", "down", "o")
+    shapes = [(dense[n].shape[0] // (2 * count), width) for n in names]
+
+    def whole(shape):
+        return pl.BlockSpec(shape, lambda h: (0,) * len(shape), pipeline_mode=pl.Buffered(1))
+
+    def columns(height):
+        return pl.BlockSpec((height, HD), lambda h: (0, h))
+
+    pair = pl.BlockSpec((width, 2 * HD), lambda h: (0, h // 2))
+    any_spec = pl.BlockSpec(memory_space=pl.ANY)
+    vmem = pl.BlockSpec(memory_space=pltpu.VMEM)
+    outs = pl.pallas_call(
+        functools.partial(attend_backward_kernel, count),
+        grid=(heads,),
+        in_specs=[columns(rows)] * 2
+        + [columns(keys)] * 3
+        + [pl.BlockSpec((1, rows, keys), lambda h: (h, 0, 0)), columns(rows), whole((width, keys)), whole((width, keys))]
+        + [pair] * 3
+        + [any_spec] * 3,
+        out_specs=[columns(1)] * 2 + [pair] * 4 + [vmem] * 3 + [any_spec] * 3,
+        out_shape=[
+            *[jax.ShapeDtypeStruct((1, width), F32)] * 2,
+            *[jax.ShapeDtypeStruct((width, width), BF)] * 4,
+            *[jax.ShapeDtypeStruct(shape, F32) for shape in shapes],
+            *[jax.ShapeDtypeStruct((rows, width), BF)] * 2,
+            jax.ShapeDtypeStruct((rows, width), F32),
+        ],
+        scratch_shapes=[
+            pltpu.VMEM((rows, keys), F32),
+            pltpu.VMEM((rows, keys), BF),
+            pltpu.VMEM((2, rows, HD), BF),
+            *[pltpu.VMEM((2, keys, HD), BF)] * 3,
+            pltpu.VMEM((keys, width), F32),
+            pltpu.SemaphoreType.DMA((3,)),
+            *scatter_dense_scratch(count, shapes),
+        ],
+        compiler_params=pltpu.CompilerParams(collective_id=1, has_side_effects=True, vmem_limit_bytes=62 * MIB),
+        name="attend_backward",
+    )(*saved, probs, d_out, inputs_t, table_t, w["q"], w["k"], w["v"], *[dense[n] for n in names])
+    return outs[:2], outs[2:6], dict(zip(names, outs[6:9])), outs[9:]
+
+
 def normalize(values):
     centre = values - jnp.mean(values, axis=-1, keepdims=True)
     spread = jnp.mean(centre * centre, axis=-1, keepdims=True)
@@ -953,7 +1053,6 @@
             db=down_bias, g2=second_gain, s2=second_shift, sb=squeeze_bias,
     )
     w = gather_attention(shards)
-    w.update(gather_dense(shards))
     cb, pb, ob, g1, s1, ub, db, g2, s2, sb = (
         w[n] for n in ("cb", "pb", "ob", "g1", "s1", "ub", "db", "g2", "s2", "sb")
     )
@@ -977,12 +1076,9 @@
     valid = jnp.concatenate([history_ok, row_ids < window[3], row_ids < window[4]])
     key_bias = jnp.where(valid, 0.0, -1e30).astype(F32)[None]
 
-    query = mm(x, w["q"])
-    keys = mm(keys_in, w["k"], out=BF)
-    values = mm(keys_in, w["v"], out=BF)
-    table = jnp.asarray(table_rows(width, 3 * rows))
-    places = mm(table, w["p"], out=BF)
-    attended, probs = attend_forward(key_bias, cb, pb, query, keys, values, places)
+    table = table_rows(width, 3 * rows)
+    (attended, probs, *saved), dense = attend_forward(key_bias, cb, pb, keys_in, jnp.asarray(table), w, shards)
+    w.update(dense)
 
     blended = x.astype(F32) + mm(attended, w["o"]) + ob
     unit1, scale1 = normalize(blended)
@@ -1013,22 +1109,19 @@
     grads["o"] = mm_tn(attended, dblended_b, BF)
     dattended = mm_nt(dblended_b, w["o"], BF)
 
-    dq, dcb, dpb, dk, dv, dplaces = attend_backward(cb, pb, query, keys, values, places, probs, dattended)
+    (dcb, dpb), squares, final, (dsqueezed, dmemory, dcurrent) = attend_backward(
+        saved, probs, dattended, keys_in.T, jnp.asarray(np.ascontiguousarray(table.T)), w, grads
+    )
+    grads.update(zip(("q", "k", "v", "p"), squares))
     grads["cb"] = dcb[0]
     grads["pb"] = dpb[0]
-    dkeys_in = mm_nt(dk, w["k"]) + mm_nt(dv, w["v"])
-    dsqueezed = dkeys_in[:rows].astype(BF)
     grads["sb"] = jnp.sum(dsqueezed.astype(F32), axis=0)
     dmade = mm_tn(collect, dsqueezed, BF)
     returned = jnp.concatenate(
         [shifted(dmade[role * pad : (role + 1) * pad], "seq", role - 4) for role in range(3)], axis=0
     )
-    from_next = shifted(dkeys_in[rows : 2 * rows].astype(BF), "seq", -1)
-    grads["q"] = mm_tn(x, dq, BF)
-    grads["k"] = mm_tn(keys_in, dk, BF)
-    grads["v"] = mm_tn(keys_in, dv, BF)
-    grads["p"] = mm_tn(table, dplaces, BF)
-    dx = dblended + mm_nt(dq, w["q"]) + dkeys_in[2 * rows :] + from_next.astype(F32)
+    from_next = shifted(dmemory, "seq", -1)
+    dx = dblended + dcurrent + from_next.astype(F32)
     dmasked = jnp.zeros((rows, width), F32)
     sq_grads = []
     for tap in range(3):
@@ -1038,7 +1131,7 @@
     grads["sq"] = jnp.concatenate(sq_grads, axis=1)
     dx = dx + jnp.where(kept, dmasked, 0.0)
 
-    final = {**scatter_dense(grads), **scatter_attention(grads)}
+    final.update(scatter_attention(grads))
     return (
         exchange_rows(outputs, head),
         exchange_rows(dx.astype(BF), head),

time: 677 us -> 612 us (0.904)
  matrix products: 176 us -> 113 us
  Pallas kernels: 414 us -> 381 us
  waiting for transfers between devices: 4.69 us -> 24.3 us
  local copies, waits for them, and re-layouts: 33.4 us -> 42.1 us
    dot_general x42 -> x31, matrix products: 176 us -> 113 us  [mm(): lax.dot_general(left, right, (contract, ((), ())), preferred_element_type...]
    pallas_call x4 -> x2, Pallas kernels: 248 us -> 215 us  [the longest x1 114 us: attend_backward(): pl.pallas_call(functools.partial(attend_backward_kernel, count), grid=(he...]
    ppermute x8, waiting for transfers between devices: 0.02 us -> 20.3 us  [shifted(): return lax.ppermute(array, axis, pairs)]
    unnamed x164 -> x141, local copies, waits for them, and re-layouts: 25.9 us -> 25.3 us
  transfers between devices with their start and end apart: 10 -> 10, of which waited for: 1 -> 4; matrix products, arithmetic and copies ran while one was open for 15% -> 10% of each run, Pallas kernels for 52% -> 27%
where the time goes in v3:
time: 612 us; the launch traced here: 605 us
  Pallas kernels  381 us (62%)
  matrix products  113 us (18%)
  local copies, waits for them, and re-layouts  42.1 us (7%)
  waiting for transfers between devices  24.3 us (4%)
  other arithmetic  23.6 us (4%)
  starting transfers between devices  19.7 us (3%)
    pallas_call x1, Pallas kernels, attend_backward(): pl.pallas_call(functools.partial(attend_backward_kernel, count), grid=(he...  114 us
    dot_general x31, matrix products, mm(): lax.dot_general(left, right, (contract, ((), ())), preferred_element_type...  113 us
    pallas_call x1, Pallas kernels, attend_forward(): pl.pallas_call(functools.partial(attend_forward_kernel, count), grid=(wid...  101 us
    pallas_call x1, Pallas kernels, scatter_attention(): pl.pallas_call(functools.partial(scatter_attention_kernel, count), in_spe...  95.1 us
    pallas_call x1, Pallas kernels, gather_attention(): pl.pallas_call(functools.partial(gather_attention_kernel, count, layout),...  71 us
    unnamed x141, local copies, waits for them, and re-layouts  25.3 us
    ppermute x8, waiting for transfers between devices, shifted(): return lax.ppermute(array, axis, pairs)  20.3 us
    ppermute x8, starting transfers between devices, shifted(): return lax.ppermute(array, axis, pairs)  17.3 us
  transfers between devices with their start and end apart: 10, of which 4 were waited for; matrix products, arithmetic and copies ran while one was open for 10% of the time, Pallas kernels for 27%

profile of v3, /device:TPU:6, one launch (start us, length us, event | category | flops | bytes accessed | tf_op | source)
XLA Modules:
  0.0 605.1 jit_solution(9982484796779088605)
XLA Ops:
  0.7 2.7 constant_dynamic-slice_fusion.1
  7.7 71.0 %gather_attention.1 = (bf16[1024,1024]{1,0:T(8,128)(2,1)S(1)}, bf16[1024,1024]{1,0:T(8,128)(2,1)S(1)}, bf16[1024,1024]{1,0:T(8,128)(2,1)S(1)}, bf16[1024,1024]{1...) custom-call(bf16[64,512]{1,0:T(8,128)(2,1)S(1)} %copy-done.9, ...), custom_call_target="tpu_custom_call" | custom-call | tf_op jit(solution)/shard_map/gather_attention/pallas_call | solution.py:309
  84.1 2.6 copy-done.13
  87.4 5.1 fusion.18
  92.5 5.1 fusion.22
  97.7 5.2 add_convert_fusion
  103.7 4.4 collective-permute-start.1
  110.0 2.7 collective-permute-start
  119.5 10.3 %collective-permute-done = bf16[176,1024]{1,0:T(8,128)(2,1)} collective-permute-done((bf16[176,1024]{1,0:T(8,128)(2,1)}, bf16[176,1024]{1,0:T(8,128)(2,1)}, u32[]{:S(2)}, u32[]{:S(2)}) %collective-permute-start) | collective-permute-done | bytes 360480 | tf_op jit(solution)/shard_map/ppermute | solution.py:33
  133.4 3.8 fusion.60
  137.3 4.6 copy.59.in_ref
  141.9 101.0 %attend_forward.1 = (bf16[512,1024]{1,0:T(8,128)(2,1)}, bf16[8,512,1536]{2,1,0:T(8,128)(2,1)}, bf16[512,1024]{1,0:T(8,128)(2,1)}, bf16[512,1024]{1,0:T(8,128)(2,...) custom-call(f32[1,1536]{1,0:T(1,128)} %add_select_fusion.bias_ref, ...), custom_call_target="tpu_custom_call" | custom-call | tf_op jit(solution)/shard_map/attend_forward/pallas_call | solution.py:815
  242.9 3.4 fusion.69
  247.3 7.8 %fusion.71 = f32[512,4096]{1,0:T(8,128)} fusion(bf16[4096,1024]{1,0:T(8,128)(2,1)S(1)} %bitcast.229, f32[512,1024]{0,1:T(8,128)S(1)} %get-tuple-element.159, f32[1024]{0:T(1024)S(1)} %bitcast.220, f32[1024]{0:T(1024)S(1)} %bitcast.210, f32[512]{0:T(512)S(1)} %add_rsqrt_fusion.1, f32[512]{0:T(512)S(1)} %broadcast_multiply_fusion.5), kind=kOutput, calls=%fused_computation.141 | convolution fusion | flops 4297588736 | bytes 18886656 | tf_op jit(solution)/shard_map/dot_general | solution.py:19
  255.1 11.1 %fusion.70 = (f32[512]{0:T(512)S(1)}, f32[512,1024]{0,1:T(8,128)S(1)}) fusion(f32[1024]{0:T(1024)S(1)} %bitcast.223, bf16[4096,1024]{1,0:T(8,128)(2,1)} %get-tuple-element.66, f32[512,4096]{1,0:T(8,128)} %fusion.71, f32[4096]{0:T(1024)S(1)} %bitcast.196, f32[1024]{0:T(1024)S(1)} %bitcast.221, f32[1024]{0:T(1024)S(1)} %bitcast.211, ...), kind=kOutput, calls=%fused_computation.140 | convolution fusion | flops 4320656896 | bytes 21006336 | tf_op jit(solution)/shard_map/dot_general | solution.py:19
  267.1 15.3 %convert_reduce_fusion = (f32[4096]{0:T(1024)S(1)}, bf16[512,4096]{1,0:T(8,128)(2,1)}) fusion(f32[512,4096]{1,0:T(8,128)} %fusion.71, f32[4096]{0:T(1024)S(1)} %bitcast.197, bf16[4096,1024]{1,0:T(8,128)(2,1)} %get-tuple-element.66, f32[512]{0:T(512)S(1)} %broadcast_multiply_fusion.2, f32[512,1024]{0,1:T(8,128)S(1)} %get-tuple-element.161, ...), kind=kOutput, calls=%fused_computation.9 | convolution fusion | flops 4345819136 | bytes 24162304 | tf_op jit(solution)/shard_map/dot_general | solution.py:19
  282.4 15.3 %convolution_convert_fusion.down = bf16[4096,1024]{1,0:T(8,128)(2,1)} fusion(f32[512,4096]{1,0:T(8,128)} %fusion.71, f32[4096]{0:T(1024)S(1)} %bitcast.198, bf16[1,1,512,1024]{2,3,1,0:T(8,128)(2,1)S(1)} %copy.87, f32[512,1024]{0,1:T(8,128)S(1)} %get-tuple-element.161, f32[512]{0:T(512)S(1)} %broadcast_multiply_fusion.2, ...), kind=kOutput, calls=%fused_computation.11 | convolution fusion | flops 4324851712 | bytes 19951616 | tf_op jit(solution)/shard_map/dot_general | solution.py:19
  297.8 11.6 %multiply_reduce_fusion = (f32[1024]{0:T(1024)S(1)}, f32[512]{0:T(512)S(1)}, f32[512]{0:T(512)S(1)}, f32[1024]{0:T(1024)S(1)}, f32[512,1024]{0,1:T(8,128)}) fusion(f32[512,1024]{0,1:T(8,128)S(1)} %get-tuple-element.159, f32[512]{0:T(512)S(1)} %add_rsqrt_fusion.1, f32[512]{0:T(512)S(1)} %broadcast_multiply_fusion.5, f32[1024]{0:T(1024)S(1)} %bitcast.212, ...), kind=kOutput, calls=%fused_computation.31 | convolution fusion | flops 4304401408 | bytes 19955712 | tf_op jit(solution)/shard_map/dot_general | solution.py:19
  309.3 2.5 fusion.64
  311.9 2.3 convolution_convert_fusion.10.do_ref
  314.2 2.7 convolution_convert_fusion.5.o
  316.9 7.6 %convolution_convert_fusion.1.up = bf16[4096,1024]{1,0:T(8,128)(2,1)} fusion(bf16[512,4096]{1,0:T(8,128)(2,1)S(1)} %copy-done.59, f32[512,1024]{0,1:T(8,128)S(1)} %get-tuple-element.159, f32[1024]{0:T(1024)S(1)} %bitcast.222, f32[1024]{0:T(1024)S(1)} %bitcast.214, f32[512]{0:T(512)S(1)} %add_rsqrt_fusion.1, f32[512]{0:T(512)S(1)} %broadcast_multiply_fusion.5), kind=kOutput, calls=%fused_computation.12 | convolution fusion | flops 4301783040 | bytes 14692352 | tf_op jit(solution)/shard_map/dot_general | solution.py:19
  324.5 113.6 %attend_backward.1 = (f32[1,1024]{1,0:T(1,128)}, f32[1,1024]{1,0:T(1,128)}, bf16[1024,1024]{1,0:T(8,128)(2,1)}, bf16[1024,1024]{1,0:T(8,128)(2,1)}, bf16[1024,10...) custom-call(bf16[512,1024]{1,0:T(8,128)(2,1)} %get-tuple-element.67., ...), custom_call_target="tpu_custom_call" | custom-call | tf_op jit(solution)/shard_map/attend_backward/pallas_call | solution.py:966
  438.1 2.3 fusion.28
  451.7 2.0 copy.74
  453.8 2.3 copy.65
  461.7 9.5 %collective-permute-done.8 = bf16[176,1024]{1,0:T(8,128)(2,1)S(1)} collective-permute-done((bf16[176,1024]{1,0:T(8,128)(2,1)}, bf16[176,1024]{1,0:T(8,128)(2,1)S(1)}, u32[]{:S(2)}, u32[]{:S(2)}) %collective-permute-start.8) | collective-permute-done | bytes 360480 | tf_op jit(solution)/shard_map/ppermute | solution.py:33
  480.5 3.3 pad_maximum_fusion.sq
  484.9 95.1 %scatter_attention.1 = (f32[64,512]{1,0:T(8,128)S(1)}, f32[64,512]{1,0:T(8,128)S(1)}, f32[64,512]{1,0:T(8,128)S(1)}, f32[64,512]{1,0:T(8,128)S(1)}, f32[32,3072]...) custom-call(bf16[1024,1024]{1,0:T(8,128)(2,1)S(1)} %copy-done.5, bf16[1024,1024]{1,0:T(8,128)(2,1)S(1)} %copy-done.6, ...), custom_call_target="tpu_custom_call" | custom-call | tf_op jit(solution)/shard_map/scatter_attention/pallas_call | solution.py:702
  584.3 2.8 add_convert_fusion.5
  587.2 2.4 collective-permute-start.9
  592.8 4.0 collective-permute-done.9
  (217 shorter events, 67.5 us)
Async XLA Ops:
  0.7 5.4 copy-start
  3.5 83.9 %copy-start.57 = (bf16[512,528]{1,0:T(8,128)(2,1)S(1)}, bf16[512,528]{1,0:T(8,128)(2,1)}, u32[]{:S(2)}) copy-start(bf16[512,528]{1,0:T(8,128)(2,1)} %constant.90.clone) | copy-start | bytes 1622020
  4.1 238.8 %copy-start.18 = (bf16[1,1,512,1024]{2,3,1,0:T(8,128)(2,1)}, bf16[1,1,512,1024]{2,3,1,0:T(8,128)(2,1)S(1)}, u32[]{:S(2)}) copy-start(bf16[1,1,512,1024]{2,3,1,0:T(8,128)(2,1)S(1)} %copy.54) | copy-start | bytes 3145732
  4.1 129.3 %collective-permute-start.3 = (bf16[512,1024]{0,1:T(8,128)(2,1)S(1)}, bf16[512,1024]{0,1:T(8,128)(2,1)}, u32[]{:S(2)}, u32[]{:S(2)}) collective-permute-start(bf16[512,1024]{0,1:T(8,128)(2,1)S(1)} %bitcast.200), channel_id=1, source_target_pairs={{0,1},{1,2},{2,3},{3,4},{4,5},{5,6},{6,7},{7,8},{8,9},{9,10},{10,1... | collective-permute-start | bytes 3145736 | tf_op jit(solution)/shard_map/ppermute | solution.py:33
  87.4 5.1 copy-start.56
  92.5 5.2 copy-start.55
  92.5 5.2 copy-start.58
  102.8 10.5 %copy-start.40 = (s32[512]{0:T(512)S(1)}, s32[512]{0:T(512)}, u32[]{:S(2)}) copy-start(s32[512]{0:T(512)} %constant.92.clone) | copy-start | bytes 6148
  102.9 10.5 %copy-start.44 = (pred[512]{0:T(512)(128)(4,1)S(1)}, pred[512]{0:T(512)(128)(4,1)}, u32[]{:S(2)}) copy-start(pred[512]{0:T(512)(128)(4,1)} %constant.122) | copy-start | bytes 1540
  102.9 10.5 %copy-start.45 = (pred[512]{0:T(512)(128)(4,1)S(1)}, pred[512]{0:T(512)(128)(4,1)}, u32[]{:S(2)}) copy-start(pred[512]{0:T(512)(128)(4,1)} %constant.121) | copy-start | bytes 1540
  103.7 27.7 %collective-permute-start.1 = (bf16[176,1024]{1,0:T(8,128)(2,1)S(1)}, bf16[176,1024]{1,0:T(8,128)(2,1)}, u32[]{:S(2)}, u32[]{:S(2)}) collective-permute-start(bf16[176,1024]{1,0:T(8,128)(2,1)S(1)} %get-tuple-element.132), channel_id=1, source_target_pairs={{0,3},{1,4},{2,5},{3,6},{4,7},{5,8},{6,9},{7,10},{8,11},{9,12},{10... | collective-permute-start | bytes 1081352 | tf_op jit(solution)/shard_map/ppermute | solution.py:33
  108.1 24.8 %collective-permute-start.2 = (bf16[176,1024]{1,0:T(8,128)(2,1)S(1)}, bf16[176,1024]{1,0:T(8,128)(2,1)S(1)}, u32[]{:S(2)}, u32[]{:S(2)}) collective-permute-start(bf16[176,1024]{1,0:T(8,128)(2,1)S(1)} %get-tuple-element.133), channel_id=1, source_target_pairs={{0,2},{1,3},{2,4},{3,5},{4,6},{5,7},{6,8},{7,9},{8,10},{9,11},{10,... | collective-permute-start | bytes 1081352 | tf_op jit(solution)/shard_map/ppermute | solution.py:33
  110.0 19.8 %collective-permute-start = (bf16[176,1024]{1,0:T(8,128)(2,1)}, bf16[176,1024]{1,0:T(8,128)(2,1)}, u32[]{:S(2)}, u32[]{:S(2)}) collective-permute-start(bf16[176,1024]{1,0:T(8,128)(2,1)} %get-tuple-element.134), channel_id=1, source_target_pairs={{0,4},{1,5},{2,6},{3,7},{4,8},{5,9},{6,10},{7,11},{8,12},{9,13},{1... | collective-permute-start | bytes 1081352 | tf_op jit(solution)/shard_map/ppermute | solution.py:33
  119.5 13.4 %copy-start.34 = (bf16[512,176]{1,0:T(8,128)(2,1)S(1)}, bf16[512,176]{1,0:T(8,128)(2,1)}, u32[]{:S(2)}) copy-start(bf16[512,176]{1,0:T(8,128)(2,1)} %constant.107) | copy-start | bytes 540676
  266.2 31.5 %copy-start.14 = (f32[512,1024]{0,1:T(8,128)}, f32[512,1024]{0,1:T(8,128)S(1)}, u32[]{:S(2)}) copy-start(f32[512,1024]{0,1:T(8,128)S(1)} %get-tuple-element.161) | copy-start | bytes 6291460
  441.5 16.7 %collective-permute-start.6 = (bf16[176,1024]{1,0:T(8,128)(2,1)}, bf16[176,1024]{1,0:T(8,128)(2,1)S(1)}, u32[]{:S(2)}, u32[]{:S(2)}) collective-permute-start(bf16[176,1024]{1,0:T(8,128)(2,1)} %get-tuple-element.131), channel_id=1, source_target_pairs={{4,0},{5,1},{6,2},{7,3},{8,4},{9,5},{10,6},{11,7},{12,8},{13,9},{1... | collective-permute-start | bytes 1081352 | tf_op jit(solution)/shard_map/ppermute | solution.py:33
  444.3 15.9 %collective-permute-start.7 = (bf16[176,1024]{1,0:T(8,128)(2,1)}, bf16[176,1024]{1,0:T(8,128)(2,1)S(1)}, u32[]{:S(2)}, u32[]{:S(2)}) collective-permute-start(bf16[176,1024]{1,0:T(8,128)(2,1)} %get-tuple-element.129), channel_id=1, source_target_pairs={{3,0},{4,1},{5,2},{6,3},{7,4},{8,5},{9,6},{10,7},{11,8},{12,9},{13... | collective-permute-start | bytes 1081352 | tf_op jit(solution)/shard_map/ppermute | solution.py:33
  447.9 142.3 %collective-permute-start.4 = (bf16[256,1024]{0,1:T(8,128)(2,1)}, bf16[256,1024]{0,1:T(8,128)(2,1)}, u32[]{:S(2)}, u32[]{:S(2)}) collective-permute-start(bf16[256,1024]{0,1:T(8,128)(2,1)} %constant_dynamic-slice_fusion.2), channel_id=1, source_target_pairs={{0,16},{16,0},{1,17},{17,1},{2,18},{18,2},{3,19},{19,3},{4,20},{20... | collective-permute-start | bytes 1572872 | tf_op jit(solution)/shard_map/ppermute | solution.py:1026
  449.8 8.2 %copy-start.38 = (f32[1,1024]{1,0:T(1,128)S(1)}, f32[1,1024]{1,0:T(1,128)}, u32[]{:S(2)}) copy-start(f32[1,1024]{1,0:T(1,128)} %get-tuple-element.80) | copy-start | bytes 12292
  449.8 8.2 %copy-start.39 = (f32[1,1024]{1,0:T(1,128)S(1)}, f32[1,1024]{1,0:T(1,128)}, u32[]{:S(2)}) copy-start(f32[1,1024]{1,0:T(1,128)} %get-tuple-element.81) | copy-start | bytes 12292
  449.8 21.3 %collective-permute-start.8 = (bf16[176,1024]{1,0:T(8,128)(2,1)}, bf16[176,1024]{1,0:T(8,128)(2,1)S(1)}, u32[]{:S(2)}, u32[]{:S(2)}) collective-permute-start(bf16[176,1024]{1,0:T(8,128)(2,1)} %get-tuple-element.130), channel_id=1, source_target_pairs={{2,0},{3,1},{4,2},{5,3},{6,4},{7,5},{8,6},{9,7},{10,8},{11,9},{12,... | collective-permute-start | bytes 1081352 | tf_op jit(solution)/shard_map/ppermute | solution.py:33
  456.1 128.0 %collective-permute-start.5 = (bf16[512,1024]{0,1:T(8,128)(2,1)}, bf16[512,1024]{0,1:T(8,128)(2,1)}, u32[]{:S(2)}, u32[]{:S(2)}) collective-permute-start(bf16[512,1024]{0,1:T(8,128)(2,1)} %copy.65), channel_id=1, source_target_pairs={{1,0},{2,1},{3,2},{4,3},{5,4},{6,5},{7,6},{8,7},{9,8},{10,9},{11,1... | collective-permute-start | bytes 3145736 | tf_op jit(solution)/shard_map/ppermute | solution.py:33
  458.1 13.0 %copy-start.24 = (bf16[512,176]{1,0:T(8,128)(2,1)S(1)}, bf16[512,176]{1,0:T(8,128)(2,1)}, u32[]{:S(2)}) copy-start(bf16[512,176]{1,0:T(8,128)(2,1)} %constant.108) | copy-start | bytes 540676
  461.6 10.0 %copy-start.19 = (bf16[1,1,512,1024]{2,3,1,0:T(8,128)(2,1)S(1)}, bf16[1,1,512,1024]{2,3,1,0:T(8,128)(2,1)}, u32[]{:S(2)}) copy-start(bf16[1,1,512,1024]{2,3,1,0:T(8,128)(2,1)} %copy-done.18) | copy-start | bytes 3145732
  480.5 99.5 %slice-start = ((s8[6291456]{0:T(1024)(128)(4,1)}), s8[4194304]{0:T(1024)(128)(4,1)S(1)}, s32[]{:S(2)}) async-start(s8[6291456]{0:T(1024)(128)(4,1)} %bitcast.194), calls=%async_computation | async-start | bytes 8388608
  484.9 95.1 %slice-start.1 = ((s8[6291456]{0:T(1024)(128)(4,1)}), s8[2097152]{0:T(1024)(128)(4,1)S(1)}, s32[]{:S(2)}) async-start(s8[6291456]{0:T(1024)(128)(4,1)} %bitcast.194), calls=%async_computation.1 | async-start | bytes 4194304
  484.9 95.1 %copy-start.26 = (bf16[1024,512]{1,0:T(8,128)(2,1)S(1)}, bf16[1024,512]{1,0:T(8,128)(2,1)}, u32[]{:S(2)}) copy-start(bf16[1024,512]{1,0:T(8,128)(2,1)} %copy-done.25) | copy-start | bytes 3145732
  584.1 6.1 %copy-start.23 = (bf16[512,1024]{0,1:T(8,128)(2,1)S(1)}, bf16[512,1024]{0,1:T(8,128)(2,1)}, u32[]{:S(2)}) copy-start(bf16[512,1024]{0,1:T(8,128)(2,1)} %copy-done.22) | copy-start | bytes 3145732
  587.2 9.7 %collective-permute-start.9 = (bf16[256,1024]{0,1:T(8,128)(2,1)S(1)}, bf16[256,1024]{0,1:T(8,128)(2,1)}, u32[]{:S(2)}, u32[]{:S(2)}) collective-permute-start(bf16[256,1024]{0,1:T(8,128)(2,1)S(1)} %constant_dynamic-slice_fusion), channel_id=1, source_target_pairs={{0,16},{16,0},{1,17},{17,1},{2,18},{18,2},{3,19},{19,3},{4,20},{20... | collective-permute-start | bytes 1572872 | tf_op jit(solution)/shard_map/ppermute | solution.py:1026
  591.4 5.4 copy-start.21
  598.2 5.1 copy-start.33
  598.2 6.7 %copy-start.1 = (s32[2,16]{1,0:T(2,128)S(1)}, s32[2,16]{1,0:T(2,128)}, u32[]{:S(2)}) copy-start(s32[2,16]{1,0:T(2,128)} %param.35) | copy-start | bytes 388
  (42 other events, 124.0 us)

commit v4 on v3

--- a/solution.py
+++ b/solution.py
@@ -25,12 +25,6 @@
 
 def mm_tn(left, right, out=F32):
     return mm(left, right, ((0,), (0,)), out)
-
-
-def shifted(array, axis, by):
-    count = lax.axis_size(axis)
-    pairs = [(i, i + by) for i in range(count) if 0 <= i + by < count]
-    return lax.ppermute(array, axis, pairs)
 
 
 def table_rows(width, count):
@@ -100,14 +94,29 @@
             return pl.when(self.a > 0)
         return lambda run: run()
 
-    def barrier(self):
+    def far(self):
+        s, count = self.s, self.count
+        for by, other in ((1, self.c == 1), (-1, self.c == 0), (2, self.b == 1), (-2, self.b == 0), (3, None), (-3, None)):
+            inside = self.inside(by)
+            yield by, inside if other is None else jnp.logical_and(inside, other)
+
+    def inside(self, by):
+        return self.s + by < self.count if by > 0 else self.s + by >= 0
+
+    def barrier(self, shifts=False):
         barrier = pltpu.get_barrier_semaphore()
         for kind in range(5):
             @self.when(kind)
             def _(kind=kind):
                 pl.semaphore_signal(barrier, inc=1, device_id=self.neighbour(kind), device_id_type=MESH)
-        ends = jnp.where(self.a == 0, 1, 0) + jnp.where(self.a == self.n - 1, 1, 0)
-        pl.semaphore_wait(barrier, 5 - ends)
+        peers = 5 - jnp.where(self.a == 0, 1, 0) - jnp.where(self.a == self.n - 1, 1, 0)
+        if shifts:
+            for by, there in self.far():
+                @pl.when(there)
+                def _(by=by):
+                    pl.semaphore_signal(barrier, inc=1, device_id=(self.h, self.s + by), device_id_type=MESH)
+                peers = peers + jnp.where(there, 1, 0)
+        pl.semaphore_wait(barrier, peers)
 
     def along(self, i):
         return (self.a + self.n // 2 + i) % self.n
@@ -182,10 +191,8 @@
         for u in range(len(self.units)):
             for kind in self.onward(u, 0, 0, 0):
                 self.send(u, kind, p.h, p.s, True, wait)
-        for u in range(len(self.units)):
-            if wait:
-                self.local(u).wait()
-            else:
+        if not wait:
+            for u in range(len(self.units)):
                 self.local(u).start()
 
     def pass_on(self, entry, wait=False):
@@ -207,7 +214,7 @@
         else:
             run()
 
-    def finish(self):
+    def arrived(self):
         p = self.place
 
         def core(i):
@@ -216,9 +223,17 @@
                 self.copy(u, CORE, h, p.seq_of(a, b, 1 - p.c)).wait_recv()
 
         repeat(4 * p.n, core)
+        for u in range(len(self.units)):
+            self.local(u).wait()
+
+    def sent(self):
         self.begin(True)
         for entry in self.sources():
             self.pass_on(entry, True)
+
+    def finish(self):
+        self.arrived()
+        self.sent()
 
     def steps(self):
         return [self.begin] + [functools.partial(self.pass_on, entry) for entry in self.sources()] + [self.finish]
@@ -251,28 +266,112 @@
     return (shard, full, view, order)
 
 
-def gather_attention_kernel(count, small_names, *refs):
-    shards, (vec, vec_up) = refs[:6], refs[11:13]
-    fulls = refs[6:11] + refs[13:14]
+def open_kernel(
+    count, small_names, q, k, v, p, sq, small, x, masked, taps_t, collect, biased,
+    q_f, k_f, v_f, p_f, sq_f, vec, vec_up, squeezed, memory,
+    small_f, taps_scr, masked_scr, sq_scr, grouped, made, made_low, arriving, load_sem, row_send, row_recv, *sems,
+):
     place = Place(count)
-    place.barrier()
-    units = [square_unit(shards[i], fulls[i], GATHER_ORDERS[i]) for i in range(4)]
-    units += block_units(shards[4], fulls[4], count, 0)
-    small, small_f = shards[5], fulls[5]
+    place.barrier(True)
+    rows, width = masked_scr.shape
+    pad = made.shape[0] // 3
 
     def small_view(ref, h, s):
         return ref.at[pl.ds(pl.multiple_of((h * count + s) * 8, 8), 8)]
 
-    units.append((small, small_f, small_view, "zxy"))
-    gather = Gather(place, units, *refs[14:])
-    for step in gather.steps():
-        step()
+    early = Gather(place, block_units(sq, sq_f, count, 0) + [(small, small_f, small_view, "zxy")], *sems[:3])
+    late = Gather(
+        place, [square_unit(*pair, GATHER_ORDERS[i]) for i, pair in enumerate(((q, q_f), (k, k_f), (v, v_f), (p, p_f)))], *sems[3:]
+    )
+
+    def rows_copy(i):
+        by = 4 - i if i < 3 else 1
+        here = pl.ds(i * pad, pad)
+        return pltpu.make_async_remote_copy(
+            src_ref=made_low.at[here] if i < 3 else x,
+            dst_ref=arriving.at[here] if i < 3 else memory,
+            send_sem=row_send.at[i],
+            recv_sem=row_recv.at[i],
+            device_id=(place.h, place.s + by),
+            device_id_type=MESH,
+        )
+
+    def send_rows(i, wait=False):
+        @pl.when(place.inside(4 - i if i < 3 else 1))
+        def _():
+            if wait:
+                rows_copy(i).wait_send()
+            else:
+                rows_copy(i).start()
+
+    def take_rows(i):
+        @pl.when(place.inside(i - 4 if i < 3 else -1))
+        def _():
+            rows_copy(i).wait_recv()
+
+    loads = [
+        pltpu.make_async_copy(source, target, load_sem.at[i])
+        for i, (source, target) in enumerate(((taps_t, taps_scr), (masked, masked_scr), (sq_f, sq_scr)))
+    ]
+    early.begin()
+    loads[0].start()
+    loads[1].start()
+    send_rows(3)
+    late.begin()
+
+    @pl.when(place.s == 0)
+    def _():
+        made_low[...] = jnp.zeros_like(made_low)
+        blank = pltpu.make_async_copy(made_low.at[pl.ds(0, rows)], memory, load_sem.at[3])
+        blank.start()
+        blank.wait()
+
+    for i in range(3):
+        @pl.when(jnp.logical_not(place.inside(i - 4)))
+        def _(i=i):
+            arriving[i * pad : (i + 1) * pad] = jnp.zeros((pad, width), BF)
+
+    entries = early.sources()
+
+    def passed(gather, depth):
+        for entry in entries:
+            if entry[0] + entry[2] + entry[3] == depth:
+                gather.pass_on(entry)
+
+    deepest = place.n + 1
+    loads[0].wait()
+    loads[1].wait()
+    passed(early, 1)
+    for tap in range(3):
+        grouped[tap] = mm(taps_scr[tap], masked_scr[...]).astype(BF)
+    for depth in range(2, deepest + 1):
+        passed(early, depth)
+        if depth > 2:
+            passed(late, depth - 2)
+    early.arrived()
+    loads[2].start()
     for slot in range(2 * count):
         for name, row, at, size, target in small_names:
             if size * 2 * count > vec.shape[1] * (4 if name == "ub" else 1) and slot >= count:
                 continue
             ref = vec_up if name == "ub" else vec
             ref[target : target + 1, slot * size : (slot + 1) * size] = small_f[slot * 8 + row : slot * 8 + row + 1, at : at + size]
+    loads[2].wait()
+    made[...] = mm_nt(grouped[0], sq_scr[:, :width]) + biased[...] * vec[2:3]
+    passed(late, deepest - 1)
+    made[...] += mm_nt(grouped[1], sq_scr[:, width : 2 * width])
+    passed(late, deepest)
+    made_low[...] = (made[...] + mm_nt(grouped[2], sq_scr[:, 2 * width :])).astype(BF)
+    for i in range(3):
+        send_rows(i)
+    late.arrived()
+    for i in range(4):
+        take_rows(i)
+    squeezed[...] = mm(collect[...], arriving[...]).astype(BF)
+    for i in range(4):
+        send_rows(i, True)
+    early.sent()
+    late.sent()
 
 
 def gather_semaphores(count, units):
@@ -293,10 +392,11 @@
     return names
 
 
-def gather_attention(w):
+def open_layer(w, x, masked, layout):
+    pad, taps, collect, biased = layout
     count = lax.axis_size("seq")
     both, seq = w["cb"].shape[0], w["ob"].shape[0]
-    width = both * 2 * count
+    rows, width = x.shape
     layout = small_layout(both, seq)
     lines = [[] for _ in range(8)]
     for name, row, at, size, target in layout:
@@ -304,29 +404,41 @@
     lines = [jnp.concatenate(parts) if parts else jnp.zeros((128,), F32) for parts in lines]
     small = jnp.stack([jnp.pad(line, (0, 128 - line.shape[0])) for line in lines])
     names = ("q", "k", "v", "p", "sq")
+    tall = w["sq"].shape[1]
     any_spec = pl.BlockSpec(memory_space=pl.ANY)
     vmem_spec = pl.BlockSpec(memory_space=pltpu.VMEM)
     outs = pl.pallas_call(
-        functools.partial(gather_attention_kernel, count, layout),
-        in_specs=[any_spec] * 6,
-        out_specs=[any_spec] * 5 + [vmem_spec] * 2,
+        functools.partial(open_kernel, count, layout),
+        in_specs=[any_spec] * 9 + [vmem_spec] * 2,
+        out_specs=[any_spec] * 5 + [vmem_spec] * 3 + [any_spec],
         out_shape=[
             *[jax.ShapeDtypeStruct((width, width), BF) for _ in range(4)],
-            jax.ShapeDtypeStruct((width, w["sq"].shape[1]), BF),
+            jax.ShapeDtypeStruct((width, tall), BF),
             jax.ShapeDtypeStruct((16, width), F32),
             jax.ShapeDtypeStruct((1, 4 * width), F32),
+            jax.ShapeDtypeStruct((rows, width), BF),
+            jax.ShapeDtypeStruct((rows, width), BF),
         ],
         scratch_shapes=[
             pltpu.VMEM((8 * 2 * count, 128), F32),
-            *gather_semaphores(count, 5 + len(halves(w["sq"].shape[0]))),
+            pltpu.VMEM((3, 3 * pad, rows), BF),
+            pltpu.VMEM((rows, width), BF),
+            pltpu.VMEM((width, tall), BF),
+            pltpu.VMEM((3, 3 * pad, width), BF),
+            pltpu.VMEM((3 * pad, width), F32),
+            pltpu.VMEM((3 * pad, width), BF),
+            pltpu.VMEM((3 * pad, width), BF),
+            pltpu.SemaphoreType.DMA((4,)),
+            pltpu.SemaphoreType.DMA((4,)),
+            pltpu.SemaphoreType.DMA((4,)),
+            *gather_semaphores(count, 1 + len(halves(w["sq"].shape[0]))),
+            *gather_semaphores(count, 4),
         ],
-        compiler_params=pltpu.CompilerParams(collective_id=0, has_side_effects=True, vmem_limit_bytes=16 * MIB),
-        name="gather_attention",
-    )(*[w[n] for n in names], small)
-    full = dict(zip(names, outs))
-    for name, row, at, size, target in layout:
-        full[name] = outs[6] if name == "ub" else outs[5][target : target + 1]
-    return full
+        compiler_params=pltpu.CompilerParams(collective_id=0, has_side_effects=True, vmem_limit_bytes=48 * MIB),
+        name="open_layer",
+    )(*[w[n] for n in names], small, x, masked, jnp.asarray(np.ascontiguousarray(taps.transpose(0, 2, 1))), jnp.asarray(collect), jnp.asarray(biased))
+    full = dict(zip(names, outs), vec=outs[5], ub=outs[6])
+    return full, outs[7], outs[8]
 
 
 class Scatter:
@@ -609,22 +721,65 @@
     return scratch
 
 
-def scatter_attention_kernel(
-    count, q, k, v, p, sq, vec, q_out, k_out, v_out, p_out, sq_out, vec_out, ub_out, sums, parts, vec_send, vec_recv, *scratch
+def close_kernel(
+    count, gq, gk, gv, gp, sqw, dcb, dpb, vec, dub, dsq, dmem, dcur, dbl, masked, kept, taps, collect_t, outputs,
+    q_out, k_out, v_out, p_out, sq_out, vec_out, ub_out, dx_out, rows_out,
+    sums, parts, vec_send, vec_recv, dmade, returned, from_next, gsq, sq_scr, dcur_scr, dbl_scr, masked_scr, taps_scr,
+    spread, dmasked, load_sem, row_send, row_recv, out_sem, out_send, out_recv, *scratch,
 ):
     place = Place(count)
-    place.barrier()
+    place.barrier(True)
     r, w = q_out.shape
+    rows, width = dsq.shape
+    half = rows // 2
+    pad = dmade.shape[0] // 3
     units, stores = [], []
-    for ref, out, order in zip((q, k, v, p), (q_out, k_out, v_out, p_out), SCATTER_ORDERS):
+    for ref, out, order in zip((gq, gk, gv, gp), (q_out, k_out, v_out, p_out), SCATTER_ORDERS):
         units.append(Scatter(place, square_pairs(ref, r, w), order, *scratch[:8]))
         stores.append(store_into(out))
         scratch = scratch[8:]
-    rows = sq_out.shape[0]
-    for at, size, order in block_scatters(rows, 0):
-        units.append(Scatter(place, block_pairs(sq, rows, at, size, count), order, *scratch[:8]))
-        stores.append(store_into(sq_out.at[pl.ds(at, size)]))
+    low_units, low_stores = [], []
+    wide = sq_out.shape[0]
+    for at, size, order in block_scatters(wide, 0):
+        low_units.append(Scatter(place, block_pairs(gsq, wide, at, size, count), order, *scratch[:8]))
+        low_stores.append(store_into(sq_out.at[pl.ds(at, size)]))
         scratch = scratch[8:]
+
+    loads = [
+        pltpu.make_async_copy(source, target, load_sem.at[i])
+        for i, (source, target) in enumerate(
+            ((taps, taps_scr), (masked, masked_scr), (sqw, sq_scr), (dcur, dcur_scr), (dbl, dbl_scr))
+        )
+    ]
+
+    def rows_copy(i):
+        by = i - 4 if i < 3 else -1
+        here = pl.ds(i * pad, pad)
+        return pltpu.make_async_remote_copy(
+            src_ref=dmade.at[here] if i < 3 else dmem,
+            dst_ref=returned.at[here] if i < 3 else from_next,
+            send_sem=row_send.at[i],
+            recv_sem=row_recv.at[i],
+            device_id=(place.h, place.s + by),
+            device_id_type=MESH,
+        )
+
+    def exchange(i, source, target, wait=False):
+        own = pltpu.make_async_copy(source.at[pl.ds(pl.multiple_of(place.h * half, half), half)], target.at[place.h], out_sem.at[i])
+        other = pltpu.make_async_remote_copy(
+            src_ref=source.at[pl.ds(pl.multiple_of((1 - place.h) * half, half), half)],
+            dst_ref=target.at[place.h],
+            send_sem=out_send.at[i],
+            recv_sem=out_recv.at[i],
+            device_id=place.neighbour(YFLIP),
+            device_id_type=MESH,
+        )
+        if wait:
+            own.wait()
+            other.wait()
+        else:
+            other.start()
+            own.start()
 
     def vec_copy(kind):
         return pltpu.make_async_remote_copy(
@@ -639,7 +794,12 @@
     def between(at):
         kinds = (CORE, XFLIP, YFLIP)
         if at == 0:
-            sums[CORE] = vec[...]
+            sums[CORE, 0:16] = vec[...]
+            sums[CORE, 0:1] = dcb[...]
+            sums[CORE, 1:2] = dpb[...]
+            sums[CORE, 2:3] = jnp.sum(dsq[...].astype(F32), axis=0, keepdims=True)
+            for i in range(4):
+                sums[CORE, 12 + i : 13 + i] = dub[:, i * width : (i + 1) * width]
             vec_copy(CORE).start()
         elif at < 3:
             vec_copy(kinds[at - 1]).wait_recv()
@@ -662,7 +822,6 @@
                     vec_copy(kind).start()
         else:
             total = sums[UP] + sums[DOWN] - (sums[YFLIP] + parts[YFLIP])
-            width = total.shape[1]
             both = vec_out.shape[1]
             k = place.h * count + place.s
             mine = pltpu.roll(total, lax.rem(width - k * both, width), 1)
@@ -678,47 +837,126 @@
                 def _(kind=kind):
                     vec_copy(kind).wait_send()
 
-    for step in scatter_steps(place, units, stores, between):
+    main = scatter_steps(place, units, stores, between)
+    low = scatter_steps(place, low_units, low_stores)
+    far = place.n - 1
+
+    for load in loads:
+        load.start()
+    dmade[...] = mm(collect_t[...], dsq[...]).astype(BF)
+    for i in range(4):
+        by = i - 4 if i < 3 else -1
+
+        @pl.when(place.inside(by))
+        def _(i=i):
+            rows_copy(i).start()
+
+        @pl.when(jnp.logical_not(place.inside(-by)))
+        def _(i=i):
+            if i < 3:
+                returned[i * pad : (i + 1) * pad] = jnp.zeros((pad, width), BF)
+            else:
+                from_next[...] = jnp.zeros_like(from_next)
+
+    exchange(0, outputs, rows_out)
+    for step in main[:5]:
         step()
-
-
-VECTORS = ("cb", "pb", "sb", "ob", "g1", "s1", "db", "g2", "s2")
-
-
-def scatter_attention(g):
+    for i in range(4):
+        @pl.when(place.inside(4 - i if i < 3 else 1))
+        def _(i=i):
+            rows_copy(i).wait_recv()
+    for load in loads:
+        load.wait()
+
+    def compressed(tap):
+        cols = slice(tap * width, (tap + 1) * width)
+        spread[...] = mm(taps_scr[tap], returned[...]).astype(BF)
+        more = mm(spread[...], sq_scr[:, cols])
+        if tap:
+            more = more + dmasked[...]
+        dmasked[...] = more
+        gsq[:, cols] = mm_tn(spread[...], masked_scr[...]).astype(BF)
+
+    compressed(0)
+    compressed(1)
+    for step in main[5 : 5 + far]:
+        step()
+    compressed(2)
+    low[0]()
+    spread[...] = (dbl_scr[...] + dcur_scr[...] + from_next[...].astype(F32) + kept[...] * dmasked[...]).astype(BF)
+    exchange(1, spread, dx_out)
+    for step in low[1:5]:
+        step()
+    for step in main[5 + far : 5 + 2 * far + 1]:
+        step()
+    for step in low[5 : 5 + far]:
+        step()
+    for step in main[6 + 2 * far : 6 + 3 * far]:
+        step()
+    for step in low[5 + far : 6 + 3 * far]:
+        step()
+    main[-1]()
+    low[-1]()
+    for i in range(4):
+        @pl.when(place.inside(i - 4 if i < 3 else -1))
+        def _(i=i):
+            rows_copy(i).wait_send()
+    exchange(0, outputs, rows_out, True)
+    exchange(1, spread, dx_out, True)
+
+
+def close_layer(g, w, layout, dsq, dmem, dcur, dbl, masked, kept, outputs):
+    pad, taps, collect, biased = layout
     count = lax.axis_size("seq")
-    width = g["q"].shape[0]
+    rows, width = dsq.shape
     both = width // (2 * count)
-    lines = [g[n].reshape(1, width) for n in VECTORS]
-    vec = jnp.concatenate(lines + [jnp.zeros((12 - len(lines), width), F32), g["ub"].reshape(-1, width)], axis=0)
     square = (width // count, width // 2)
-    narrow = (both, g["sq"].shape[1])
+    tall = w["sq"].shape[1]
     scratch = []
     for order in SCATTER_ORDERS:
         scratch += scatter_scratch(count, square, order)
     for at, size, order in block_scatters(both, 0):
-        scratch += scatter_scratch(count, (size, narrow[1]), order)
+        scratch += scatter_scratch(count, (size, tall), order)
     vmem = pl.BlockSpec(memory_space=pltpu.VMEM)
+    any_spec = pl.BlockSpec(memory_space=pl.ANY)
     outs = pl.pallas_call(
-        functools.partial(scatter_attention_kernel, count),
-        in_specs=[pl.BlockSpec(memory_space=pl.ANY)] * 5 + [vmem],
-        out_specs=[vmem] * 7,
+        functools.partial(close_kernel, count),
+        in_specs=[any_spec] * 5 + [vmem] * 5 + [any_spec] * 4 + [vmem] + [any_spec] + [vmem] + [any_spec],
+        out_specs=[vmem] * 7 + [any_spec] * 2,
         out_shape=[jax.ShapeDtypeStruct(square, F32)] * 4
-        + [jax.ShapeDtypeStruct(s, F32) for s in (narrow, (16, both), (1, 4 * both))],
+        + [jax.ShapeDtypeStruct(s, F32) for s in ((both, tall), (16, both), (1, 4 * both))]
+        + [jax.ShapeDtypeStruct((2, rows // 2, width), BF)] * 2,
         scratch_shapes=[
             pltpu.VMEM((5, 16, width), F32),
             pltpu.VMEM((5, 16, width), F32),
             pltpu.SemaphoreType.DMA((5,)),
             pltpu.SemaphoreType.DMA((5,)),
+            pltpu.VMEM((3 * pad, width), BF),
+            pltpu.VMEM((3 * pad, width), BF),
+            pltpu.VMEM((rows, width), BF),
+            pltpu.VMEM((width, tall), BF),
+            pltpu.VMEM((width, tall), BF),
+            pltpu.VMEM((rows, width), F32),
+            pltpu.VMEM((rows, width), F32),
+            pltpu.VMEM((rows, width), BF),
+            pltpu.VMEM((3, rows, 3 * pad), BF),
+            pltpu.VMEM((rows, width), BF),
+            pltpu.VMEM((rows, width), F32),
+            pltpu.SemaphoreType.DMA((5,)),
+            *[pltpu.SemaphoreType.DMA((4,))] * 2,
+            *[pltpu.SemaphoreType.DMA((2,))] * 3,
             *scratch,
         ],
-        compiler_params=pltpu.CompilerParams(collective_id=2, has_side_effects=True, vmem_limit_bytes=48 * MIB),
-        name="scatter_attention",
-    )(g["q"], g["k"], g["v"], g["p"], g["sq"], vec)
+        compiler_params=pltpu.CompilerParams(collective_id=2, has_side_effects=True, vmem_limit_bytes=60 * MIB),
+        name="close_layer",
+    )(
+        g["q"], g["k"], g["v"], g["p"], w["sq"], g["cb"], g["pb"], g["sums"], g["ub"],
+        dsq, dmem, dcur, dbl, masked, kept, jnp.asarray(taps), jnp.asarray(np.ascontiguousarray(collect.T)), outputs,
+    )
     final = dict(zip(("q", "k", "v", "p", "sq"), outs[:5]))
     final.update({n: outs[5][i] for i, n in enumerate(VECTORS)})
     final["ub"] = outs[6].reshape(4 * both)
-    return final
+    return final, outs[7], outs[8]
 
 
 def spread_steps(steps, points):
@@ -729,8 +967,8 @@
 
 
 def attend_forward_kernel(
-    count, bias_ref, cb_ref, pb_ref, in_ref, table_ref, wq_ref, wk_ref, wv_ref, wp_ref, up, down, o,
-    out_ref, p_ref, cq_ref, pq_ref, k_ref, v_ref, pl_ref, up_f, down_f, o_f,
+    count, bias_ref, vec_ref, in0_ref, in1_ref, in2_ref, table_ref, wq_ref, wk_ref, wv_ref, wp_ref, up, down, o,
+    out_ref, p_ref, cq_ref, pq_ref, k_ref, v_ref, pl_ref, in_t_ref, up_f, down_f, o_f,
     s_scr, x_scr, *sems,
 ):
     turn, turns = pl.program_id(0), pl.num_programs(0)
@@ -756,21 +994,21 @@
     rows, keys = cq_ref.shape[0], k_ref.shape[0]
     scale = HD ** (-0.5)
     point(0)
-    query = mm(in_ref[2 * rows :], wq_ref[...])
-    cq_ref[...] = ((query + cb_ref[...]) * scale).astype(BF)
-    pq_ref[...] = ((query + pb_ref[...]) * scale).astype(BF)
-
-    def project(source, weight, target):
-        def one(i):
-            here = pl.ds(pl.multiple_of(i * rows, rows), rows)
-            target[here] = mm(source[here], weight[...]).astype(BF)
-
-        repeat(keys // rows, one)
-
-    project(in_ref, wk_ref, k_ref)
+    sources = (in0_ref, in1_ref, in2_ref)
+    query = mm(in2_ref[...], wq_ref[...])
+    cq_ref[...] = ((query + vec_ref[0:1]) * scale).astype(BF)
+    pq_ref[...] = ((query + vec_ref[1:2]) * scale).astype(BF)
+    for i, source in enumerate(sources):
+        k_ref[i * rows : (i + 1) * rows] = mm(source[...], wk_ref[...]).astype(BF)
     point(1)
-    project(in_ref, wv_ref, v_ref)
-    project(table_ref, wp_ref, pl_ref)
+    for i, source in enumerate(sources):
+        v_ref[i * rows : (i + 1) * rows] = mm(source[...], wv_ref[...]).astype(BF)
+        here = slice(i * rows, (i + 1) * rows)
+        pl_ref[here] = mm(table_ref[here], wp_ref[...]).astype(BF)
+
+        @pl.when(turn == i)
+        def _(source=source, here=here):
+            in_t_ref[:, here] = source[...].T
     step = 32
     for head in range(heads):
         point(2 + head)
@@ -798,10 +1036,10 @@
         last()
 
 
-def attend_forward(key_bias, content_bias, position_bias, keys_in, table, w, shards):
+def attend_forward(key_bias, squeezed, memory, x, table, w, shards):
     count = lax.axis_size("seq")
-    keys, width = keys_in.shape
-    rows = keys // 3
+    rows, width = x.shape
+    keys = 3 * rows
     pair = 2 * HD
     names = ("up", "down", "o")
 
@@ -815,18 +1053,20 @@
     outs = pl.pallas_call(
         functools.partial(attend_forward_kernel, count),
         grid=(width // pair,),
-        in_specs=[whole((1, keys)), columns(1), columns(1), whole((keys, width)), whole((keys, width))]
+        in_specs=[whole((1, keys)), columns(16), *[whole((rows, width))] * 3, whole((keys, width))]
         + [columns(width)] * 4
         + [any_spec] * 3,
         out_specs=[columns(rows), pl.BlockSpec((2, rows, keys), lambda t: (t, 0, 0))]
         + [columns(rows)] * 2
         + [columns(keys)] * 3
+        + [pl.BlockSpec((width, keys), lambda t: (0, 0))]
         + [any_spec] * 3,
         out_shape=[
             jax.ShapeDtypeStruct((rows, width), BF),
             jax.ShapeDtypeStruct((width // HD, rows, keys), BF),
             *[jax.ShapeDtypeStruct((rows, width), BF)] * 2,
             *[jax.ShapeDtypeStruct((keys, width), BF)] * 3,
+            jax.ShapeDtypeStruct((width, keys), BF),
             *[jax.ShapeDtypeStruct((shards[n].shape[0] * 2 * count, width), BF) for n in names],
         ],
         scratch_shapes=[
@@ -836,8 +1076,8 @@
         ],
         compiler_params=pltpu.CompilerParams(collective_id=3, has_side_effects=True, vmem_limit_bytes=56 * MIB),
         name="attend_forward",
-    )(key_bias, content_bias, position_bias, keys_in, table, w["q"], w["k"], w["v"], w["p"], *[shards[n] for n in names])
-    return outs[:7], dict(zip(names, outs[7:]))
+    )(key_bias, w["vec"], squeezed, memory, x, table, w["q"], w["k"], w["v"], w["p"], *[shards[n] for n in names])
+    return outs[:8], dict(zip(names, outs[8:]))
 
 
 BACKWARD_PLAN = (
@@ -1012,21 +1252,145 @@
 
 def gelu_parts(u):
     root = np.float32(np.sqrt(2.0 / np.pi))
-    inner = root * (u + 0.044715 * u * u * u)
-    tanh = jnp.tanh(inner)
-    value = 0.5 * u * (1.0 + tanh)
-    slope = 0.5 * (1.0 + tanh) + 0.5 * u * (1.0 - tanh * tanh) * root * (1.0 + 3 * 0.044715 * u * u)
+    square = u * u
+    tanh = jnp.tanh(u * (root + (root * 0.044715) * square))
+    half = 0.5 * u
+    value = half + half * tanh
+    slope = 0.5 + 0.5 * tanh + half * (1.0 - tanh * tanh) * (root + (3 * 0.044715 * root) * square)
     return value, slope
 
 
-def exchange_rows(array, head):
-    half = array.shape[0] // 2
-    mine = lax.dynamic_slice_in_dim(array, head * half, half, 0)
-    theirs = lax.dynamic_slice_in_dim(array, (1 - head) * half, half, 0)
-    other = lax.ppermute(theirs, "head", [(0, 1), (1, 0)])
-    first = jnp.where(head == 0, mine, other)
-    second = jnp.where(head == 0, other, mine)
-    return jnp.stack([first, second])[:, None]
+VECTORS = ("cb", "pb", "sb", "ob", "g1", "s1", "db", "g2", "s2")
+
+
+def feed_kernel(
+    att_ref, x_ref, ct_ref, wo_ref, up_ref, down_ref, ub_ref, vec_ref,
+    out_ref, gup_ref, gdown_ref, go_ref, dub_ref, sums_ref, dbl_ref, datt_ref,
+    unit, scale, normed, acc, hidden, slope, dy, dy_low,
+):
+    turn = pl.program_id(0)
+    chunks = pl.num_programs(0) // 2
+    rows = x_ref.shape[0]
+    at = {name: slice(i, i + 1) for i, name in enumerate(VECTORS)}
+
+    def by_rows(run):
+        repeat(rows // 128, lambda k: run(pl.ds(pl.multiple_of(k * 128, 128), 128)))
+
+    def tally(name, values):
+        sums_ref[at[name]] += jnp.sum(values, axis=0, keepdims=True)
+
+    @pl.when(turn == 0)
+    def _():
+        sums_ref[...] = jnp.zeros_like(sums_ref)
+        acc[...] = mm(att_ref[...], wo_ref[...])
+
+        def first(here):
+            unit[here], scale[here] = normalize(x_ref[here].astype(F32) + acc[here] + vec_ref[at["ob"]])
+            normed[here] = (unit[here] * vec_ref[at["g1"]] + vec_ref[at["s1"]]).astype(BF)
+            acc[here] = jnp.zeros_like(acc[here])
+
+        by_rows(first)
+
+    @pl.when(turn < chunks)
+    def _():
+        value, slope_here = gelu_parts(mm_nt(normed[...], up_ref[...]) + ub_ref[...])
+        hidden[turn] = value.astype(BF)
+        slope[turn] = slope_here.astype(BF)
+        acc[...] += mm(hidden[turn], down_ref[...])
+
+    @pl.when(turn == chunks - 1)
+    def _():
+        def second(here):
+            unit2, scale2 = normalize(normed[here].astype(F32) + acc[here] + vec_ref[at["db"]])
+            out_ref[here] = (unit2 * vec_ref[at["g2"]] + vec_ref[at["s2"]]).astype(BF)
+            ct = ct_ref[here].astype(F32)
+            tally("g2", ct * unit2)
+            tally("s2", ct)
+            dy[here] = normalize_back(ct, vec_ref[at["g2"]], unit2, scale2)
+            tally("db", dy[here])
+            dy_low[here] = dy[here].astype(BF)
+            acc[here] = jnp.zeros_like(acc[here])
+
+        by_rows(second)
+
+    @pl.when(turn >= chunks)
+    def _():
+        j = 2 * chunks - 1 - turn
+        gdown_ref[...] = mm_tn(hidden[j], dy_low[...]).astype(BF)
+        du = (mm_nt(dy_low[...], down_ref[...]) * slope[j].astype(F32)).astype(BF)
+        dub_ref[...] = jnp.sum(du.astype(F32), axis=0, keepdims=True)
+        gup_ref[...] = mm_tn(du, normed[...]).astype(BF)
+        acc[...] += mm(du, up_ref[...])
+
+    @pl.when(turn == 2 * chunks - 1)
+    def _():
+        def third(here):
+            dnormed = dy[here] + acc[here]
+            tally("g1", dnormed * unit[here])
+            tally("s1", dnormed)
+            dbl = normalize_back(dnormed, vec_ref[at["g1"]], unit[here], scale[here])
+            tally("ob", dbl)
+            dbl_ref[here] = dbl
+            dy_low[here] = dbl.astype(BF)
+
+        by_rows(third)
+        go_ref[...] = mm_tn(att_ref[...], dy_low[...]).astype(BF)
+        datt_ref[...] = mm_nt(dy_low[...], wo_ref[...]).astype(BF)
+
+
+def feed(attended, x, ct, w):
+    rows, width = x.shape
+    hidden = w["up"].shape[0]
+    size = 512
+    chunks = hidden // size
+
+    def whole(shape):
+        return pl.BlockSpec(shape, lambda t: (0,) * len(shape), pipeline_mode=pl.Buffered(1))
+
+    def kept(shape):
+        return pl.BlockSpec(shape, lambda t: (0,) * len(shape))
+
+    def weight(t):
+        return jnp.where(t < chunks, t, 2 * chunks - 1 - t)
+
+    def grad(t):
+        return jnp.where(t < chunks, chunks - 1, 2 * chunks - 1 - t)
+
+    outs = pl.pallas_call(
+        feed_kernel,
+        grid=(2 * chunks,),
+        in_specs=[whole((rows, width))] * 3
+        + [whole((width, width))]
+        + [pl.BlockSpec((size, width), lambda t: (weight(t), 0))] * 2
+        + [pl.BlockSpec((1, size), lambda t: (0, weight(t))), whole((16, width))],
+        out_specs=[kept((rows, width))]
+        + [pl.BlockSpec((size, width), lambda t: (grad(t), 0))] * 2
+        + [kept((width, width)), pl.BlockSpec((1, size), lambda t: (0, grad(t))), kept((16, width))]
+        + [kept((rows, width))] * 2,
+        out_shape=[
+            jax.ShapeDtypeStruct((rows, width), BF),
+            *[jax.ShapeDtypeStruct((hidden, width), BF)] * 2,
+            jax.ShapeDtypeStruct((width, width), BF),
+            jax.ShapeDtypeStruct((1, hidden), F32),
+            jax.ShapeDtypeStruct((16, width), F32),
+            jax.ShapeDtypeStruct((rows, width), F32),
+            jax.ShapeDtypeStruct((rows, width), BF),
+        ],
+        scratch_shapes=[
+            pltpu.VMEM((rows, width), F32),
+            pltpu.VMEM((rows, 1), F32),
+            pltpu.VMEM((rows, width), BF),
+            pltpu.VMEM((rows, width), F32),
+            pltpu.VMEM((chunks, rows, size), BF),
+            pltpu.VMEM((chunks, rows, size), BF),
+            pltpu.VMEM((rows, width), F32),
+            pltpu.VMEM((rows, width), BF),
+        ],
+        compiler_params=pltpu.CompilerParams(vmem_limit_bytes=56 * MIB),
+        name="feed",
+    )(attended, x, ct, w["o"], w["up"], w["down"], w["ub"], w["vec"])
+    outputs, gup, gdown, go, dub, sums, dbl, datt = outs
+    return outputs, dict(up=gup, down=gdown, o=go, ub=dub, sums=sums), dbl, datt
 
 
 def body(
@@ -1045,31 +1409,17 @@
     window = lax.dynamic_slice_in_dim(padded_lengths, seq, 5, 0)
     own_length = window[4]
 
-    memory = shifted(x, "seq", 1)
-    shards = dict(
-            q=query_weight, k=key_weight, v=value_weight, p=position_weight,
-            o=output_weight, up=up_weight.T, down=down_weight, sq=squeeze_weight.T,
-            cb=content_bias, pb=position_bias, ob=output_bias, g1=first_gain, s1=first_shift, ub=up_bias,
-            db=down_bias, g2=second_gain, s2=second_shift, sb=squeeze_bias,
-    )
-    w = gather_attention(shards)
-    cb, pb, ob, g1, s1, ub, db, g2, s2, sb = (
-        w[n] for n in ("cb", "pb", "ob", "g1", "s1", "ub", "db", "g2", "s2", "sb")
-    )
-
-    pad, taps, collect, biased = squeeze_layout(rows)
+    layout = squeeze_layout(rows)
     row_ids = jnp.arange(rows)
     kept = (row_ids < own_length)[:, None]
     masked = jnp.where(kept, x, jnp.zeros_like(x))
-    made = biased * sb
-    for tap in range(3):
-        made = made + mm_nt(mm_tn(taps[tap], masked, BF), w["sq"][:, tap * width : (tap + 1) * width])
-    made = made.astype(BF)
-    arrived = jnp.concatenate(
-        [shifted(made[role * pad : (role + 1) * pad], "seq", 4 - role) for role in range(3)], axis=0
+    shards = dict(
+        q=query_weight, k=key_weight, v=value_weight, p=position_weight,
+        o=output_weight, up=up_weight.T, down=down_weight, sq=squeeze_weight.T,
+        cb=content_bias, pb=position_bias, ob=output_bias, g1=first_gain, s1=first_shift, ub=up_bias,
+        db=down_bias, g2=second_gain, s2=second_shift, sb=squeeze_bias,
     )
-    squeezed = mm(collect, arrived, out=BF)
-    keys_in = jnp.concatenate([squeezed, memory, x], axis=0)
+    w, squeezed, memory = open_layer(shards, x, masked, layout)
 
     flat = np.arange(0, 3 * rows, 3)
     history_ok = jnp.asarray(flat % rows) < window[:3][flat // rows]
@@ -1077,64 +1427,24 @@
     key_bias = jnp.where(valid, 0.0, -1e30).astype(F32)[None]
 
     table = table_rows(width, 3 * rows)
-    (attended, probs, *saved), dense = attend_forward(key_bias, cb, pb, keys_in, jnp.asarray(table), w, shards)
+    (attended, probs, *saved, keys_in_t), dense = attend_forward(key_bias, squeezed, memory, x, jnp.asarray(table), w, shards)
     w.update(dense)
 
-    blended = x.astype(F32) + mm(attended, w["o"]) + ob
-    unit1, scale1 = normalize(blended)
-    normed = (unit1 * g1 + s1).astype(BF)
-    u = mm_nt(normed, w["up"]) + ub
-    hidden_f, slope = gelu_parts(u)
-    hidden = hidden_f.astype(BF)
-    unit2, scale2 = normalize(normed.astype(F32) + mm(hidden, w["down"]) + db)
-    outputs = (unit2 * g2 + s2).astype(BF)
-
-    grads = {}
-    ct = lax.dynamic_index_in_dim(cotangent[:, 0], head, 0, keepdims=False).astype(F32)
-    grads["g2"] = jnp.sum(ct * unit2, axis=0)
-    grads["s2"] = jnp.sum(ct, axis=0)
-    dy = normalize_back(ct, g2, unit2, scale2)
-    grads["db"] = jnp.sum(dy, axis=0)
-    dy_b = dy.astype(BF)
-    grads["down"] = mm_tn(hidden, dy_b, BF)
-    du = (mm_nt(dy_b, w["down"]) * slope).astype(BF)
-    grads["ub"] = jnp.sum(du.astype(F32), axis=0)
-    grads["up"] = mm_tn(du, normed, BF)
-    dnormed = dy + mm(du, w["up"])
-    grads["g1"] = jnp.sum(dnormed * unit1, axis=0)
-    grads["s1"] = jnp.sum(dnormed, axis=0)
-    dblended = normalize_back(dnormed, g1, unit1, scale1)
-    grads["ob"] = jnp.sum(dblended, axis=0)
-    dblended_b = dblended.astype(BF)
-    grads["o"] = mm_tn(attended, dblended_b, BF)
-    dattended = mm_nt(dblended_b, w["o"], BF)
+    ct = lax.dynamic_index_in_dim(cotangent[:, 0], head, 0, keepdims=False)
+    outputs, grads, dblended, dattended = feed(attended, x, ct, w)
 
     (dcb, dpb), squares, final, (dsqueezed, dmemory, dcurrent) = attend_backward(
-        saved, probs, dattended, keys_in.T, jnp.asarray(np.ascontiguousarray(table.T)), w, grads
+        saved, probs, dattended, keys_in_t, jnp.asarray(np.ascontiguousarray(table.T)), w, grads
     )
     grads.update(zip(("q", "k", "v", "p"), squares))
-    grads["cb"] = dcb[0]
-    grads["pb"] = dpb[0]
-    grads["sb"] = jnp.sum(dsqueezed.astype(F32), axis=0)
-    dmade = mm_tn(collect, dsqueezed, BF)
-    returned = jnp.concatenate(
-        [shifted(dmade[role * pad : (role + 1) * pad], "seq", role - 4) for role in range(3)], axis=0
+    grads["cb"] = dcb
+    grads["pb"] = dpb
+    more, input_rows, output_rows = close_layer(
+        grads, w, layout, dsqueezed, dmemory, dcurrent, dblended, masked, kept.astype(F32), outputs
     )
-    from_next = shifted(dmemory, "seq", -1)
-    dx = dblended + dcurrent + from_next.astype(F32)
-    dmasked = jnp.zeros((rows, width), F32)
-    sq_grads = []
-    for tap in range(3):
-        spread = mm(taps[tap], returned, out=BF)
-        dmasked = dmasked + mm(spread, w["sq"][:, tap * width : (tap + 1) * width])
-        sq_grads.append(mm_tn(spread, masked, BF))
-    grads["sq"] = jnp.concatenate(sq_grads, axis=1)
-    dx = dx + jnp.where(kept, dmasked, 0.0)
-
-    final.update(scatter_attention(grads))
+    final.update(more)
     return (
-        exchange_rows(outputs, head),
-        exchange_rows(dx.astype(BF), head),
+        output_rows[:, None], input_rows[:, None],
         final["q"], final["k"], final["v"], final["p"], final["cb"], final["pb"],
         final["o"], final["ob"], final["g1"], final["s1"], final["up"].T, final["ub"],
         final["down"], final["db"], final["g2"], final["s2"], final["sq"].T, final["sb"],

time: 612 us -> 544 us (0.89)
  Pallas kernels: 381 us -> 508 us
  matrix products: 113 us -> 0 us
  waiting for transfers between devices: 24.3 us -> 0 us
  local copies, waits for them, and re-layouts: 42.1 us -> 17.9 us
  starting transfers between devices: 19.7 us -> 0 us
  other arithmetic: 23.6 us -> 7.55 us
    pallas_call x2 -> x3, Pallas kernels: 166 us -> 299 us  [the longest x1 145 us: close_layer(): pl.pallas_call(functools.partial(close_kernel, count), in_specs=[any_spec...]
    dot_general x31 -> x0, matrix products: 113 us -> none  [mm(): lax.dot_general(left, right, (contract, ((), ())), preferred_element_type...]
    ppermute x10 -> x0, waiting for transfers between devices: 24.3 us -> none  [the longest x8 20.3 us: shifted(): return lax.ppermute(array, axis, pairs)]
    ppermute x10 -> x0, starting transfers between devices: 19.7 us -> none  [the longest x8 17.3 us: shifted(): return lax.ppermute(array, axis, pairs)]
    unnamed x141 -> x84, local copies, waits for them, and re-layouts: 25.3 us -> 14.6 us
    reduce_sum x7 -> x0, other arithmetic: 6.85 us -> none  [the longest x1 2.55 us: body(): grads['ob'] = jnp.sum(dblended, axis=0)]
  transfers between devices with their start and end apart: 10 -> 0, of which waited for: 4 -> 0; matrix products, arithmetic and copies ran while one was open for 10% -> 0% of each run, Pallas kernels for 27% -> 0%
where the time goes in v4:
time: 544 us; the launch traced here: 534 us
  Pallas kernels  508 us (93%)
  local copies, waits for them, and re-layouts  17.9 us (3%)
  other arithmetic  7.55 us (1%)
    pallas_call x1, Pallas kernels, close_layer(): pl.pallas_call(functools.partial(close_kernel, count), in_specs=[any_spec...  145 us
    pallas_call x1, Pallas kernels, attend_backward(): pl.pallas_call(functools.partial(attend_backward_kernel, count), grid=(he...  112 us
    pallas_call x1, Pallas kernels, open_layer(): pl.pallas_call(functools.partial(open_kernel, count, layout), in_specs=[a...  102 us
    pallas_call x1, Pallas kernels, attend_forward(): pl.pallas_call(functools.partial(attend_forward_kernel, count), grid=(wid...  96.5 us
    pallas_call x1, Pallas kernels, feed(): pl.pallas_call(feed_kernel, grid=(2 * chunks,), in_specs=[whole((rows, wi...  51.8 us
    unnamed x84, local copies, waits for them, and re-layouts  14.6 us

profile of v4, /device:TPU:6, one launch (start us, length us, event | category | flops | bytes accessed | tf_op | source)
XLA Modules:
  0.0 534.5 jit_solution(3928459844972888806)
XLA Ops:
  0.9 0.5 copy-done
  1.4 0.1 pad_dynamic-slice_fusion
  1.4 0.6 fusion.7
  2.0 2.6 select_compare_fusion
  4.7 0.7 iota_compare_fusion.1
  5.4 0.7 iota_compare_fusion.2
  6.0 0.6 add_select_fusion.bias_ref
  6.6 1.4 broadcast_select_fusion
  8.3 0.1 fusion.6
  8.4 102.4 %open_layer.1 = (bf16[1024,1024]{1,0:T(8,128)(2,1)}, bf16[1024,1024]{1,0:T(8,128)(2,1)}, bf16[1024,1024]{1,0:T(8,128)(2,1)}, bf16[1024,1024]{1,0:T(8,128)(2,1)},...) custom-call(bf16[64,512]{1,0:T(8,128)(2,1)S(1)} %copy-done.10, ...), custom_call_target="tpu_custom_call" | custom-call | tf_op jit(solution)/shard_map/open_layer/pallas_call | solution.py:410
  110.9 1.0 copy-done.4
  111.8 1.0 copy-done.5
  112.8 0.6 copy-done.14
  113.4 1.8 copy.51
  115.2 96.5 %attend_forward.1 = (bf16[512,1024]{1,0:T(8,128)(2,1)}, bf16[8,512,1536]{2,1,0:T(8,128)(2,1)}, bf16[512,1024]{1,0:T(8,128)(2,1)}, bf16[512,1024]{1,0:T(8,128)(2,...) custom-call(f32[1,1536]{1,0:T(1,128)} %add_select_fusion.bias_ref, ...), custom_call_target="tpu_custom_call" | custom-call | tf_op jit(solution)/shard_map/attend_forward/pallas_call | solution.py:1053
  211.7 1.0 dynamic-slice_bitcast_fusion.ct_ref
  212.8 51.8 %feed.1 = (bf16[512,1024]{1,0:T(8,128)(2,1)}, bf16[4096,1024]{1,0:T(8,128)(2,1)}, bf16[4096,1024]{1,0:T(8,128)(2,1)}, bf16[1024,1024]{1,0:T(8,128)(2,1)}, f32[1,...) custom-call(bf16[512,1024]{1,0:T(8,128)(2,1)} %get-tuple-element.82.att_ref, ...), custom_call_target="tpu_custom_call" | custom-call | tf_op jit(solution)/shard_map/feed/pallas_call | solution.py:1359
  264.6 111.8 %attend_backward.1 = (f32[1,1024]{1,0:T(1,128)}, f32[1,1024]{1,0:T(1,128)}, bf16[1024,1024]{1,0:T(8,128)(2,1)}, bf16[1024,1024]{1,0:T(8,128)(2,1)}, bf16[1024,10...) custom-call(bf16[512,1024]{1,0:T(8,128)(2,1)} %get-tuple-element.76., ...), custom_call_target="tpu_custom_call" | custom-call | tf_op jit(solution)/shard_map/attend_backward/pallas_call | solution.py:1206
  376.4 1.4 fusion.kept
  377.8 145.0 %close_layer.1 = (f32[64,512]{1,0:T(8,128)}, f32[64,512]{1,0:T(8,128)}, f32[64,512]{1,0:T(8,128)}, f32[64,512]{1,0:T(8,128)}, f32[32,3072]{1,0:T(8,128)}, /*inde...) custom-call(bf16[1024,1024]{1,0:T(8,128)(2,1)} %get-tuple-element.92.gq, ...), custom_call_target="tpu_custom_call" | custom-call | tf_op jit(solution)/shard_map/close_layer/pallas_call | solution.py:922
  522.8 1.5 slice_bitcast_fusion
  524.3 1.0 copy.54
  525.4 2.3 copy.65
  527.7 1.0 copy.66
  528.7 0.7 copy.67
  529.3 0.7 copy.68
  530.0 0.7 copy.69
  530.7 0.7 copy.70
  531.3 0.7 copy.71
  532.0 0.5 copy.72
  532.5 0.8 copy.73
  533.3 0.7 copy.74
  (76 shorter events, 0.4 us)
Async XLA Ops:
  0.7 7.7 %copy-start.6 = (bf16[512,528]{1,0:T(8,128)(2,1)S(1)}, bf16[512,528]{1,0:T(8,128)(2,1)}, u32[]{:S(2)}) copy-start(bf16[512,528]{1,0:T(8,128)(2,1)} %constant.59.clone.collect) | copy-start | bytes 1622020
  0.7 7.7 %copy-start.7 = (f32[528,1]{1,0:T(8,128)S(1)}, f32[528,1]{1,0:T(8,128)}, u32[]{:S(2)}) copy-start(f32[528,1]{1,0:T(8,128)} %constant.60.clone.biased) | copy-start | bytes 6340
  0.7 7.4 %copy-start.25 = (bf16[128]{0:T(256)(128)(2,1)S(1)}, bf16[128]{0:T(256)(128)(2,1)}, u32[]{:S(2)}) copy-start(bf16[128]{0:T(256)(128)(2,1)} %param.44) | copy-start | bytes 772
  0.7 7.4 %copy-start.27 = (bf16[64]{0:T(256)(128)(2,1)S(1)}, bf16[64]{0:T(256)(128)(2,1)}, u32[]{:S(2)}) copy-start(bf16[64]{0:T(256)(128)(2,1)} %param.47) | copy-start | bytes 388
  0.7 7.4 %copy-start.26 = (bf16[64]{0:T(256)(128)(2,1)S(1)}, bf16[64]{0:T(256)(128)(2,1)}, u32[]{:S(2)}) copy-start(bf16[64]{0:T(256)(128)(2,1)} %param.48) | copy-start | bytes 388
  0.7 7.4 %copy-start.31 = (bf16[64]{0:T(256)(128)(2,1)S(1)}, bf16[64]{0:T(256)(128)(2,1)}, u32[]{:S(2)}) copy-start(bf16[64]{0:T(256)(128)(2,1)} %param.40) | copy-start | bytes 388
  0.7 7.4 %copy-start.30 = (bf16[64]{0:T(256)(128)(2,1)S(1)}, bf16[64]{0:T(256)(128)(2,1)}, u32[]{:S(2)}) copy-start(bf16[64]{0:T(256)(128)(2,1)} %param.41) | copy-start | bytes 388
  0.8 7.4 %copy-start.29 = (bf16[64]{0:T(256)(128)(2,1)S(1)}, bf16[64]{0:T(256)(128)(2,1)}, u32[]{:S(2)}) copy-start(bf16[64]{0:T(256)(128)(2,1)} %param.42) | copy-start | bytes 388
  0.8 7.4 %copy-start.28 = (bf16[64]{0:T(256)(128)(2,1)S(1)}, bf16[64]{0:T(256)(128)(2,1)}, u32[]{:S(2)}) copy-start(bf16[64]{0:T(256)(128)(2,1)} %param.46) | copy-start | bytes 388
  0.8 7.5 %copy-start.34 = (bf16[32]{0:T(256)(128)(2,1)S(1)}, bf16[32]{0:T(256)(128)(2,1)}, u32[]{:S(2)}) copy-start(bf16[32]{0:T(256)(128)(2,1)} %param.37) | copy-start | bytes 196
  0.8 7.5 %copy-start.33 = (bf16[32]{0:T(256)(128)(2,1)S(1)}, bf16[32]{0:T(256)(128)(2,1)}, u32[]{:S(2)}) copy-start(bf16[32]{0:T(256)(128)(2,1)} %param.38) | copy-start | bytes 196
  0.8 7.5 %copy-start.32 = (bf16[32]{0:T(256)(128)(2,1)S(1)}, bf16[32]{0:T(256)(128)(2,1)}, u32[]{:S(2)}) copy-start(bf16[32]{0:T(256)(128)(2,1)} %param.50) | copy-start | bytes 196
  0.8 7.6 %copy-start.9 = (bf16[3072,32]{0,1:T(8,128)(2,1)S(1)}, bf16[3072,32]{0,1:T(8,128)(2,1)}, u32[]{:S(2)}) copy-start(bf16[3072,32]{0,1:T(8,128)(2,1)} %param.49) | copy-start | bytes 589828
  0.8 7.6 %copy-start.10 = (bf16[64,512]{1,0:T(8,128)(2,1)S(1)}, bf16[64,512]{1,0:T(8,128)(2,1)}, u32[]{:S(2)}) copy-start(bf16[64,512]{1,0:T(8,128)(2,1)} %q.1) | copy-start | bytes 196612
  0.8 7.6 %copy-start.11 = (bf16[64,512]{1,0:T(8,128)(2,1)S(1)}, bf16[64,512]{1,0:T(8,128)(2,1)}, u32[]{:S(2)}) copy-start(bf16[64,512]{1,0:T(8,128)(2,1)} %k.1) | copy-start | bytes 196612
  0.8 7.6 %copy-start.12 = (bf16[64,512]{1,0:T(8,128)(2,1)S(1)}, bf16[64,512]{1,0:T(8,128)(2,1)}, u32[]{:S(2)}) copy-start(bf16[64,512]{1,0:T(8,128)(2,1)} %v.1) | copy-start | bytes 196612
  0.8 7.6 %copy-start.13 = (bf16[64,512]{1,0:T(8,128)(2,1)S(1)}, bf16[64,512]{1,0:T(8,128)(2,1)}, u32[]{:S(2)}) copy-start(bf16[64,512]{1,0:T(8,128)(2,1)} %p.1) | copy-start | bytes 196612
  8.0 102.8 %copy-start.2 = (bf16[512,1024]{1,0:T(8,128)(2,1)}, bf16[512,1024]{1,0:T(8,128)(2,1)S(1)}, u32[]{:S(2)}) copy-start(bf16[512,1024]{1,0:T(8,128)(2,1)S(1)} %get-tuple-element.139.x.in2_ref.x_ref) | copy-start | bytes 3145732
  8.0 102.8 %copy-start.3 = (bf16[512,1024]{1,0:T(8,128)(2,1)}, bf16[512,1024]{1,0:T(8,128)(2,1)S(1)}, u32[]{:S(2)}) copy-start(bf16[512,1024]{1,0:T(8,128)(2,1)S(1)} %get-tuple-element.138.masked) | copy-start | bytes 3145732
  113.4 1.8 copy-start.8
  115.2 96.5 %copy-start.16 = (bf16[2,1,512,1024]{3,2,1,0:T(8,128)(2,1)S(1)}, bf16[2,1,512,1024]{3,2,1,0:T(8,128)(2,1)}, u32[]{:S(2)}) copy-start(bf16[2,1,512,1024]{3,2,1,0:T(8,128)(2,1)} %param.51) | copy-start | bytes 6291460
  377.8 146.5 %copy-start.18 = (f32[128,1024]{1,0:T(8,128)S(1)}, f32[128,1024]{1,0:T(8,128)}, u32[]{:S(2)}) copy-start(f32[128,1024]{1,0:T(8,128)} %get-tuple-element.114) | copy-start | bytes 1572868
  522.8 4.9 copy-start.15
  525.3 3.3 copy-start.24
  525.3 4.0 copy-start.23
  525.3 4.7 copy-start.22
  525.3 5.3 copy-start.21
  527.7 3.6 copy-start.20
  527.7 4.3 copy-start.35
  527.7 4.8 copy-start.17
  527.7 5.6 %copy-start.19 = (f32[32,3072]{1,0:T(8,128)S(1)}, f32[32,3072]{1,0:T(8,128)}, u32[]{:S(2)}) copy-start(f32[32,3072]{1,0:T(8,128)} %get-tuple-element.117) | copy-start | bytes 1179652
  527.7 6.3 %copy-start.1 = (s32[2,16]{1,0:T(2,128)S(1)}, s32[2,16]{1,0:T(2,128)}, u32[]{:S(2)}) copy-start(s32[2,16]{1,0:T(2,128)} %param.32) | copy-start | bytes 388
  (4 other events, 3.2 us)

commit v5 on v4

--- a/solution.py
+++ b/solution.py
@@ -164,7 +164,7 @@
                     for y in (0, 1):
                         if t or x or y:
                             found.append((t, sign, x, y))
-        return sorted(found, key=lambda e: e[0] + e[2] + e[3])
+        return sorted(found, key=lambda e: e[0] + 2 * (e[2] + e[3]))
 
     def onward(self, u, sign, x, y):
         order = self.units[u][3]
@@ -266,15 +266,30 @@
     return (shard, full, view, order)
 
 
+def kept_rows(rows, window):
+    at = lax.broadcasted_iota(jnp.int32, rows.shape, 0)
+    return jnp.where(at < window[4], rows.astype(F32), 0.0).astype(rows.dtype)
+
+
+def key_bias(rows, window):
+    key = lax.broadcasted_iota(jnp.int32, (1, 3 * rows), 1)
+    flat = 3 * key
+    source = jnp.where(flat >= 2 * rows, 2, jnp.where(flat >= rows, 1, 0))
+    source = jnp.where(key >= 2 * rows, 4, jnp.where(key >= rows, 3, source))
+    first = jnp.where(key >= 2 * rows, 2 * rows, jnp.where(key >= rows, rows, source * rows))
+    limit = sum(jnp.where(source == i, window[i], 0) for i in range(5))
+    return jnp.where(jnp.where(key < rows, flat, key) - first < limit, 0.0, -1e30)
+
+
 def open_kernel(
-    count, small_names, q, k, v, p, sq, small, x, masked, taps_t, collect, biased,
-    q_f, k_f, v_f, p_f, sq_f, vec, vec_up, squeezed, memory,
-    small_f, taps_scr, masked_scr, sq_scr, grouped, made, made_low, arriving, load_sem, row_send, row_recv, *sems,
+    count, small_names, q, k, v, p, sq, small, both, taps_t, window, biased,
+    q_f, k_f, v_f, p_f, sq_f, vec, vec_up, made_out, memory,
+    small_f, taps_scr, x_scr, sq_scr, grouped, made, load_sem, row_send, row_recv, *sems,
 ):
     place = Place(count)
     place.barrier(True)
-    rows, width = masked_scr.shape
-    pad = made.shape[0] // 3
+    rows, width = x_scr.shape
+    x = both.at[place.h]
 
     def small_view(ref, h, s):
         return ref.at[pl.ds(pl.multiple_of((h * count + s) * 8, 8), 8)]
@@ -283,95 +298,97 @@
     late = Gather(
         place, [square_unit(*pair, GATHER_ORDERS[i]) for i, pair in enumerate(((q, q_f), (k, k_f), (v, v_f), (p, p_f)))], *sems[3:]
     )
-
-    def rows_copy(i):
-        by = 4 - i if i < 3 else 1
-        here = pl.ds(i * pad, pad)
-        return pltpu.make_async_remote_copy(
-            src_ref=made_low.at[here] if i < 3 else x,
-            dst_ref=arriving.at[here] if i < 3 else memory,
-            send_sem=row_send.at[i],
-            recv_sem=row_recv.at[i],
-            device_id=(place.h, place.s + by),
-            device_id_type=MESH,
-        )
-
-    def send_rows(i, wait=False):
-        @pl.when(place.inside(4 - i if i < 3 else 1))
-        def _():
-            if wait:
-                rows_copy(i).wait_send()
-            else:
-                rows_copy(i).start()
-
-    def take_rows(i):
-        @pl.when(place.inside(i - 4 if i < 3 else -1))
-        def _():
-            rows_copy(i).wait_recv()
-
+    rows_copy = pltpu.make_async_remote_copy(
+        src_ref=x,
+        dst_ref=memory,
+        send_sem=row_send,
+        recv_sem=row_recv,
+        device_id=(place.h, place.s + 1),
+        device_id_type=MESH,
+    )
     loads = [
         pltpu.make_async_copy(source, target, load_sem.at[i])
-        for i, (source, target) in enumerate(((taps_t, taps_scr), (masked, masked_scr), (sq_f, sq_scr)))
+        for i, (source, target) in enumerate(((taps_t, taps_scr), (x, x_scr), (sq_f, sq_scr)))
     ]
     early.begin()
+    late.begin()
+
+    @pl.when(place.inside(1))
+    def _():
+        rows_copy.start()
+
     loads[0].start()
     loads[1].start()
-    send_rows(3)
-    late.begin()
+    blank = pltpu.make_async_copy(made_out.at[pl.ds(0, rows)], memory, load_sem.at[3])
 
     @pl.when(place.s == 0)
     def _():
-        made_low[...] = jnp.zeros_like(made_low)
-        blank = pltpu.make_async_copy(made_low.at[pl.ds(0, rows)], memory, load_sem.at[3])
+        made_out[...] = jnp.zeros_like(made_out)
         blank.start()
         blank.wait()
 
-    for i in range(3):
-        @pl.when(jnp.logical_not(place.inside(i - 4)))
-        def _(i=i):
-            arriving[i * pad : (i + 1) * pad] = jnp.zeros((pad, width), BF)
-
-    entries = early.sources()
-
-    def passed(gather, depth):
-        for entry in entries:
-            if entry[0] + entry[2] + entry[3] == depth:
-                gather.pass_on(entry)
-
-    deepest = place.n + 1
     loads[0].wait()
     loads[1].wait()
-    passed(early, 1)
-    for tap in range(3):
-        grouped[tap] = mm(taps_scr[tap], masked_scr[...]).astype(BF)
-    for depth in range(2, deepest + 1):
-        passed(early, depth)
-        if depth > 2:
-            passed(late, depth - 2)
+    x_scr[...] = kept_rows(x_scr[...], window)
+    entries = early.sources()
+
+    def group(tap):
+        grouped[tap] = mm(taps_scr[tap], x_scr[...]).astype(BF)
+
+    def square(tap):
+        more = mm_nt(grouped[tap], sq_scr[:, tap * width : (tap + 1) * width])
+        if tap:
+            made[...] += more
+        else:
+            made[...] = more + biased[...] * vec[2:3]
+
+    def unpack():
+        for slot in range(2 * count):
+            for name, row, at, size, target in small_names:
+                if size * 2 * count > vec.shape[1] * (4 if name == "ub" else 1) and slot >= count:
+                    continue
+                ref = vec_up if name == "ub" else vec
+                ref[target : target + 1, slot * size : (slot + 1) * size] = small_f[slot * 8 + row : slot * 8 + row + 1, at : at + size]
+
+    lag = len(entries) // OPEN_LAG
+    for i, entry in enumerate(entries):
+        early.pass_on(entry)
+        if i >= lag:
+            late.pass_on(entries[i - lag])
+        if i < 3:
+            group(i)
     early.arrived()
     loads[2].start()
-    for slot in range(2 * count):
-        for name, row, at, size, target in small_names:
-            if size * 2 * count > vec.shape[1] * (4 if name == "ub" else 1) and slot >= count:
-                continue
-            ref = vec_up if name == "ub" else vec
-            ref[target : target + 1, slot * size : (slot + 1) * size] = small_f[slot * 8 + row : slot * 8 + row + 1, at : at + size]
+    unpack()
     loads[2].wait()
-    made[...] = mm_nt(grouped[0], sq_scr[:, :width]) + biased[...] * vec[2:3]
-    passed(late, deepest - 1)
-    made[...] += mm_nt(grouped[1], sq_scr[:, width : 2 * width])
-    passed(late, deepest)
-    made_low[...] = (made[...] + mm_nt(grouped[2], sq_scr[:, 2 * width :])).astype(BF)
-    for i in range(3):
-        send_rows(i)
+    rest = spread_steps([functools.partial(late.pass_on, entry) for entry in entries[len(entries) - lag :]], 3)
+    for tap in range(3):
+        for step in rest[tap]:
+            step()
+        square(tap)
+    made_out[...] = made[...].astype(BF)
     late.arrived()
-    for i in range(4):
-        take_rows(i)
-    squeezed[...] = mm(collect[...], arriving[...]).astype(BF)
-    for i in range(4):
-        send_rows(i, True)
+
+    @pl.when(place.inside(-1))
+    def _():
+        rows_copy.wait_recv()
+
+    @pl.when(place.inside(1))
+    def _():
+        rows_copy.wait_send()
+
     early.sent()
     late.sent()
+
+
+def spread_steps(steps, points):
+    out = [[] for _ in range(points)]
+    for i, step in enumerate(steps):
+        out[i * points // len(steps)].append(step)
+    return out
+
+
+OPEN_LAG = 2
 
 
 def gather_semaphores(count, units):
@@ -392,11 +409,11 @@
     return names
 
 
-def open_layer(w, x, masked, layout):
+def open_layer(w, inputs, window, layout):
     pad, taps, collect, biased = layout
     count = lax.axis_size("seq")
     both, seq = w["cb"].shape[0], w["ob"].shape[0]
-    rows, width = x.shape
+    rows, width = inputs.shape[1:]
     layout = small_layout(both, seq)
     lines = [[] for _ in range(8)]
     for name, row, at, size, target in layout:
@@ -404,41 +421,38 @@
     lines = [jnp.concatenate(parts) if parts else jnp.zeros((128,), F32) for parts in lines]
     small = jnp.stack([jnp.pad(line, (0, 128 - line.shape[0])) for line in lines])
     names = ("q", "k", "v", "p", "sq")
-    tall = w["sq"].shape[1]
     any_spec = pl.BlockSpec(memory_space=pl.ANY)
     vmem_spec = pl.BlockSpec(memory_space=pltpu.VMEM)
     outs = pl.pallas_call(
         functools.partial(open_kernel, count, layout),
-        in_specs=[any_spec] * 9 + [vmem_spec] * 2,
+        in_specs=[any_spec] * 8 + [pl.BlockSpec(memory_space=pltpu.SMEM), vmem_spec],
         out_specs=[any_spec] * 5 + [vmem_spec] * 3 + [any_spec],
         out_shape=[
             *[jax.ShapeDtypeStruct((width, width), BF) for _ in range(4)],
-            jax.ShapeDtypeStruct((width, tall), BF),
+            jax.ShapeDtypeStruct((width, w["sq"].shape[1]), BF),
             jax.ShapeDtypeStruct((16, width), F32),
             jax.ShapeDtypeStruct((1, 4 * width), F32),
-            jax.ShapeDtypeStruct((rows, width), BF),
+            jax.ShapeDtypeStruct((3 * pad, width), BF),
             jax.ShapeDtypeStruct((rows, width), BF),
         ],
         scratch_shapes=[
             pltpu.VMEM((8 * 2 * count, 128), F32),
             pltpu.VMEM((3, 3 * pad, rows), BF),
             pltpu.VMEM((rows, width), BF),
-            pltpu.VMEM((width, tall), BF),
+            pltpu.VMEM((width, w["sq"].shape[1]), BF),
             pltpu.VMEM((3, 3 * pad, width), BF),
             pltpu.VMEM((3 * pad, width), F32),
-            pltpu.VMEM((3 * pad, width), BF),
-            pltpu.VMEM((3 * pad, width), BF),
             pltpu.SemaphoreType.DMA((4,)),
-            pltpu.SemaphoreType.DMA((4,)),
-            pltpu.SemaphoreType.DMA((4,)),
+            *[pltpu.SemaphoreType.DMA] * 2,
             *gather_semaphores(count, 1 + len(halves(w["sq"].shape[0]))),
             *gather_semaphores(count, 4),
         ],
-        compiler_params=pltpu.CompilerParams(collective_id=0, has_side_effects=True, vmem_limit_bytes=48 * MIB),
+        compiler_params=pltpu.CompilerParams(collective_id=0, has_side_effects=True, vmem_limit_bytes=62 * MIB),
         name="open_layer",
-    )(*[w[n] for n in names], small, x, masked, jnp.asarray(np.ascontiguousarray(taps.transpose(0, 2, 1))), jnp.asarray(collect), jnp.asarray(biased))
-    full = dict(zip(names, outs), vec=outs[5], ub=outs[6])
-    return full, outs[7], outs[8]
+    )(
+        *[w[n] for n in names], small, inputs, jnp.asarray(np.ascontiguousarray(taps.transpose(0, 2, 1))), window, jnp.asarray(biased)
+    )
+    return dict(zip(names, outs), vec=outs[5], ub=outs[6]), outs[7], outs[8]
 
 
 class Scatter:
@@ -721,18 +735,23 @@
     return scratch
 
 
+CLOSE_PLAN = (
+    *("m0", ":load", "m1", "m2", ":wait", "c0", "m3", "c1", "m4", "c2", "l0"),
+    *("m5", "l1", "l2", "l3", "l4", "m6", ":memory", "l5", ":out", "m7", "l6", "m8", "l7", ":rows", "l8", "m9", "l9"),
+)
+
+
 def close_kernel(
-    count, gq, gk, gv, gp, sqw, dcb, dpb, vec, dub, dsq, dmem, dcur, dbl, masked, kept, taps, collect_t, outputs,
+    count, gq, gk, gv, gp, sqw, dcb, dpb, dsb, vec, dub, dmade, dmem, dcur, dbl, masked, window, taps, outputs,
     q_out, k_out, v_out, p_out, sq_out, vec_out, ub_out, dx_out, rows_out,
-    sums, parts, vec_send, vec_recv, dmade, returned, from_next, gsq, sq_scr, dcur_scr, dbl_scr, masked_scr, taps_scr,
+    sums, parts, vec_send, vec_recv, returned, from_next, gsq, sq_scr, dcur_scr, dbl_scr, masked_scr, taps_scr,
     spread, dmasked, load_sem, row_send, row_recv, out_sem, out_send, out_recv, *scratch,
 ):
     place = Place(count)
     place.barrier(True)
     r, w = q_out.shape
-    rows, width = dsq.shape
+    rows, width = spread.shape
     half = rows // 2
-    pad = dmade.shape[0] // 3
     units, stores = [], []
     for ref, out, order in zip((gq, gk, gv, gp), (q_out, k_out, v_out, p_out), SCATTER_ORDERS):
         units.append(Scatter(place, square_pairs(ref, r, w), order, *scratch[:8]))
@@ -748,19 +767,22 @@
     loads = [
         pltpu.make_async_copy(source, target, load_sem.at[i])
         for i, (source, target) in enumerate(
-            ((taps, taps_scr), (masked, masked_scr), (sqw, sq_scr), (dcur, dcur_scr), (dbl, dbl_scr))
+            (
+                (taps, taps_scr), (masked.at[place.h], masked_scr), (sqw, sq_scr), (dcur, dcur_scr), (dbl, dbl_scr),
+            )
         )
     ]
 
+    pad = dmade.shape[0] // 3
+
     def rows_copy(i):
-        by = i - 4 if i < 3 else -1
         here = pl.ds(i * pad, pad)
         return pltpu.make_async_remote_copy(
             src_ref=dmade.at[here] if i < 3 else dmem,
             dst_ref=returned.at[here] if i < 3 else from_next,
             send_sem=row_send.at[i],
             recv_sem=row_recv.at[i],
-            device_id=(place.h, place.s + by),
+            device_id=(place.h, place.s + (i - 4 if i < 3 else -1)),
             device_id_type=MESH,
         )
 
@@ -797,7 +819,7 @@
             sums[CORE, 0:16] = vec[...]
             sums[CORE, 0:1] = dcb[...]
             sums[CORE, 1:2] = dpb[...]
-            sums[CORE, 2:3] = jnp.sum(dsq[...].astype(F32), axis=0, keepdims=True)
+            sums[CORE, 2:3] = dsb[...]
             for i in range(4):
                 sums[CORE, 12 + i : 13 + i] = dub[:, i * width : (i + 1) * width]
             vec_copy(CORE).start()
@@ -841,32 +863,20 @@
     low = scatter_steps(place, low_units, low_stores)
     far = place.n - 1
 
-    for load in loads:
-        load.start()
-    dmade[...] = mm(collect_t[...], dsq[...]).astype(BF)
-    for i in range(4):
-        by = i - 4 if i < 3 else -1
-
-        @pl.when(place.inside(by))
-        def _(i=i):
+    def give(i):
+        @pl.when(place.inside(i - 4 if i < 3 else -1))
+        def _():
             rows_copy(i).start()
 
-        @pl.when(jnp.logical_not(place.inside(-by)))
-        def _(i=i):
+        @pl.when(jnp.logical_not(place.inside(4 - i if i < 3 else 1)))
+        def _():
             if i < 3:
                 returned[i * pad : (i + 1) * pad] = jnp.zeros((pad, width), BF)
             else:
                 from_next[...] = jnp.zeros_like(from_next)
 
-    exchange(0, outputs, rows_out)
-    for step in main[:5]:
-        step()
-    for i in range(4):
-        @pl.when(place.inside(4 - i if i < 3 else 1))
-        def _(i=i):
-            rows_copy(i).wait_recv()
-    for load in loads:
-        load.wait()
+    for i in range(3):
+        give(i)
 
     def compressed(tap):
         cols = slice(tap * width, (tap + 1) * width)
@@ -877,26 +887,44 @@
         dmasked[...] = more
         gsq[:, cols] = mm_tn(spread[...], masked_scr[...]).astype(BF)
 
-    compressed(0)
-    compressed(1)
-    for step in main[5 : 5 + far]:
-        step()
-    compressed(2)
-    low[0]()
-    spread[...] = (dbl_scr[...] + dcur_scr[...] + from_next[...].astype(F32) + kept[...] * dmasked[...]).astype(BF)
-    exchange(1, spread, dx_out)
-    for step in low[1:5]:
-        step()
-    for step in main[5 + far : 5 + 2 * far + 1]:
-        step()
-    for step in low[5 : 5 + far]:
-        step()
-    for step in main[6 + 2 * far : 6 + 3 * far]:
-        step()
-    for step in low[5 + far : 6 + 3 * far]:
-        step()
-    main[-1]()
-    low[-1]()
+    def run(steps):
+        for step in steps:
+            step()
+
+    def part(steps, k):
+        cuts = [0, 1, 2, 3, 4, 5, 5 + far, 5 + 2 * far, 6 + 2 * far, 6 + 3 * far, 7 + 3 * far]
+        run(steps[cuts[k] : cuts[k + 1]])
+
+    def load_all():
+        for load in loads:
+            load.start()
+
+    def wait_all():
+        for load in loads:
+            load.wait()
+        masked_scr[...] = kept_rows(masked_scr[...], window)
+        for i in range(3):
+            @pl.when(place.inside(4 - i))
+            def _(i=i):
+                rows_copy(i).wait_recv()
+
+    def send_rows():
+        @pl.when(place.inside(1))
+        def _():
+            rows_copy(3).wait_recv()
+
+        spread[...] = (dbl_scr[...] + dcur_scr[...] + from_next[...].astype(F32) + kept_rows(dmasked[...], window)).astype(BF)
+        exchange(1, spread, dx_out)
+
+    for item in CLOSE_PLAN:
+        if item[0] == "m":
+            part(main, int(item[1:]))
+        elif item[0] == "l":
+            part(low, int(item[1:]))
+        elif item[0] == "c":
+            compressed(int(item[1:]))
+        else:
+            {"load": load_all, "wait": wait_all, "rows": send_rows, "out": lambda: exchange(0, outputs, rows_out), "memory": lambda: give(3)}[item[1:]]()
     for i in range(4):
         @pl.when(place.inside(i - 4 if i < 3 else -1))
         def _(i=i):
@@ -905,10 +933,10 @@
     exchange(1, spread, dx_out, True)
 
 
-def close_layer(g, w, layout, dsq, dmem, dcur, dbl, masked, kept, outputs):
+def close_layer(g, w, layout, dmade, dmem, dcur, dbl, masked, window, outputs):
     pad, taps, collect, biased = layout
     count = lax.axis_size("seq")
-    rows, width = dsq.shape
+    rows, width = dbl.shape
     both = width // (2 * count)
     square = (width // count, width // 2)
     tall = w["sq"].shape[1]
@@ -921,7 +949,7 @@
     any_spec = pl.BlockSpec(memory_space=pl.ANY)
     outs = pl.pallas_call(
         functools.partial(close_kernel, count),
-        in_specs=[any_spec] * 5 + [vmem] * 5 + [any_spec] * 4 + [vmem] + [any_spec] + [vmem] + [any_spec],
+        in_specs=[any_spec] * 5 + [vmem] * 5 + [any_spec] * 5 + [pl.BlockSpec(memory_space=pltpu.SMEM)] + [any_spec] * 2,
         out_specs=[vmem] * 7 + [any_spec] * 2,
         out_shape=[jax.ShapeDtypeStruct(square, F32)] * 4
         + [jax.ShapeDtypeStruct(s, F32) for s in ((both, tall), (16, both), (1, 4 * both))]
@@ -931,7 +959,6 @@
             pltpu.VMEM((5, 16, width), F32),
             pltpu.SemaphoreType.DMA((5,)),
             pltpu.SemaphoreType.DMA((5,)),
-            pltpu.VMEM((3 * pad, width), BF),
             pltpu.VMEM((3 * pad, width), BF),
             pltpu.VMEM((rows, width), BF),
             pltpu.VMEM((width, tall), BF),
@@ -947,11 +974,11 @@
             *[pltpu.SemaphoreType.DMA((2,))] * 3,
             *scratch,
         ],
-        compiler_params=pltpu.CompilerParams(collective_id=2, has_side_effects=True, vmem_limit_bytes=60 * MIB),
+        compiler_params=pltpu.CompilerParams(collective_id=2, has_side_effects=True, vmem_limit_bytes=62 * MIB),
         name="close_layer",
     )(
-        g["q"], g["k"], g["v"], g["p"], w["sq"], g["cb"], g["pb"], g["sums"], g["ub"],
-        dsq, dmem, dcur, dbl, masked, kept, jnp.asarray(taps), jnp.asarray(np.ascontiguousarray(collect.T)), outputs,
+        g["q"], g["k"], g["v"], g["p"], w["sq"], g["cb"], g["pb"], g["sb"], g["sums"], g["ub"],
+        dmade, dmem, dcur, dbl, masked, window, jnp.asarray(taps), outputs,
     )
     final = dict(zip(("q", "k", "v", "p", "sq"), outs[:5]))
     final.update({n: outs[5][i] for i, n in enumerate(VECTORS)})
@@ -959,17 +986,14 @@
     return final, outs[7], outs[8]
 
 
-def spread_steps(steps, points):
-    out = [[] for _ in range(points)]
-    for i, step in enumerate(steps):
-        out[i * points // len(steps)].append(step)
-    return out
+FORWARD_SHARE = 0.25
 
 
 def attend_forward_kernel(
-    count, bias_ref, vec_ref, in0_ref, in1_ref, in2_ref, table_ref, wq_ref, wk_ref, wv_ref, wp_ref, up, down, o,
+    count, window, vec_ref, in1_ref, both, table_ref, wq_ref, wk_ref, wv_ref, wp_ref,
+    collect, made, up, down, o,
     out_ref, p_ref, cq_ref, pq_ref, k_ref, v_ref, pl_ref, in_t_ref, up_f, down_f, o_f,
-    s_scr, x_scr, *sems,
+    s_scr, x_scr, arriving, in0_ref, in2_ref, bias_ref, in_sem, row_send, row_recv, *sems,
 ):
     turn, turns = pl.program_id(0), pl.num_programs(0)
     place = Place(count)
@@ -979,35 +1003,93 @@
     gather = Gather(place, units, *sems)
     first, *steps, last = gather.steps()
     heads = cq_ref.shape[1] // HD
+    rows, keys = cq_ref.shape[0], k_ref.shape[0]
+    width = in2_ref.shape[1]
+    pad = arriving.shape[0] // 3
+    scale = HD ** (-0.5)
     points = 2 + heads
-    plan = spread_steps(steps, turns * points - 1)
+    ahead = int(len(steps) * FORWARD_SHARE)
+    early = spread_steps(steps[:ahead], 4)
+    plan = [[]] * 2 + spread_steps(steps[ahead:], turns * points - 3) + [[]]
+
+    def run(chosen):
+        for step in chosen:
+            step()
 
     def point(k):
         for t in range(turns):
-            chosen = plan[t * points + k - 1] if t or k else [place.barrier, first]
-            if chosen:
+            if t * points + k and plan[t * points + k - 1]:
                 @pl.when(turn == t)
-                def _(chosen=chosen):
-                    for step in chosen:
-                        step()
-
-    rows, keys = cq_ref.shape[0], k_ref.shape[0]
-    scale = HD ** (-0.5)
+                def _(chosen=plan[t * points + k - 1]):
+                    run(chosen)
+
+    def rows_copy(i):
+        here = pl.ds(i * pad, pad)
+        return pltpu.make_async_remote_copy(
+            src_ref=made.at[here],
+            dst_ref=arriving.at[here],
+            send_sem=row_send.at[i],
+            recv_sem=row_recv.at[i],
+            device_id=(place.h, place.s + 4 - i),
+            device_id_type=MESH,
+        )
+
+    @pl.when(turn == 0)
+    def _():
+        load = pltpu.make_async_copy(both.at[place.h], in2_ref, in_sem)
+        load.start()
+        place.barrier(True)
+        for i in range(3):
+            @pl.when(place.inside(4 - i))
+            def _(i=i):
+                rows_copy(i).start()
+
+            @pl.when(jnp.logical_not(place.inside(i - 4)))
+            def _(i=i):
+                arriving[i * pad : (i + 1) * pad] = jnp.zeros((pad, width), BF)
+
+        first()
+        bias_ref[...] = key_bias(rows, window)
+        load.wait()
+
     point(0)
-    sources = (in0_ref, in1_ref, in2_ref)
     query = mm(in2_ref[...], wq_ref[...])
     cq_ref[...] = ((query + vec_ref[0:1]) * scale).astype(BF)
     pq_ref[...] = ((query + vec_ref[1:2]) * scale).astype(BF)
-    for i, source in enumerate(sources):
-        k_ref[i * rows : (i + 1) * rows] = mm(source[...], wk_ref[...]).astype(BF)
-    point(1)
-    for i, source in enumerate(sources):
-        v_ref[i * rows : (i + 1) * rows] = mm(source[...], wv_ref[...]).astype(BF)
+
+    def project(i, source):
+        here = slice(i * rows, (i + 1) * rows)
+        k_ref[here] = mm(source[...], wk_ref[...]).astype(BF)
+        v_ref[here] = mm(source[...], wv_ref[...]).astype(BF)
+
+    def ahead_of_rows(k):
+        @pl.when(turn == 0)
+        def _():
+            run(early[k])
+
+    project(1, in1_ref)
+    ahead_of_rows(0)
+    project(2, in2_ref)
+    ahead_of_rows(1)
+    for i in range(3):
         here = slice(i * rows, (i + 1) * rows)
         pl_ref[here] = mm(table_ref[here], wp_ref[...]).astype(BF)
-
-        @pl.when(turn == i)
-        def _(source=source, here=here):
+    ahead_of_rows(2)
+    point(1)
+
+    @pl.when(turn == 0)
+    def _():
+        run(early[3])
+        for i in range(3):
+            @pl.when(place.inside(i - 4))
+            def _(i=i):
+                rows_copy(i).wait_recv()
+        in0_ref[...] = mm(collect[...], arriving[...]).astype(BF)
+
+    project(0, in0_ref)
+    for i, source in enumerate((in0_ref, in1_ref, in2_ref)):
+        @pl.when(turn == i + 1)
+        def _(source=source, here=slice(i * rows, (i + 1) * rows)):
             in_t_ref[:, here] = source[...].T
     step = 32
     for head in range(heads):
@@ -1033,12 +1115,17 @@
 
     @pl.when(turn == turns - 1)
     def _():
+        for i in range(3):
+            @pl.when(place.inside(4 - i))
+            def _(i=i):
+                rows_copy(i).wait_send()
         last()
 
 
-def attend_forward(key_bias, squeezed, memory, x, table, w, shards):
+def attend_forward(window, memory, inputs, made, table, layout, w, shards):
+    pad, taps, collect, biased = layout
     count = lax.axis_size("seq")
-    rows, width = x.shape
+    rows, width = memory.shape
     keys = 3 * rows
     pair = 2 * HD
     names = ("up", "down", "o")
@@ -1053,9 +1140,10 @@
     outs = pl.pallas_call(
         functools.partial(attend_forward_kernel, count),
         grid=(width // pair,),
-        in_specs=[whole((1, keys)), columns(16), *[whole((rows, width))] * 3, whole((keys, width))]
+        in_specs=[pl.BlockSpec(memory_space=pltpu.SMEM), columns(16), whole((rows, width)), any_spec, whole((keys, width))]
         + [columns(width)] * 4
-        + [any_spec] * 3,
+        + [whole((rows, 3 * pad))]
+        + [any_spec] * 4,
         out_specs=[columns(rows), pl.BlockSpec((2, rows, keys), lambda t: (t, 0, 0))]
         + [columns(rows)] * 2
         + [columns(keys)] * 3
@@ -1072,26 +1160,35 @@
         scratch_shapes=[
             pltpu.VMEM((rows, keys), F32),
             pltpu.VMEM((rows, keys), F32),
+            pltpu.VMEM((3 * pad, width), BF),
+            *[pltpu.VMEM((rows, width), BF)] * 2,
+            pltpu.VMEM((1, keys), F32),
+            pltpu.SemaphoreType.DMA,
+            pltpu.SemaphoreType.DMA((3,)),
+            pltpu.SemaphoreType.DMA((3,)),
             *gather_semaphores(count, sum(len(halves(shards[n].shape[0])) for n in names)),
         ],
-        compiler_params=pltpu.CompilerParams(collective_id=3, has_side_effects=True, vmem_limit_bytes=56 * MIB),
+        compiler_params=pltpu.CompilerParams(collective_id=3, has_side_effects=True, vmem_limit_bytes=62 * MIB),
         name="attend_forward",
-    )(key_bias, w["vec"], squeezed, memory, x, table, w["q"], w["k"], w["v"], w["p"], *[shards[n] for n in names])
+    )(
+        window, w["vec"], memory, inputs, table, w["q"], w["k"], w["v"], w["p"],
+        jnp.asarray(collect), made, *[shards[n] for n in names],
+    )
     return outs[:8], dict(zip(names, outs[8:]))
 
 
 BACKWARD_PLAN = (
     (0, 0), (0, 1), (0, 2), (1, 1), (1, 2),
-    (3, 3), (4, 1), (4, 2),
-    (5, 0), (5, 1), (5, 2),
-    (5, 3),
-    (6, 1), (7, 0), (7, 2),
+    (3, 0), (3, 3), (4, 1),
+    (4, 2), (5, 1), (5, 3),
+    (6, 0),
+    (6, 2), (7, 0), (7, 3),
 )
 
 
 def attend_backward_kernel(
-    count, cq_ref, pq_ref, k_ref, v_ref, pl_ref, p_ref, do_ref, in_t_ref, table_t_ref, wq_ref, wk_ref, wv_ref, up, down, o,
-    dcb_ref, dpb_ref, gq_ref, gk_ref, gv_ref, gp_ref, up_out, down_out, o_out, dsq_out, dmem_out, dcur_out,
+    count, cq_ref, pq_ref, k_ref, v_ref, pl_ref, p_ref, do_ref, in_t_ref, table_t_ref, wq_ref, wk_ref, wv_ref, collect_t, up, down, o,
+    dcb_ref, dpb_ref, gq_ref, gk_ref, gv_ref, gp_ref, dsb_ref, dmade_ref, up_out, down_out, o_out, dmem_out, dcur_out,
     dp_scr, ds_scr, dq_scr, dk_scr, dv_scr, dpl_scr, total, out_sem, *scratch,
 ):
     head, heads = pl.program_id(0), pl.num_programs(0)
@@ -1172,21 +1269,25 @@
                 more = more + mm_nt(dq, wq_ref[...])
             total[here] += more
 
+    width = total.shape[1]
+
     @pl.when(head == heads - 1)
     def _():
-        width = total.shape[1]
         own = pltpu.make_async_copy(total.at[pl.ds(2 * rows, rows)], dcur_out, out_sem.at[0])
         own.start()
-        for i, out in enumerate((dsq_out, dmem_out)):
-            ds_scr[:, :width] = total[i * rows : (i + 1) * rows].astype(BF)
-            copy = pltpu.make_async_copy(ds_scr.at[:, pl.ds(0, width)], out, out_sem.at[1 + i])
-            copy.start()
-            copy.wait()
+        ds_scr[:, :width] = total[rows : 2 * rows].astype(BF)
+        back = pltpu.make_async_copy(ds_scr.at[:, pl.ds(0, width)], dmem_out, out_sem.at[1])
+        back.start()
+        dsq = total[:rows].astype(BF)
+        dsb_ref[...] = jnp.sum(dsq.astype(F32), axis=0, keepdims=True)
+        dmade_ref[...] = mm(collect_t[...], dsq).astype(BF)
+        last()
         own.wait()
-        last()
-
-
-def attend_backward(saved, probs, d_out, inputs_t, table_t, w, dense):
+        back.wait()
+
+
+def attend_backward(saved, probs, d_out, inputs_t, table_t, layout, w, dense):
+    pad, taps, collect, biased = layout
     count = lax.axis_size("seq")
     rows, width = d_out.shape
     keys = inputs_t.shape[1]
@@ -1210,13 +1311,16 @@
         + [columns(keys)] * 3
         + [pl.BlockSpec((1, rows, keys), lambda h: (h, 0, 0)), columns(rows), whole((width, keys)), whole((width, keys))]
         + [pair] * 3
+        + [whole((3 * pad, rows))]
         + [any_spec] * 3,
-        out_specs=[columns(1)] * 2 + [pair] * 4 + [vmem] * 3 + [any_spec] * 3,
+        out_specs=[columns(1)] * 2 + [pair] * 4 + [pl.BlockSpec((1, width), lambda h: (0, 0)), vmem] + [vmem] * 3 + [any_spec] * 2,
         out_shape=[
             *[jax.ShapeDtypeStruct((1, width), F32)] * 2,
             *[jax.ShapeDtypeStruct((width, width), BF)] * 4,
+            jax.ShapeDtypeStruct((1, width), F32),
+            jax.ShapeDtypeStruct((3 * pad, width), BF),
             *[jax.ShapeDtypeStruct(shape, F32) for shape in shapes],
-            *[jax.ShapeDtypeStruct((rows, width), BF)] * 2,
+            jax.ShapeDtypeStruct((rows, width), BF),
             jax.ShapeDtypeStruct((rows, width), F32),
         ],
         scratch_shapes=[
@@ -1225,13 +1329,17 @@
             pltpu.VMEM((2, rows, HD), BF),
             *[pltpu.VMEM((2, keys, HD), BF)] * 3,
             pltpu.VMEM((keys, width), F32),
-            pltpu.SemaphoreType.DMA((3,)),
+            pltpu.SemaphoreType.DMA((2,)),
             *scatter_dense_scratch(count, shapes),
         ],
         compiler_params=pltpu.CompilerParams(collective_id=1, has_side_effects=True, vmem_limit_bytes=62 * MIB),
         name="attend_backward",
-    )(*saved, probs, d_out, inputs_t, table_t, w["q"], w["k"], w["v"], *[dense[n] for n in names])
-    return outs[:2], outs[2:6], dict(zip(names, outs[6:9])), outs[9:]
+    )(
+        *saved, probs, d_out, inputs_t, table_t, w["q"], w["k"], w["v"],
+        jnp.asarray(np.ascontiguousarray(collect.T)), *[dense[n] for n in names],
+    )
+    grads = dict(zip(("cb", "pb", "q", "k", "v", "p", "sb"), outs))
+    return grads, dict(zip(names, outs[8:11])), (outs[7], *outs[11:])
 
 
 def normalize(values):
@@ -1264,13 +1372,13 @@
 
 
 def feed_kernel(
-    att_ref, x_ref, ct_ref, wo_ref, up_ref, down_ref, ub_ref, vec_ref,
+    att_ref, x_all, ct_all, wo_ref, up_ref, down_ref, ub_ref, vec_ref,
     out_ref, gup_ref, gdown_ref, go_ref, dub_ref, sums_ref, dbl_ref, datt_ref,
-    unit, scale, normed, acc, hidden, slope, dy, dy_low,
+    unit, scale, normed, acc, hidden, slope, dy, dy_low, x_ref, ct_ref, load_sem,
 ):
     turn = pl.program_id(0)
     chunks = pl.num_programs(0) // 2
-    rows = x_ref.shape[0]
+    rows = att_ref.shape[0]
     at = {name: slice(i, i + 1) for i, name in enumerate(VECTORS)}
 
     def by_rows(run):
@@ -1279,10 +1387,17 @@
     def tally(name, values):
         sums_ref[at[name]] += jnp.sum(values, axis=0, keepdims=True)
 
+    book = lax.axis_index("head")
+    x_load = pltpu.make_async_copy(x_all.at[book], x_ref, load_sem.at[0])
+    ct_load = pltpu.make_async_copy(ct_all.at[book], ct_ref, load_sem.at[1])
+
     @pl.when(turn == 0)
     def _():
+        x_load.start()
+        ct_load.start()
         sums_ref[...] = jnp.zeros_like(sums_ref)
         acc[...] = mm(att_ref[...], wo_ref[...])
+        x_load.wait()
 
         def first(here):
             unit[here], scale[here] = normalize(x_ref[here].astype(F32) + acc[here] + vec_ref[at["ob"]])
@@ -1300,6 +1415,8 @@
 
     @pl.when(turn == chunks - 1)
     def _():
+        ct_load.wait()
+
         def second(here):
             unit2, scale2 = normalize(normed[here].astype(F32) + acc[here] + vec_ref[at["db"]])
             out_ref[here] = (unit2 * vec_ref[at["g2"]] + vec_ref[at["s2"]]).astype(BF)
@@ -1339,9 +1456,9 @@
 
 
 def feed(attended, x, ct, w):
-    rows, width = x.shape
+    rows, width = attended.shape
     hidden = w["up"].shape[0]
-    size = 512
+    size = 1024
     chunks = hidden // size
 
     def whole(shape):
@@ -1359,7 +1476,8 @@
     outs = pl.pallas_call(
         feed_kernel,
         grid=(2 * chunks,),
-        in_specs=[whole((rows, width))] * 3
+        in_specs=[whole((rows, width))]
+        + [pl.BlockSpec(memory_space=pl.ANY)] * 2
         + [whole((width, width))]
         + [pl.BlockSpec((size, width), lambda t: (weight(t), 0))] * 2
         + [pl.BlockSpec((1, size), lambda t: (0, weight(t))), whole((16, width))],
@@ -1384,13 +1502,48 @@
             pltpu.VMEM((chunks, rows, size), BF),
             pltpu.VMEM((chunks, rows, size), BF),
             pltpu.VMEM((rows, width), F32),
-            pltpu.VMEM((rows, width), BF),
+            *[pltpu.VMEM((rows, width), BF)] * 3,
+            pltpu.SemaphoreType.DMA((2,)),
         ],
-        compiler_params=pltpu.CompilerParams(vmem_limit_bytes=56 * MIB),
+        compiler_params=pltpu.CompilerParams(vmem_limit_bytes=62 * MIB),
         name="feed",
     )(attended, x, ct, w["o"], w["up"], w["down"], w["ub"], w["vec"])
     outputs, gup, gdown, go, dub, sums, dbl, datt = outs
     return outputs, dict(up=gup, down=gdown, o=go, ub=dub, sums=sums), dbl, datt
+
+
+def results_kernel(*refs):
+    count = (len(refs) - 2) // 3
+    sources, targets, blocks = (refs[i * count : (i + 1) * count] for i in range(3))
+    turned, sem = refs[3 * count :]
+    for i in range(count):
+        pltpu.make_async_copy(sources[i], blocks[i], sem.at[i]).start()
+    for i in range(count):
+        pltpu.make_async_copy(sources[i], blocks[i], sem.at[i]).wait()
+        if not i:
+            turned[...] = blocks[0][...].T
+        pltpu.make_async_copy(blocks[i] if i else turned, targets[i], sem.at[i]).start()
+    for i in range(count):
+        pltpu.make_async_copy(blocks[i] if i else turned, targets[i], sem.at[i]).wait()
+
+
+def results(first, rest):
+    any_spec = pl.BlockSpec(memory_space=pl.ANY)
+    arrays = [first, *rest]
+    shapes = [first.shape[::-1], *[a.shape for a in rest]]
+    return pl.pallas_call(
+        results_kernel,
+        in_specs=[any_spec] * len(arrays),
+        out_specs=[any_spec] * len(arrays),
+        out_shape=[jax.ShapeDtypeStruct(shape, a.dtype) for shape, a in zip(shapes, arrays)],
+        scratch_shapes=[
+            *[pltpu.VMEM(a.shape, a.dtype) for a in arrays],
+            pltpu.VMEM(first.shape[::-1], first.dtype),
+            pltpu.SemaphoreType.DMA((len(arrays),)),
+        ],
+        compiler_params=pltpu.CompilerParams(vmem_limit_bytes=62 * MIB),
+        name="results",
+    )(*arrays)
 
 
 def body(
@@ -1403,50 +1556,41 @@
     head = lax.axis_index("head")
     rows, width = inputs.shape[2:]
 
-    x = lax.dynamic_index_in_dim(inputs[:, 0], head, 0, keepdims=False)
     book_lengths = lax.dynamic_index_in_dim(lengths, head, 0, keepdims=False)
     padded_lengths = jnp.concatenate([jnp.zeros((4,), jnp.int32), book_lengths])
     window = lax.dynamic_slice_in_dim(padded_lengths, seq, 5, 0)
-    own_length = window[4]
-
+    x = inputs[:, 0]
     layout = squeeze_layout(rows)
-    row_ids = jnp.arange(rows)
-    kept = (row_ids < own_length)[:, None]
-    masked = jnp.where(kept, x, jnp.zeros_like(x))
     shards = dict(
         q=query_weight, k=key_weight, v=value_weight, p=position_weight,
         o=output_weight, up=up_weight.T, down=down_weight, sq=squeeze_weight.T,
         cb=content_bias, pb=position_bias, ob=output_bias, g1=first_gain, s1=first_shift, ub=up_bias,
         db=down_bias, g2=second_gain, s2=second_shift, sb=squeeze_bias,
     )
-    w, squeezed, memory = open_layer(shards, x, masked, layout)
-
-    flat = np.arange(0, 3 * rows, 3)
-    history_ok = jnp.asarray(flat % rows) < window[:3][flat // rows]
-    valid = jnp.concatenate([history_ok, row_ids < window[3], row_ids < window[4]])
-    key_bias = jnp.where(valid, 0.0, -1e30).astype(F32)[None]
+    w, made, memory = open_layer(shards, x, window, layout)
 
     table = table_rows(width, 3 * rows)
-    (attended, probs, *saved, keys_in_t), dense = attend_forward(key_bias, squeezed, memory, x, jnp.asarray(table), w, shards)
+    (attended, probs, *saved, keys_in_t), dense = attend_forward(
+        window, memory, x, made, jnp.asarray(table), layout, w, shards
+    )
     w.update(dense)
 
-    ct = lax.dynamic_index_in_dim(cotangent[:, 0], head, 0, keepdims=False)
-    outputs, grads, dblended, dattended = feed(attended, x, ct, w)
-
-    (dcb, dpb), squares, final, (dsqueezed, dmemory, dcurrent) = attend_backward(
-        saved, probs, dattended, keys_in_t, jnp.asarray(np.ascontiguousarray(table.T)), w, grads
+    outputs, grads, dblended, dattended = feed(attended, x, cotangent[:, 0], w)
+
+    more, final, (dmade, dmemory, dcurrent) = attend_backward(
+        saved, probs, dattended, keys_in_t, jnp.asarray(np.ascontiguousarray(table.T)), layout, w, grads
     )
-    grads.update(zip(("q", "k", "v", "p"), squares))
-    grads["cb"] = dcb
-    grads["pb"] = dpb
     more, input_rows, output_rows = close_layer(
-        grads, w, layout, dsqueezed, dmemory, dcurrent, dblended, masked, kept.astype(F32), outputs
+        {**grads, **more}, w, layout, dmade, dmemory, dcurrent, dblended, x, window, outputs
     )
     final.update(more)
+    names = ("down", "o", "q", "k", "v", "p", "sq")
+    final["up"], output_rows, input_rows, *rest = results(final["up"], [output_rows, input_rows, *[final[n] for n in names]])
+    final.update(zip(names, rest))
     return (
         output_rows[:, None], input_rows[:, None],
         final["q"], final["k"], final["v"], final["p"], final["cb"], final["pb"],
-        final["o"], final["ob"], final["g1"], final["s1"], final["up"].T, final["ub"],
+        final["o"], final["ob"], final["g1"], final["s1"], final["up"], final["ub"],
         final["down"], final["db"], final["g2"], final["s2"], final["sq"].T, final["sb"],
     )
 

time: 544 us -> 499 us (0.917)
  Pallas kernels: 508 us -> 482 us
  local copies, waits for them, and re-layouts: 17.9 us -> 4.74 us
    pallas_call x1, Pallas kernels: 102 us -> 76 us  [open_layer(): pl.pallas_call(functools.partial(open_kernel, count, layout), in_specs=[a...]
    pallas_call x1, Pallas kernels: 96.5 us -> 118 us  [attend_forward(): pl.pallas_call(functools.partial(attend_forward_kernel, count), grid=(wid...]
    pallas_call x1, Pallas kernels: 145 us -> 126 us  [close_layer(): pl.pallas_call(functools.partial(close_kernel, count), in_specs=[any_spec...]
    unnamed x84 -> x10, local copies, waits for them, and re-layouts: 14.6 us -> 2.99 us
where the time goes in v5:
time: 499 us; the launch traced here: 490 us
  Pallas kernels  482 us (97%)
    pallas_call x1, Pallas kernels, close_layer(): pl.pallas_call(functools.partial(close_kernel, count), in_specs=[any_spec...  126 us
    pallas_call x1, Pallas kernels, attend_forward(): pl.pallas_call(functools.partial(attend_forward_kernel, count), grid=(wid...  118 us
    pallas_call x1, Pallas kernels, attend_backward(): pl.pallas_call(functools.partial(attend_backward_kernel, count), grid=(he...  109 us
    pallas_call x1, Pallas kernels, open_layer(): pl.pallas_call(functools.partial(open_kernel, count, layout), in_specs=[a...  76 us
    pallas_call x1, Pallas kernels, feed(): pl.pallas_call(feed_kernel, grid=(2 * chunks,), in_specs=[whole((rows, wi...  49.1 us

profile of v5, /device:TPU:6, one launch (start us, length us, event | category | flops | bytes accessed | tf_op | source)
XLA Modules:
  0.0 489.8 jit_solution(1689435894668606573)
XLA Ops:
  0.7 0.0 copy-start
  0.7 0.7 copy-done
  1.3 0.6 pad_dynamic-slice_fusion.window
  1.9 0.8 fusion.4
  2.7 0.8 fusion.2
  3.5 0.8 bitcast_convert_fusion
  4.2 0.6 stack.49.small
  4.9 1.8 copy.48
  6.6 76.0 %open_layer.1 = (bf16[1024,1024]{1,0:T(8,128)(2,1)}, bf16[1024,1024]{1,0:T(8,128)(2,1)}, bf16[1024,1024]{1,0:T(8,128)(2,1)}, bf16[1024,1024]{1,0:T(8,128)(2,1)},...) custom-call(bf16[64,512]{1,0:T(8,128)(2,1)} %q.1, ...), custom_call_target="tpu_custom_call" | custom-call | tf_op jit(solution)/shard_map/open_layer/pallas_call | solution.py:426
  82.7 118.3 %attend_forward.1 = (bf16[512,1024]{1,0:T(8,128)(2,1)}, bf16[8,512,1536]{2,1,0:T(8,128)(2,1)}, bf16[512,1024]{1,0:T(8,128)(2,1)}, bf16[512,1024]{1,0:T(8,128)(2,...) custom-call(s32[5]{0:T(128)} %pad_dynamic-slice_fusion.window, ...), custom_call_target="tpu_custom_call" | custom-call | tf_op jit(solution)/shard_map/attend_forward/pallas_call | solution.py:1140
  201.0 49.1 %feed.1 = (bf16[512,1024]{1,0:T(8,128)(2,1)}, bf16[4096,1024]{1,0:T(8,128)(2,1)}, bf16[4096,1024]{1,0:T(8,128)(2,1)}, bf16[1024,1024]{1,0:T(8,128)(2,1)}, f32[1,...) custom-call(bf16[512,1024]{1,0:T(8,128)(2,1)} %get-tuple-element.93.att_ref, ...), custom_call_target="tpu_custom_call" | custom-call | tf_op jit(solution)/shard_map/feed/pallas_call | solution.py:1476
  250.0 109.0 %attend_backward.1 = (f32[1,1024]{1,0:T(1,128)}, f32[1,1024]{1,0:T(1,128)}, bf16[1024,1024]{1,0:T(8,128)(2,1)}, bf16[1024,1024]{1,0:T(8,128)(2,1)}, bf16[1024,10...) custom-call(bf16[512,1024]{1,0:T(8,128)(2,1)} %get-tuple-element.87., ...), custom_call_target="tpu_custom_call" | custom-call | tf_op jit(solution)/shard_map/attend_backward/pallas_call | solution.py:1307
  359.1 126.0 %close_layer.1 = (f32[64,512]{1,0:T(8,128)}, f32[64,512]{1,0:T(8,128)}, f32[64,512]{1,0:T(8,128)}, f32[64,512]{1,0:T(8,128)}, f32[32,3072]{1,0:T(8,128)}, /*inde...) custom-call(bf16[1024,1024]{1,0:T(8,128)(2,1)} %get-tuple-element.104.gq, ...), custom_call_target="tpu_custom_call" | custom-call | tf_op jit(solution)/shard_map/close_layer/pallas_call | solution.py:950
  485.1 0.0 copy-start.1
  485.1 0.0 copy-start.2
  485.1 0.0 copy-start.3
  485.1 3.3 results.1
  488.5 0.0 copy-done.2
  488.5 0.5 slice_bitcast_fusion
  489.0 0.0 copy-done.3
  489.0 0.5 copy.52
  489.6 0.0 copy-done.1
  (2 shorter events, 0.0 us)
Async XLA Ops:
  0.7 0.7 copy-start
  485.1 4.4 copy-start.1
  485.1 3.4 copy-start.2
  485.1 3.9 copy-start.3

commit v6 on v5

--- a/solution.py
+++ b/solution.py
@@ -736,8 +736,8 @@
 
 
 CLOSE_PLAN = (
-    *("m0", ":load", "m1", "m2", ":wait", "c0", "m3", "c1", "m4", "c2", "l0"),
-    *("m5", "l1", "l2", "l3", "l4", "m6", ":memory", "l5", ":out", "m7", "l6", "m8", "l7", ":rows", "l8", "m9", "l9"),
+    *(":memory", "m0", ":load", "m1", "m2", ":wait", "c0", "m3", "c1", "m4", "c2", "l0"),
+    *("m5", "l1", "l2", "l3", "l4", "m6", "l5", ":out", "m7", "l6", "m8", "l7", ":rows", "l8", "m9", "l9"),
 )
 
 
@@ -1180,9 +1180,9 @@
 BACKWARD_PLAN = (
     (0, 0), (0, 1), (0, 2), (1, 1), (1, 2),
     (3, 0), (3, 3), (4, 1),
-    (4, 2), (5, 1), (5, 3),
-    (6, 0),
-    (6, 2), (7, 0), (7, 3),
+    (5, 0), (5, 2), (5, 3),
+    (6, 1),
+    (7, 0), (7, 1), (7, 3),
 )
 
 

time: 499 us -> 496 us (level)
  no operation moved by 1% of the time
where the time goes in v6:
time: 496 us; the launch traced here: 487 us
  Pallas kernels  479 us (97%)
    pallas_call x1, Pallas kernels, close_layer(): pl.pallas_call(functools.partial(close_kernel, count), in_specs=[any_spec...  124 us
    pallas_call x1, Pallas kernels, attend_forward(): pl.pallas_call(functools.partial(attend_forward_kernel, count), grid=(wid...  118 us
    pallas_call x1, Pallas kernels, attend_backward(): pl.pallas_call(functools.partial(attend_backward_kernel, count), grid=(he...  108 us
    pallas_call x1, Pallas kernels, open_layer(): pl.pallas_call(functools.partial(open_kernel, count, layout), in_specs=[a...  76 us
    pallas_call x1, Pallas kernels, feed(): pl.pallas_call(feed_kernel, grid=(2 * chunks,), in_specs=[whole((rows, wi...  49.1 us

profile of v6, /device:TPU:6, one launch (start us, length us, event | category | flops | bytes accessed | tf_op | source)
XLA Modules:
  0.0 486.9 jit_solution(7436509302458858545)
XLA Ops:
  0.7 0.0 copy-start
  0.7 0.7 copy-done
  1.3 0.6 pad_dynamic-slice_fusion.window
  1.9 0.8 fusion.4
  2.7 0.8 fusion.2
  3.5 0.8 bitcast_convert_fusion
  4.2 0.6 stack.49.small
  4.9 1.8 copy.48
  6.6 76.0 %open_layer.1 = (bf16[1024,1024]{1,0:T(8,128)(2,1)}, bf16[1024,1024]{1,0:T(8,128)(2,1)}, bf16[1024,1024]{1,0:T(8,128)(2,1)}, bf16[1024,1024]{1,0:T(8,128)(2,1)},...) custom-call(bf16[64,512]{1,0:T(8,128)(2,1)} %q.1, ...), custom_call_target="tpu_custom_call" | custom-call | tf_op jit(solution)/shard_map/open_layer/pallas_call | solution.py:426
  82.7 118.3 %attend_forward.1 = (bf16[512,1024]{1,0:T(8,128)(2,1)}, bf16[8,512,1536]{2,1,0:T(8,128)(2,1)}, bf16[512,1024]{1,0:T(8,128)(2,1)}, bf16[512,1024]{1,0:T(8,128)(2,...) custom-call(s32[5]{0:T(128)} %pad_dynamic-slice_fusion.window, ...), custom_call_target="tpu_custom_call" | custom-call | tf_op jit(solution)/shard_map/attend_forward/pallas_call | solution.py:1140
  201.0 49.1 %feed.1 = (bf16[512,1024]{1,0:T(8,128)(2,1)}, bf16[4096,1024]{1,0:T(8,128)(2,1)}, bf16[4096,1024]{1,0:T(8,128)(2,1)}, bf16[1024,1024]{1,0:T(8,128)(2,1)}, f32[1,...) custom-call(bf16[512,1024]{1,0:T(8,128)(2,1)} %get-tuple-element.93.att_ref, ...), custom_call_target="tpu_custom_call" | custom-call | tf_op jit(solution)/shard_map/feed/pallas_call | solution.py:1476
  250.0 108.0 %attend_backward.1 = (f32[1,1024]{1,0:T(1,128)}, f32[1,1024]{1,0:T(1,128)}, bf16[1024,1024]{1,0:T(8,128)(2,1)}, bf16[1024,1024]{1,0:T(8,128)(2,1)}, bf16[1024,10...) custom-call(bf16[512,1024]{1,0:T(8,128)(2,1)} %get-tuple-element.87., ...), custom_call_target="tpu_custom_call" | custom-call | tf_op jit(solution)/shard_map/attend_backward/pallas_call | solution.py:1307
  358.1 124.1 %close_layer.1 = (f32[64,512]{1,0:T(8,128)}, f32[64,512]{1,0:T(8,128)}, f32[64,512]{1,0:T(8,128)}, f32[64,512]{1,0:T(8,128)}, f32[32,3072]{1,0:T(8,128)}, /*inde...) custom-call(bf16[1024,1024]{1,0:T(8,128)(2,1)} %get-tuple-element.104.gq, ...), custom_call_target="tpu_custom_call" | custom-call | tf_op jit(solution)/shard_map/close_layer/pallas_call | solution.py:950
  482.2 0.0 copy-start.1
  482.2 0.0 copy-start.2
  482.2 0.0 copy-start.3
  482.2 3.3 results.1
  485.6 0.0 copy-done.2
  485.6 0.5 slice_bitcast_fusion
  486.1 0.0 copy-done.3
  486.1 0.5 copy.52
  486.6 0.0 copy-done.1
  (2 shorter events, 0.0 us)
Async XLA Ops:
  0.7 0.7 copy-start
  482.2 4.4 copy-start.1
  482.2 3.4 copy-start.2
  482.2 3.9 copy-start.3
